TPU v7x, 32 devices: a whole 2x2x4 slice. The times are simulated.
32 devices in a mesh: dp: 8 (over y, x, core), seq: 4 (over z).
Axes of the slice: x: 2, y: 2, z: 4, core: 2. Of those that a mesh axis runs over, the one named last changes fastest.
Arguments:
- tokens: bfloat16 [16, 1024, 1024], P('dp', 'seq'), may hold values from -17 to 17
- positions: int32 [16, 1024], P('dp', 'seq'), may hold values from 0 to 4092, as said below
- cotangent: bfloat16 [16, 1024, 1024], P('dp', 'seq'), may hold values from -6 to 6
- q_weight: bfloat16 [1024, 1024], P('dp'), may hold values from -0.1875 to 0.1875
- key_matrix: bfloat16 [1024, 512], P('dp'), may hold values from -0.1875 to 0.1875
- value_matrix: bfloat16 [1024, 512], P('dp'), may hold values from -0.1875 to 0.1875
- out_weight: bfloat16 [1024, 1024], P('dp'), may hold values from -2 to 2
- gate_weight: bfloat16 [1024, 4608], P('dp'), may hold values from -0.1875 to 0.1875
- up_weight: bfloat16 [1024, 4608], P('dp'), may hold values from -0.1875 to 0.1875
- down_weight: bfloat16 [1024, 4608], P('dp'), may hold values from -0.375 to 0.375
- attn_gain: float32 [1024], replicated, may hold values from 0.1 to 1.9
- ffn_gain: float32 [1024], replicated, may hold values from 0.1 to 1.9
- q_gain: float32 [64], replicated, may hold values from 0.1 to 1.9
- k_gain: float32 [64], replicated, may hold values from 0.1 to 1.9
Outputs:
- output: bfloat16 [16, 1024, 1024], P('dp', 'seq')
- input_grad: bfloat16 [16, 1024, 1024], P('dp', 'seq')
- q_weight_grad: float32 [1024, 1024], P('dp')
- k_weight_grad: float32 [1024, 512], P('dp')
- v_weight_grad: float32 [1024, 512], P('dp')
- out_weight_grad: float32 [1024, 1024], P('dp')
- gate_weight_grad: float32 [1024, 4608], P('dp')
- up_weight_grad: float32 [1024, 4608], P('dp')
- down_weight_grad: float32 [1024, 4608], P('dp')
- attn_gain_grad: float32 [1024], replicated
- ffn_gain_grad: float32 [1024], replicated
- q_gain_grad: float32 [64], replicated
- k_gain_grad: float32 [64], replicated
Inputs may be any that keep to these rules, and one draw needn't show every extreme that they name: Along each sequence the positions rise by 1 to 4 from one token to the next, the first being 0; in one sequence every step is 4.
All inputs are finite; a program needn't handle non-finite values.
Results may differ from a plain program's by a relative error of at most 0.02.
Values may be sent and summed in bfloat16 or wider, within the bound.
No kernel may reach another device: no remote copies, remote signals or barrier semaphores. Data moves between devices by JAX's collectives and lax.ppermute only.
A program may use at most 320 MiB of HBM per device.

v0:
```python
import jax
import jax.numpy as jnp
from jax import lax
from jax.sharding import PartitionSpec as P

epsilon = 1e-05
rope_base = 1000000.0
contract_last = (((1,), (1,)), ((), ()))
contract_first = (((0,), (0,)), ((), ()))


def rms_scale(value_heads):
    return lax.rsqrt(jnp.mean(value_heads * value_heads, axis=-1, keepdims=True) + epsilon)


def rotate(value_heads, cosines, sine_table):
    half_dim = value_heads.shape[-1] // 2
    first_half = value_heads[..., :half_dim]
    second_half = value_heads[..., half_dim:]
    return jnp.concatenate(
        [
            first_half * cosines - second_half * sine_table,
            second_half * cosines + first_half * sine_table,
        ],
        axis=-1,
    )


def unrotate(grads_in, cosines, sine_table):
    half_dim = grads_in.shape[-1] // 2
    first_half = grads_in[..., :half_dim]
    second_half = grads_in[..., half_dim:]
    return jnp.concatenate(
        [
            first_half * cosines + second_half * sine_table,
            second_half * cosines - first_half * sine_table,
        ],
        axis=-1,
    )


def angles(positions, head_dim):
    freq_index = jnp.arange(head_dim // 2, dtype=jnp.float32)
    inverse = rope_base ** (-(2.0 * freq_index) / head_dim)
    turned = positions.astype(jnp.float32)[:, None] * inverse[None, :]
    return (jnp.cos(turned)[:, None, :], jnp.sin(turned)[:, None, :])


def norm_back(grad_out, normed_hat, inv_scale, gain):
    scaled = grad_out * gain
    return inv_scale * (scaled - normed_hat * jnp.mean(scaled * normed_hat, axis=-1, keepdims=True))


def matmul(left, right):
    return jnp.dot(left, right, preferred_element_type=jnp.float32)


def matmul_t(left, right):
    return lax.dot_general(left, right, contract_last, preferred_element_type=jnp.float32)


def matmul_tn(left, right):
    return lax.dot_general(left, right, contract_first, preferred_element_type=jnp.float32)


def reduce_rows(term_fn, keep_rows):
    return lax.psum_scatter(
        term_fn(jnp.int32(0), lax.axis_size(("dp", "seq")) * keep_rows),
        ("dp", "seq"),
        scatter_dimension=0,
        tiled=True,
    )


def local(
    tokens,
    positions,
    cotangent,
    q_weight,
    key_matrix,
    value_matrix,
    out_weight,
    gate_weight,
    up_weight,
    down_weight,
    attn_gain,
    ffn_gain,
    q_gain,
    k_gain,
):
    seq_count, tok_local, model_width = tokens.shape
    rank_count = lax.axis_size("seq")
    row_count = seq_count * tok_local
    head_dim = q_gain.shape[0]
    q_cols = q_weight.shape[1]
    kv_cols = key_matrix.shape[1]
    ff_width = gate_weight.shape[1]
    local_q = q_cols // head_dim // rank_count
    local_kv = kv_cols // head_dim // rank_count
    group_size = local_q // local_kv
    sequence_length = tok_local * rank_count
    block_rows = min(512, sequence_length)
    block_count = sequence_length // block_rows
    score_scale = head_dim ** (-0.5)
    keep_rows = model_width // (lax.axis_size("dp") * rank_count)
    f32 = jnp.float32
    bf16 = jnp.bfloat16
    flat_in = tokens.reshape(row_count, model_width).astype(f32)
    in_scale = rms_scale(flat_in)
    in_hat = flat_in * in_scale
    normed_in = (in_hat * attn_gain).astype(bf16)
    q_part = lax.all_gather(q_weight, "dp", axis=0, tiled=True)
    k_part = lax.all_gather(key_matrix, "dp", axis=0, tiled=True)
    v_part = lax.all_gather(value_matrix, "dp", axis=0, tiled=True)
    out_part = lax.all_gather(out_weight, "dp", axis=0, tiled=True)
    columns = normed_in
    q_proj = matmul(columns, q_part)
    key_projected = matmul(columns, k_part)
    v_proj = matmul(columns, v_part)
    out_full = out_part
    cosines, sine_table = angles(positions.reshape(row_count), head_dim)
    q_heads = q_proj.reshape(row_count, q_cols // head_dim, head_dim)
    q_inv = rms_scale(q_heads)
    q_hat = q_heads * q_inv
    query_rows_all = rotate(q_hat * q_gain, cosines, sine_table).astype(bf16)
    key_heads = key_projected.reshape(row_count, kv_cols // head_dim, head_dim)
    k_inv = rms_scale(key_heads)
    k_hat = key_heads * k_inv
    key_rows = rotate(k_hat * k_gain, cosines, sine_table).astype(bf16)
    value_rows = v_proj.astype(bf16)
    q_send = query_rows_all.reshape(seq_count, tok_local, rank_count, local_q * head_dim)
    kv_send = jnp.concatenate(
        [
            key_rows.reshape(seq_count, tok_local, rank_count, local_kv * head_dim),
            value_rows.reshape(seq_count, tok_local, rank_count, local_kv * head_dim),
        ],
        axis=3,
    )
    q_here, kv_here = (
        lax.all_to_all(q_send, "seq", split_axis=2, concat_axis=1, tiled=True),
        lax.all_to_all(kv_send, "seq", split_axis=2, concat_axis=1, tiled=True),
    )
    q_local = q_here.reshape(seq_count, sequence_length, local_kv, group_size, head_dim)
    k_local = kv_here[:, :, 0, : local_kv * head_dim].reshape(
        seq_count, sequence_length, local_kv, head_dim
    )
    v_local = kv_here[:, :, 0, local_kv * head_dim :].reshape(
        seq_count, sequence_length, local_kv, head_dim
    )

    def block_scores(q_block, block_index):
        key_span = (block_index + 1) * block_rows
        raw_scores = (
            jnp.einsum(
                "sqhgd,skhd->shgqk", q_block, k_local[:, :key_span], preferred_element_type=f32
            )
            * score_scale
        )
        query_pos = block_index * block_rows + jnp.arange(block_rows)[:, None]
        key_pos = jnp.arange(key_span)[None, :]
        return jnp.where(key_pos <= query_pos, raw_scores, -1e30)

    attended_list = []
    log_list = []
    for block_index in range(block_count):
        row_lo = block_index * block_rows
        key_span = row_lo + block_rows
        scores = block_scores(q_local[:, row_lo : row_lo + block_rows], block_index)
        row_max = jnp.max(scores, axis=-1, keepdims=True)
        exp_terms = jnp.exp(scores - row_max)
        summed = jnp.sum(exp_terms, axis=-1, keepdims=True)
        probs = exp_terms / summed
        log_list.append(row_max + jnp.log(summed))
        attended_list.append(
            jnp.einsum(
                "shgqk,skhd->sqhgd",
                probs.astype(bf16),
                v_local[:, :key_span],
                preferred_element_type=f32,
            )
        )
    attended_output = jnp.concatenate(attended_list, axis=1)
    log_total = jnp.concatenate(log_list, axis=3)
    mixed_send = attended_output.astype(bf16).reshape(
        seq_count, sequence_length, 1, local_q * head_dim
    )
    mixed_back = lax.all_to_all(mixed_send, "seq", split_axis=1, concat_axis=2, tiled=True)
    mixed_rows = mixed_back.reshape(row_count, q_cols)
    residual = flat_in + matmul_t(mixed_rows, out_full)
    mid_scale = rms_scale(residual)
    mid_hat = residual * mid_scale
    normed_mid = (mid_hat * ffn_gain).astype(bf16)
    gate_part = lax.all_gather(gate_weight, "dp", axis=0, tiled=True)
    up_part = lax.all_gather(up_weight, "dp", axis=0, tiled=True)
    columns = normed_mid
    gate_proj = matmul(columns, gate_part)
    up_proj = matmul(columns, up_part)
    sigmoid_gate = jax.nn.sigmoid(gate_proj)
    activated = gate_proj * sigmoid_gate
    hidden = (activated * up_proj).astype(bf16)
    ffn_branch = matmul_t(hidden, lax.all_gather(down_weight, "dp", axis=0, tiled=True))
    output = (residual + ffn_branch).astype(bf16).reshape(seq_count, tok_local, model_width)
    d_ffn = cotangent.reshape(row_count, model_width)
    columns = d_ffn
    d_hidden = matmul(columns, lax.all_gather(down_weight, "dp", axis=0, tiled=True))
    d_gate = (d_hidden * up_proj * sigmoid_gate * (1.0 + gate_proj * (1.0 - sigmoid_gate))).astype(
        bf16
    )
    d_up = (d_hidden * activated).astype(bf16)
    gate_part, up_part = lax.all_gather((gate_weight, up_weight), "dp", axis=0, tiled=True)
    d_mid = matmul_t(d_gate, gate_part) + matmul_t(d_up, up_part)
    ffn_gain_part = jnp.sum(d_mid * mid_hat, axis=0)
    d_resid = d_ffn.astype(f32) + norm_back(d_mid, mid_hat, mid_scale, ffn_gain)
    d_attn = d_resid.astype(bf16)
    d_mixed = matmul(d_attn, out_full).astype(bf16)
    d_mixed_send = d_mixed.reshape(seq_count, tok_local, rank_count, local_q * head_dim)
    d_mixed_here = lax.all_to_all(d_mixed_send, "seq", split_axis=2, concat_axis=1, tiled=True)
    d_mixed_local = d_mixed_here.reshape(seq_count, sequence_length, local_kv, group_size, head_dim)
    d_key = jnp.zeros((seq_count, sequence_length, local_kv, head_dim), f32)
    d_value = jnp.zeros((seq_count, sequence_length, local_kv, head_dim), f32)
    d_query_list = []
    for block_index in range(block_count):
        row_lo = block_index * block_rows
        key_span = row_lo + block_rows
        q_block = q_local[:, row_lo : row_lo + block_rows]
        grad_block = d_mixed_local[:, row_lo : row_lo + block_rows]
        probs = jnp.exp(
            block_scores(q_block, block_index) - log_total[:, :, :, row_lo : row_lo + block_rows]
        )
        d_value = d_value.at[:, :key_span].add(
            jnp.einsum(
                "shgqk,sqhgd->skhd", probs.astype(bf16), grad_block, preferred_element_type=f32
            )
        )
        d_weights = jnp.einsum(
            "sqhgd,skhd->shgqk", grad_block, v_local[:, :key_span], preferred_element_type=f32
        )
        delta = jnp.sum(
            grad_block.astype(f32) * attended_output[:, row_lo : row_lo + block_rows], axis=-1
        )
        delta = jnp.transpose(delta, (0, 2, 3, 1))[..., None]
        d_scores = (probs * (d_weights - delta)).astype(bf16)
        d_query_list.append(
            jnp.einsum(
                "shgqk,skhd->sqhgd", d_scores, k_local[:, :key_span], preferred_element_type=f32
            )
            * score_scale
        )
        d_key = d_key.at[:, :key_span].add(
            jnp.einsum("shgqk,sqhgd->skhd", d_scores, q_block, preferred_element_type=f32)
            * score_scale
        )
    d_query = (
        jnp.concatenate(d_query_list, axis=1)
        .astype(bf16)
        .reshape(seq_count, sequence_length, 1, local_q * head_dim)
    )
    d_kv = jnp.concatenate(
        [
            d_key.astype(bf16).reshape(seq_count, sequence_length, 1, local_kv * head_dim),
            d_value.astype(bf16).reshape(seq_count, sequence_length, 1, local_kv * head_dim),
        ],
        axis=3,
    )
    d_query_rows, d_kv_rows = (
        lax.all_to_all(d_query, "seq", split_axis=1, concat_axis=2, tiled=True),
        lax.all_to_all(d_kv, "seq", split_axis=1, concat_axis=2, tiled=True),
    )
    d_q_rot = d_query_rows.reshape(row_count, q_cols // head_dim, head_dim).astype(f32)
    d_k_rot = (
        d_kv_rows[..., : local_kv * head_dim]
        .reshape(row_count, kv_cols // head_dim, head_dim)
        .astype(f32)
    )
    d_v_proj = d_kv_rows[..., local_kv * head_dim :].reshape(row_count, kv_cols)
    d_q_normed = unrotate(d_q_rot, cosines, sine_table)
    d_k_normed = unrotate(d_k_rot, cosines, sine_table)
    q_gain_part = jnp.sum(d_q_normed * q_hat, axis=(0, 1))
    k_gain_part = jnp.sum(d_k_normed * k_hat, axis=(0, 1))
    d_q_proj = norm_back(d_q_normed, q_hat, q_inv, q_gain).reshape(row_count, q_cols).astype(bf16)
    d_k_proj = norm_back(d_k_normed, k_hat, k_inv, k_gain).reshape(row_count, kv_cols).astype(bf16)
    q_part, k_part, v_part = lax.all_gather(
        (q_weight, key_matrix, value_matrix), "dp", axis=0, tiled=True
    )
    d_normed_in = (
        matmul_t(d_q_proj, q_part) + matmul_t(d_k_proj, k_part) + matmul_t(d_v_proj, v_part)
    )
    attn_gain_part = jnp.sum(d_normed_in * in_hat, axis=0)
    input_grad = (
        (d_resid + norm_back(d_normed_in, in_hat, in_scale, attn_gain))
        .astype(bf16)
        .reshape(seq_count, tok_local, model_width)
    )

    def every_term(offset, amount):
        return jnp.concatenate(
            [
                jnp.concatenate(
                    [
                        matmul_tn(normed_mid, d_gate),
                        matmul_tn(normed_mid, d_up),
                        matmul_tn(d_ffn, hidden),
                    ],
                    axis=1,
                ),
                matmul_tn(d_attn, mixed_rows),
                jnp.concatenate(
                    [
                        matmul_tn(normed_in, d_q_proj),
                        matmul_tn(normed_in, d_k_proj),
                        matmul_tn(normed_in, d_v_proj),
                    ],
                    axis=1,
                ),
            ],
            axis=1,
        )

    combined = reduce_rows(every_term, keep_rows)
    ffn_part = combined[:, : 3 * ff_width]
    out_part = combined[:, 3 * ff_width : 3 * ff_width + q_cols]
    first_part = combined[:, 3 * ff_width + q_cols :]
    ffn_full, out_grad, first_full = (
        lax.all_gather(ffn_part.astype(jnp.bfloat16), "seq", axis=0, tiled=True).astype(
            ffn_part.dtype
        ),
        lax.all_gather(out_part.astype(jnp.bfloat16), "seq", axis=0, tiled=True).astype(
            out_part.dtype
        ),
        lax.all_gather(first_part.astype(jnp.bfloat16), "seq", axis=0, tiled=True).astype(
            first_part.dtype
        ),
    )
    gain_grads = lax.psum((attn_gain_part, ffn_gain_part, q_gain_part, k_gain_part), ("dp", "seq"))
    return (
        output,
        input_grad,
        first_full[:, :q_cols],
        first_full[:, q_cols : q_cols + kv_cols],
        first_full[:, q_cols + kv_cols :],
        out_grad,
        ffn_full[:, :ff_width],
        ffn_full[:, ff_width : 2 * ff_width],
        ffn_full[:, 2 * ff_width :],
        gain_grads[0],
        gain_grads[1],
        gain_grads[2],
        gain_grads[3],
    )


def solution(mesh):
    in_specs = (
        P("dp", "seq", None),
        P("dp", "seq"),
        P("dp", "seq", None),
        P("dp", None),
        P("dp", None),
        P("dp", None),
        P("dp", None),
        P("dp", None),
        P("dp", None),
        P("dp", None),
        P(),
        P(),
        P(),
        P(),
    )
    out_specs = (
        P("dp", "seq", None),
        P("dp", "seq", None),
        P("dp", None),
        P("dp", None),
        P("dp", None),
        P("dp", None),
        P("dp", None),
        P("dp", None),
        P("dp", None),
        P(),
        P(),
        P(),
        P(),
    )
    return jax.shard_map(local, mesh=mesh, in_specs=in_specs, out_specs=out_specs, check_vma=False)
```

profile of v0, /device:TPU:0, one launch (start us, length us, event | category | flops | bytes accessed | tf_op | source)
XLA Modules:
  0.0 1240.8 jit_solution(9845809243946968209)
XLA Ops:
  13.9 22.2 %all-gather.11.cloned.1.call-done = bf16[1024,512]{1,0:T(8,128)(2,1)} async-done(((bf16[128,512]{1,0:T(8,128)(2,1)}), bf16[1024,512]{1,0:T(8,128)(2,1)}) %all-gather.11.cloned.1.call-update) | async-done | bytes 1048592 | tf_op jit(solution)/shard_map/all_gather | solution.py:114
  40.9 20.6 %all-gather.9.cloned.1.call-done = bf16[1024,512]{1,0:T(8,128)(2,1)} async-done(((bf16[128,512]{1,0:T(8,128)(2,1)}), bf16[1024,512]{1,0:T(8,128)(2,1)}) %all-gather.9.cloned.1.call-update) | async-done | bytes 1048592 | tf_op jit(solution)/shard_map/all_gather | solution.py:113
  72.6 18.8 %all-gather.13.cloned.1.call-done = bf16[1024,1024]{1,0:T(8,128)(2,1)} async-done(((bf16[128,1024]{1,0:T(8,128)(2,1)}), bf16[1024,1024]{1,0:T(8,128)(2,1)}) %all-gather.13.cloned.1.call-update) | async-done | bytes 2097168 | tf_op jit(solution)/shard_map/all_gather | solution.py:112
  110.1 22.6 %all-to-all-done.1 = bf16[2,256,4,256]{1,0,3,2:T(2,128)(2,1)S(1)} async-done(((bf16[2,256,4,256]{1,0,3,2:T(2,128)(2,1)}), bf16[2,256,4,256]{1,0,3,2:T(2,128)(2,1)S(1)}, u32[]{:S(2)}, u32[]{:S(2)}) %all-to-all-start.1) | async-done | bytes 1048608 | tf_op jit(solution)/shard_map/all_to_all | solution.py:140
  144.0 7.8 fusion.5
  151.9 10.3 fusion.2
  162.2 9.4 fusion.84
  178.1 25.7 %all-to-all-done.2 = bf16[2,1024,1,256]{3,0,2,1:T(2,128)(2,1)S(1)} async-done(((bf16[2,1024,1,256]{3,0,2,1:T(2,128)(2,1)}), bf16[2,1024,1,256]{3,0,2,1:T(2,128)(2,1)S(1)}, u32[]{:S(2)}, u32[]{:S(2)}) %all-to-all-start.2) | async-done | bytes 1048608 | tf_op jit(solution)/shard_map/all_to_all | solution.py:187
  209.6 12.3 fusion.87
  221.9 20.3 %all-gather.17.cloned.1.call-done = bf16[1024,4608]{1,0:T(8,128)(2,1)} async-done(((bf16[128,4608]{1,0:T(8,128)(2,1)}), bf16[1024,4608]{1,0:T(8,128)(2,1)}) %all-gather.17.cloned.1.call-update) | async-done | bytes 9437200 | tf_op jit(solution)/shard_map/all_gather | solution.py:193
  242.3 11.0 fusion.86
  253.3 49.7 %all-gather.21.cloned.1.call-done = bf16[1024,4608]{1,0:T(8,128)(2,1)} async-done(((bf16[128,4608]{1,0:T(8,128)(2,1)}), bf16[1024,4608]{1,0:T(8,128)(2,1)}) %all-gather.21.cloned.1.call-update) | async-done | bytes 9437200 | tf_op jit(solution)/shard_map/all_gather | solution.py:201
  303.0 17.6 %multiply_convert_fusion = (bf16[512,4608]{1,0:T(8,128)(2,1)}, bf16[512,4608]{1,0:T(8,128)(2,1)}, bf16[512,4608]{1,0:T(8,128)(2,1)}) fusion(f32[512,4608]{1,0:T(8,128)} %fusion.86, f32[512,4608]{1,0:T(8,128)} %fusion.87, bf16[512,1024]{1,0:T(8,128)(2,1)} %bitcast.306, bf16[1024,4608]{1,0:T(8,128)(2,1)} %all-gather.21.cloned.1.call-done), kind=kOutput, calls=%fused_computation.12 | convolution fusion | flops 4867227648 | bytes 43515904 | tf_op jit(solution)/shard_map/dot_general | solution.py:55
  320.6 9.2 fusion.88
  329.8 8.1 multiply_reduce_fusion.1
  347.6 5.0 all-to-all-start.3
  352.6 11.8 convolution_dynamic-update-slice_fusion.1
  364.4 11.6 convolution_dynamic-update-slice_fusion
  383.7 5.9 fusion.50
  390.1 6.4 fusion.7
  396.5 8.9 fusion.44
  405.4 11.1 fusion.1
  422.1 6.8 fusion.47
  437.6 11.8 bitcast_dynamic-update-slice_fusion
  465.0 5.0 all-to-all-start.4
  485.6 9.2 all-to-all-done.4
  517.6 613.0 %reduce-scatter.2.cloned.1.call-done = f32[32,16896]{1,0:T(8,128)} async-done(((f32[1024,16896]{1,0:T(8,128)}), f32[32,16896]{1,0:T(8,128)}) %reduce-scatter.2.cloned.1.call-update) | async-done | bytes 2162704 | tf_op jit(solution)/shard_map/reduce_scatter | solution.py:67
  1134.4 10.3 add_convert_fusion
  1149.6 42.6 %all-reduce.2 = (f32[1024]{0:T(1024)}, f32[1024]{0:T(1024)}, f32[64]{0:T(128)}, f32[64]{0:T(128)}) all-reduce(f32[1024]{0:T(1024)S(1)} %get-tuple-element.81, f32[1024]{0:T(1024)S(1)} %get-tuple-element.79, f32[64]{0:T(128)S(1)} %get-tuple-element.77, f32[64]{0:T(128)S(1)} %get-tuple-element.83), channel_id=1, replica_groups=mesh['dp'=8,'seq'=4] {'dp','seq'}, use_global_device_ids=true, to_apply=%region_16.17 | all-reduce | flops 2176 | bytes 17408 | tf_op jit(solution)/shard_map/psum | solution.py:334
  1195.3 15.5 %all_gather.44 = bf16[128,1024]{1,0:T(8,128)(2,1)S(1)} all-gather(bf16[32,1024]{1,0:T(8,128)(2,1)S(1)} %slice-done), channel_id=1, replica_groups=mesh['dp'=8,'seq'=4] {'seq'}, dimensions={0}, use_global_device_ids=true | all-gather | bytes 327680 | tf_op jit(solution)/shard_map/all_gather | solution.py:327
  1211.7 15.5 %all_gather.43 = bf16[128,2048]{1,0:T(8,128)(2,1)S(1)} all-gather(bf16[32,2048]{1,0:T(8,128)(2,1)S(1)} %slice-done.1), channel_id=1, replica_groups=mesh['dp'=8,'seq'=4] {'seq'}, dimensions={0}, use_global_device_ids=true | all-gather | bytes 655360 | tf_op jit(solution)/shard_map/all_gather | solution.py:330
  1228.8 5.2 fusion.80
  (237 shorter events, 164.4 us)
Async XLA Ops:
  7.2 28.9 %all-gather.11.cloned.1.call-start = ((), (), s32[]{:S(2)}) async-start(), calls=%async_computation.8 | async-start | bytes 1179648 | tf_op jit(solution)/shard_map/all_gather | solution.py:114
  7.9 53.6 %all-gather.9.cloned.1.call-start = ((), (), s32[]{:S(2)}) async-start(), calls=%async_computation.7 | async-start | bytes 1179648 | tf_op jit(solution)/shard_map/all_gather | solution.py:113
  8.7 82.7 %all-gather.13.cloned.1.call-start = ((), (), s32[]{:S(2)}) async-start(), calls=%async_computation.9 | async-start | bytes 2359296 | tf_op jit(solution)/shard_map/all_gather | solution.py:112
  9.4 196.6 %all-gather.15.cloned.1.call-start = ((), (), s32[]{:S(2)}) async-start(), calls=%async_computation.10 | async-start | bytes 2359296 | tf_op jit(solution)/shard_map/all_gather | solution.py:115
  10.0 199.6 %all-gather.19.cloned.1.call-start = ((), (), s32[]{:S(2)}) async-start(), calls=%async_computation.12 | async-start | bytes 10616832 | tf_op jit(solution)/shard_map/all_gather | solution.py:194
  10.6 231.7 %all-gather.17.cloned.1.call-start = ((), (), s32[]{:S(2)}) async-start(), calls=%async_computation.11 | async-start | bytes 10616832 | tf_op jit(solution)/shard_map/all_gather | solution.py:193
  11.2 291.8 %all-gather.21.cloned.1.call-start = ((), (), s32[]{:S(2)}) async-start(), calls=%async_computation.13 | async-start | bytes 10616832 | tf_op jit(solution)/shard_map/all_gather | solution.py:201
  13.3 82.1 %copy-start.11 = (bf16[2,256,1024]{2,1,0:T(8,128)(2,1)}, bf16[2,256,1024]{2,1,0:T(8,128)(2,1)S(1)}, u32[]{:S(2)}) copy-start(bf16[2,256,1024]{2,1,0:T(8,128)(2,1)S(1)} %fusion.32) | copy-start | bytes 3145732
  13.9 86.1 %copy-start.26 = (f32[512,32]{0,1:T(8,128)}, f32[512,32]{0,1:T(8,128)S(1)}, u32[]{:S(2)}) copy-start(f32[512,32]{0,1:T(8,128)S(1)} %get-tuple-element.111) | copy-start | bytes 196612
  13.9 86.1 %copy-start.28 = (f32[512,32]{0,1:T(8,128)}, f32[512,32]{0,1:T(8,128)S(1)}, u32[]{:S(2)}) copy-start(f32[512,32]{0,1:T(8,128)S(1)} %get-tuple-element.112) | copy-start | bytes 196612
  38.9 25.9 %copy-start.50 = (f32[64]{0:T(128)S(1)}, f32[64]{0:T(128)}, u32[]{:S(2)}) copy-start(f32[64]{0:T(128)} %param.39) | copy-start | bytes 772
  68.0 33.6 %all-to-all-start = ((bf16[2,256,4,256]{3,1,0,2:T(8,128)(2,1)}), bf16[2,256,4,256]{3,1,0,2:T(8,128)(2,1)S(1)}, u32[]{:S(2)}, u32[]{:S(2)}) async-start(bf16[2,256,4,256]{3,1,0,2:T(8,128)(2,1)} %pad_maximum_fusion.1), calls=%async_computation | async-start | bytes 2097152 | tf_op jit(solution)/shard_map/all_to_all | solution.py:141
  101.6 31.0 %all-to-all-start.1 = ((bf16[2,256,4,256]{1,0,3,2:T(2,128)(2,1)}), bf16[2,256,4,256]{1,0,3,2:T(2,128)(2,1)S(1)}, u32[]{:S(2)}, u32[]{:S(2)}) async-start(bf16[2,256,4,256]{1,0,3,2:T(2,128)(2,1)} %convert_element_type.176), calls=%async_computation.1 | async-start | bytes 2097152 | tf_op jit(solution)/shard_map/all_to_all | solution.py:140
  134.2 9.8 copy-start.14
  151.9 10.3 copy-start.39
  162.2 9.8 copy-start.25
  174.4 29.5 %all-to-all-start.2 = ((bf16[2,1024,1,256]{3,0,2,1:T(2,128)(2,1)}), bf16[2,1024,1,256]{3,0,2,1:T(2,128)(2,1)S(1)}, u32[]{:S(2)}, u32[]{:S(2)}) async-start(bf16[2,1024,1,256]{3,0,2,1:T(2,128)(2,1)} %pad_maximum_fusion.3), calls=%async_computation.2 | async-start | bytes 2097152 | tf_op jit(solution)/shard_map/all_to_all | solution.py:187
  209.3 120.5 %copy-start.7 = (f32[512,1024]{1,0:T(8,128)}, f32[512,1024]{1,0:T(8,128)S(1)}, u32[]{:S(2)}) copy-start(f32[512,1024]{1,0:T(8,128)S(1)} %get-tuple-element.128) | copy-start | bytes 6291460
  347.6 31.3 %all-to-all-start.3 = ((bf16[2,256,4,256]{1,3,0,2:T(8,128)(2,1)}), bf16[2,256,4,256]{1,3,0,2:T(8,128)(2,1)}, u32[]{:S(2)}, u32[]{:S(2)}) async-start(bf16[2,256,4,256]{1,3,0,2:T(8,128)(2,1)} %copy.117), calls=%async_computation.3 | async-start | bytes 2097152 | tf_op jit(solution)/shard_map/all_to_all | solution.py:217
  383.6 12.9 %copy-start.17 = (bf16[2,1024,2,2,64]{1,4,3,2,0:T(8,128)(2,1)}, bf16[2,1024,2,2,64]{1,4,3,2,0:T(8,128)(2,1)S(1)}, u32[]{:S(2)}) copy-start(bf16[2,1024,2,2,64]{1,4,3,2,0:T(8,128)(2,1)S(1)} %reshape.504) | copy-start | bytes 3145732
  405.4 13.2 %copy-start.15 = (bf16[2,1024,2,2,64]{1,4,3,2,0:T(8,128)(2,1)S(1)}, bf16[2,1024,2,2,64]{1,4,3,2,0:T(8,128)(2,1)}, u32[]{:S(2)}) copy-start(bf16[2,1024,2,2,64]{1,4,3,2,0:T(8,128)(2,1)} %copy-done.14) | copy-start | bytes 3145732
  433.3 31.6 %all-to-all-start.5 = ((bf16[2,1024,1,256]{3,0,2,1:T(2,128)(2,1)}), bf16[2,1024,1,256]{3,0,2,1:T(2,128)(2,1)}, u32[]{:S(2)}, u32[]{:S(2)}) async-start(bf16[2,1024,1,256]{3,0,2,1:T(2,128)(2,1)} %pad_maximum_fusion.5), calls=%async_computation.5 | async-start | bytes 2097152 | tf_op jit(solution)/shard_map/all_to_all | solution.py:267
  437.6 11.9 copy-start.19
  455.5 14.7 %copy-start.16 = (bf16[64,8,4,256]{3,1,2,0:T(8,128)(2,1)S(1)}, bf16[64,8,4,256]{3,1,2,0:T(8,128)(2,1)}, u32[]{:S(2)}) copy-start(bf16[64,8,4,256]{3,1,2,0:T(8,128)(2,1)} %copy.162) | copy-start | bytes 3145732
  465.0 29.9 %all-to-all-start.4 = ((bf16[2,1024,1,256]{3,0,2,1:T(2,128)(2,1)}), bf16[2,1024,1,256]{3,0,2,1:T(2,128)(2,1)}, u32[]{:S(2)}, u32[]{:S(2)}) async-start(bf16[2,1024,1,256]{3,0,2,1:T(2,128)(2,1)} %pad_maximum_fusion.4), calls=%async_computation.4 | async-start | bytes 2097152 | tf_op jit(solution)/shard_map/all_to_all | solution.py:266
  470.0 660.6 %reduce-scatter.2.cloned.1.call-start = ((), (), s32[]{:S(2)}) async-start(), calls=%async_computation.14 | async-start | bytes 71368704 | tf_op jit(solution)/shard_map/reduce_scatter | solution.py:67
  517.3 711.5 %all-gather.23.cloned.1.call-start = ((), (), s32[]{:S(2)}) async-start(), calls=%async_computation.15 | async-start | bytes 4423680 | tf_op jit(solution)/shard_map/all_gather | solution.py:324
  1134.3 10.3 copy-start.13
  1134.3 11.1 copy-start.24
  1134.3 11.1 copy-start.35
  1149.6 45.7 %slice-start = ((bf16[32,16896]{1,0:T(8,128)(2,1)}), bf16[32,1024]{1,0:T(8,128)(2,1)S(1)}, s32[]{:S(2)}) async-start(bf16[32,16896]{1,0:T(8,128)(2,1)} %copy-done.10), calls=%async_computation.16 | async-start | bytes 131072 | tf_op jit(solution)/shard_map/slice | solution.py:321
  1149.6 62.1 %slice-start.1 = ((bf16[32,16896]{1,0:T(8,128)(2,1)}), bf16[32,2048]{1,0:T(8,128)(2,1)S(1)}, s32[]{:S(2)}) async-start(bf16[32,16896]{1,0:T(8,128)(2,1)} %copy-done.10), calls=%async_computation.17 | async-start | bytes 262144 | tf_op jit(solution)/shard_map/slice | solution.py:322
  (38 other events, 175.5 us)
Sparse Core Ops, SparseCore 0:
  9.9 26.1 all-gather.10
  38.0 23.4 all-gather.8
  63.5 27.8 all-gather.12
  93.1 27.8 all-gather.14
  122.8 58.8 all-gather.18
  183.4 58.8 all-gather.16
  244.1 58.8 all-gather.20
  517.5 613.1 reduce-scatter.1
  1134.5 73.3 all-gather.22
where the time goes:
time: 1250 us; the launch traced here: 1240 us
  waiting for transfers between devices  809 us (65%)
  matrix products  206 us (16%)
  blocking collectives  73.6 us (6%)
  local copies, waits for them, and re-layouts  63 us (5%)
  other arithmetic  45.4 us (4%)
  starting transfers between devices  28.2 us (2%)
  between operations  15.1 us (1%)
    reduce_scatter x1, waiting for transfers between devices, reduce_rows(): lax.psum_scatter(term_fn(jnp.int32(0), lax.axis_size(('dp', 'seq')) * kee...  613 us
    all_gather x1, waiting for transfers between devices, local(): lax.all_gather(down_weight, 'dp', axis=0, tiled=True)  49.7 us
    dot_general x7, matrix products, matmul(): return jnp.dot(left, right, preferred_element_type=jnp.float32)  49.6 us
    dot_general x7, matrix products, matmul_tn(): lax.dot_general(left, right, contract_first, preferred_element_type=jnp.f...  46.4 us
    psum x1, blocking collectives, local(): lax.psum((attn_gain_part, ffn_gain_part, q_gain_part, k_gain_part), ('dp'...  42.6 us
    dot_general x7, matrix products, matmul_t(): lax.dot_general(left, right, contract_last, preferred_element_type=jnp.fl...  35.4 us
    all_to_all x1, waiting for transfers between devices, local(): lax.all_to_all(mixed_send, 'seq', split_axis=1, concat_axis=2, tiled=True)  25.7 us
  transfers between devices with their start and end apart: 15, of which 10 were waited for; matrix products, arithmetic and copies ran while one was open for 15% of the time, Pallas kernels for 0%

commit v1 on v0

v1 whole, which is shorter than its diff:
```python
import functools

import jax
import jax.numpy as jnp
from jax import lax
from jax.experimental import pallas as pl
from jax.experimental.pallas import tpu as pltpu
from jax.sharding import Mesh, PartitionSpec as P

epsilon = 1e-05
rope_base = 1000000.0
f32 = jnp.float32
bf16 = jnp.bfloat16
SWAP = ((0, 1), (1, 0))
EVERY = ("o", "x", "c", "z", "s")
NT = (((1,), (1,)), ((), ()))
NN = (((1,), (0,)), ((), ()))


def dot(left, right, dims=NN):
    return lax.dot_general(left, right, dims, preferred_element_type=f32)


def rms_scale(rows):
    return lax.rsqrt(jnp.mean(rows * rows, axis=-1, keepdims=True) + epsilon)


def norm_back(grad_out, normed_hat, inv_scale, gain):
    scaled = grad_out * gain
    return inv_scale * (scaled - normed_hat * jnp.mean(scaled * normed_hat, axis=-1, keepdims=True))


def square():
    return lax.axis_size("o") == 2 and lax.axis_size("x") == 2


def pair_group():
    return lax.axis_size("s") == 1


def relative(array):
    if not square():
        return array
    quarter = array.shape[-1] // 4
    blocks = [array[..., i * quarter : (i + 1) * quarter] for i in range(4)]
    here_x = lax.axis_index("x") == 1
    here_o = lax.axis_index("o") == 1
    blocks = [jnp.where(here_x, blocks[i ^ 1], blocks[i]) for i in range(4)]
    blocks = [jnp.where(here_o, blocks[i ^ 2], blocks[i]) for i in range(4)]
    return jnp.concatenate(blocks, axis=-1)


def by_core(own, other, axis):
    first = lax.axis_index("c") == 0
    return jnp.concatenate([jnp.where(first, own, other), jnp.where(first, other, own)], axis=axis)


def swap_core(array):
    return lax.ppermute(array, "c", SWAP)


def half_of(array, axis, which):
    size = array.shape[axis] // 2
    low = lax.slice_in_dim(array, 0, size, axis=axis)
    high = lax.slice_in_dim(array, size, 2 * size, axis=axis)
    return jnp.where(which == 0, low, high)


def group_gather(rows):
    if pair_group():
        return by_core(rows[None], swap_core(rows)[None], 0)
    return lax.all_gather(rows, ("s", "c"), axis=0)


def group_scatter(parts):
    if pair_group():
        core = lax.axis_index("c")
        away = sum(half_of(p, 0, 1 - core)[0].astype(f32) for p in parts).astype(bf16)
        mine = sum(half_of(p, 0, core)[0].astype(f32) for p in parts)
        return mine + swap_core(away).astype(f32)
    total = sum(p.astype(f32) for p in parts)
    return lax.psum_scatter(total, ("s", "c"), scatter_dimension=0, tiled=False)


def to_sequence(rows):
    core = lax.axis_index("c")
    away = half_of(rows, 1, 1 - core)
    mine = half_of(rows, 1, core)
    every = by_core(mine, swap_core(away), 0)
    return lax.all_to_all(every, "z", 0, 0, tiled=True)


def from_sequence(rows):
    core = lax.axis_index("c")
    every = lax.all_to_all(rows, "z", 0, 0, tiled=True)
    away = half_of(every, 0, 1 - core)
    mine = half_of(every, 0, core)
    return by_core(mine, swap_core(away), 1)


def gather_rows(parts):
    core = lax.axis_index("c")
    low, high = parts
    mine = jnp.where(core == 0, low, high)
    away = jnp.where(core == 0, high, low)
    own = by_core(mine, swap_core(away), 1)
    if square():
        half = own.shape[1] // 2
        by_x = lax.ppermute(own, "x", SWAP)
        by_o = lax.ppermute(own, "o", SWAP)
        diag_low = lax.ppermute(by_x[:, :half], "o", SWAP)
        diag_high = lax.ppermute(by_o[:, half:], "x", SWAP)
        return [own, by_x, by_o, diag_low, diag_high]
    return [lax.all_gather(own, ("o", "x"), axis=1, tiled=True)]


def grad_slots(model):
    if square():
        return [(2, 0), (3, 0), (0, 0), (3, 1), (2, 1), (1, 0), (0, 1), (1, 1)], [2, 2, 2, 2]
    return [(0, i) for i in range(8)], [8]


def line_sum(part):
    if lax.axis_size("z") != 4:
        return lax.psum(part.astype(f32), "z")
    at = lax.axis_index("z")
    total = part + lax.ppermute(part, "z", ((0, 1), (3, 2))).astype(f32)
    total = total.astype(bf16)
    total = (total.astype(f32) + lax.ppermute(total, "z", ((1, 2), (2, 1))).astype(f32)).astype(bf16)
    back = lax.ppermute(total, "z", ((1, 0), (2, 3)))
    return jnp.where((at == 0) | (at == 3), back, total)


def reduce_rows(outs):
    if square():
        send_a, send_b, keep_a, keep_b = outs
        half = keep_a.shape[1] // 2
        come_a = lax.ppermute(send_a, "x", SWAP)
        come_b = lax.ppermute(send_b, "o", SWAP)

        def add(left, right, which):
            span = slice(which * half, (which + 1) * half)
            return left[:, span].astype(f32) + right[:, span].astype(f32)

        last_a = lax.ppermute(add(keep_a, come_a, 1).astype(bf16), "o", SWAP)
        last_b = lax.ppermute(add(keep_b, come_b, 1).astype(bf16), "x", SWAP)
        low = (add(keep_a, come_a, 0) + last_a.astype(f32)).astype(bf16)
        high = (add(keep_b, come_b, 0) + last_b.astype(f32)).astype(bf16)
    else:
        full = lax.psum_scatter(outs[0].astype(f32), ("o", "x"), scatter_dimension=1, tiled=True)
        half = full.shape[1] // 2
        low, high = full[:, :half].astype(bf16), full[:, half:].astype(bf16)
    low, high = line_sum(low), line_sum(high)
    core = lax.axis_index("c")
    mine = jnp.where(core == 0, low, high)
    away = jnp.where(core == 0, high, low)
    if pair_group():
        other = swap_core(away)
        return [jnp.where(core == 0, mine, other), jnp.where(core == 0, other, mine)]
    both = by_core(mine[None], swap_core(away)[None], 0)
    every = lax.all_gather(both, "s", axis=0, tiled=True)
    return [every[i] for i in range(every.shape[0])]


def fill(scratch, refs, take):
    row = 0
    for ref in refs:
        block = take(ref)
        scratch[row : row + block.shape[0], :] = block
        row += block.shape[0]


def ffn_kernel(blocks, slots, steps, x_ref, xt_ref, cot_ref, cott_ref, *rest):
    weights, rest = rest[:blocks], rest[blocks:]
    outs = max(o for o, _ in slots) + 1
    out_ref, mid_ref = rest[0], rest[1]
    grads = rest[2 : 2 + outs]
    gate, up, down, hid, dgate, dup, out_acc, mid_acc = rest[2 + outs :]
    step = pl.program_id(0)
    for i, scratch in enumerate((gate, up, down)):
        fill(scratch, weights, lambda ref: ref[i])

    @pl.when(step == 0)
    def _():
        out_acc[...] = jnp.zeros_like(out_acc)
        mid_acc[...] = jnp.zeros_like(mid_acc)

    rows = 256

    def body(i, carry):
        at = pl.ds(pl.multiple_of(i * rows, rows), rows)
        x = x_ref[at, :]
        g = dot(x, gate[...])
        u = dot(x, up[...])
        dh = dot(cot_ref[at, :], down[...])
        sig = jax.nn.sigmoid(g)
        act = g * sig
        h = (act * u).astype(bf16)
        dg = (dh * u * sig * (1.0 + g * (1.0 - sig))).astype(bf16)
        du = (dh * act).astype(bf16)
        hid[at, :] = h
        dgate[at, :] = dg
        dup[at, :] = du
        out_acc[at, :] += dot(h, down[...], NT)
        mid_acc[at, :] += dot(dg, gate[...], NT) + dot(du, up[...], NT)
        return carry

    lax.fori_loop(0, x_ref.shape[0] // rows, body, 0)
    size = xt_ref.shape[0] // 8
    for block in range(4):
        at = slice(2 * block * size, 2 * (block + 1) * size)
        xt = xt_ref[at, :]
        three = (dot(xt, dgate[...]), dot(xt, dup[...]), dot(cott_ref[at, :], hid[...]))
        for i, term in enumerate(three):
            term = term.astype(bf16)
            for part in range(2):
                which, row = slots[2 * block + part]
                grads[which][i, row * size : (row + 1) * size, :] = term[
                    part * size : (part + 1) * size
                ]

    @pl.when(step == steps - 1)
    def _():
        out_ref[...] = out_acc[...].astype(bf16)
        mid_ref[...] = mid_acc[...].astype(bf16)


def whole_spec(shape):
    zeros = (0,) * len(shape)
    return pl.BlockSpec(shape, lambda *_: zeros)


def single_spec(shape):
    zeros = (0,) * len(shape)
    return pl.BlockSpec(shape, lambda *_: zeros, pipeline_mode=pl.Buffered(1))


def ffn_call(x, x_t, cot, cot_t, weights):
    rows, model = x.shape
    width = weights[0].shape[2]
    tile = 256 if width % 256 == 0 else 128
    steps = width // tile
    slots, heights = grad_slots(model)
    size = model // 8
    return pl.pallas_call(
        functools.partial(ffn_kernel, len(weights), slots, steps),
        grid=(steps,),
        in_specs=[single_spec(a.shape) for a in (x, x_t, cot, cot_t)]
        + [pl.BlockSpec((3, w.shape[1], tile), lambda j: (0, 0, j)) for w in weights],
        out_specs=[single_spec((rows, model))] * 2
        + [pl.BlockSpec((3, n * size, tile), lambda j: (0, 0, j)) for n in heights],
        out_shape=[jax.ShapeDtypeStruct((rows, model), bf16)] * 2
        + [jax.ShapeDtypeStruct((3, n * size, width), bf16) for n in heights],
        scratch_shapes=[pltpu.VMEM((model, tile), bf16)] * 3
        + [pltpu.VMEM((rows, tile), bf16)] * 3
        + [pltpu.VMEM((rows, model), f32)] * 2,
        compiler_params=pltpu.CompilerParams(vmem_limit_bytes=58 * 2**20),
        cost_estimate=pl.CostEstimate(
            flops=18 * rows * model * width,
            bytes_accessed=6 * rows * model * 2 + 12 * model * width,
            transcendentals=rows * width,
        ),
        name="ffn",
    )(x, x_t, cot, cot_t, *weights)


def lanes_first():
    return lax.broadcasted_iota(jnp.int32, (1, 128), 1) < 64


def head_mean(square_terms):
    first = lanes_first()
    low = jnp.sum(jnp.where(first, square_terms, 0.0), axis=-1, keepdims=True)
    high = jnp.sum(jnp.where(first, 0.0, square_terms), axis=-1, keepdims=True)
    return jnp.where(first, low, high) * (1.0 / 64)


def partner(u):
    low = (lax.broadcasted_iota(jnp.int32, (1, 128), 1) & 63) < 32
    return jnp.where(low, -pltpu.roll(u, 96, 1), pltpu.roll(u, 32, 1))


def project(x_ref, weights, w_scr, qkv):
    fill(w_scr, weights, lambda ref: ref[0])
    members, quarters, size, model = x_ref.shape
    span = members * size
    for i in range(quarters):
        qkv[i * span : (i + 1) * span, :] = dot(x_ref[:, i].reshape(span, model), w_scr[...])


def heads_of(u, gain, cosines, sines):
    inv = lax.rsqrt(head_mean(u * u) + epsilon)
    hat = u * inv
    turned = hat * gain
    return inv, hat, turned * cosines + partner(turned) * sines


def stack_heads(block):
    return jnp.concatenate([block[:, :64], block[:, 64:]], axis=0)


def unstack_heads(turned):
    half = turned.shape[1] // 2
    return jnp.concatenate([turned[:, :half], turned[:, half:]], axis=0).T


BLOCK = 256


def probs_of(q2, keys, block):
    parts = []
    for at in range(block + 1):
        parts.append(dot(keys[at * BLOCK : (at + 1) * BLOCK, :], q2, NT))
    key_at = lax.broadcasted_iota(jnp.int32, parts[-1].shape, 0)
    query_at = lax.broadcasted_iota(jnp.int32, parts[-1].shape, 1) & (BLOCK - 1)
    parts[-1] = jnp.where(key_at <= query_at, parts[-1], -1e30)
    top = functools.reduce(jnp.maximum, [jnp.max(p, axis=0, keepdims=True) for p in parts])
    parts = [jnp.exp(p - top) for p in parts]
    total = functools.reduce(jnp.add, [jnp.sum(p, axis=0, keepdims=True) for p in parts])
    inv = 1.0 / total
    return [p * inv for p in parts]


def natural_store(ref, block, value):
    members, quarters, size, _ = ref.shape
    span = members * size
    for at in range(0, BLOCK, size):
        row = block * BLOCK + at
        ref[(row % span) // size, row // span] = value[at : at + size]


def natural_load(ref, block):
    members, quarters, size, _ = ref.shape
    span = members * size
    parts = []
    for at in range(0, BLOCK, size):
        row = block * BLOCK + at
        parts.append(ref[(row % span) // size, row // span])
    return jnp.concatenate(parts, axis=0)


def attention_kernel(blocks, x_ref, cos_ref, sin_ref, qg_ref, kg_ref, *rest):
    weights, rest = rest[:blocks], rest[blocks:]
    mixed_ref, w_scr, qkv, q_scr, k_scr, vt_scr = rest
    project(x_ref, weights, w_scr, qkv)
    cosines, sines = cos_ref[...], sin_ref[...]
    _, _, q = heads_of(qkv[:, :128], qg_ref[...], cosines, sines)
    q_scr[...] = q.astype(bf16) * jnp.asarray(0.125, bf16)
    _, _, k = heads_of(qkv[:, 128:], kg_ref[...], cosines, sines)
    k_scr[...] = k[:, :64].astype(bf16)
    vt_scr[...] = qkv[:, 192:].astype(bf16).T
    for block in range(q_scr.shape[0] // BLOCK):
        at = slice(block * BLOCK, (block + 1) * BLOCK)
        q2 = stack_heads(q_scr[at, :])
        probs = probs_of(q2, k_scr, block)
        total = None
        for i, p in enumerate(probs):
            term = dot(vt_scr[:, i * BLOCK : (i + 1) * BLOCK], p.astype(bf16))
            total = term if total is None else total + term
        natural_store(mixed_ref, block, unstack_heads(total).astype(bf16))


def attention_back_kernel(blocks, slots, steps, x_ref, xt_ref, cos_ref, sin_ref, qg_ref, kg_ref, dm_ref, *rest):
    weights, rest = rest[:blocks], rest[blocks:]
    outs = max(o for o, _ in slots) + 1
    din_ref, gains_ref = rest[:2]
    grads = rest[2 : 2 + outs]
    w_scr, qkv, q_scr, k_scr, v_scr, kt_scr, dq_scr, dkv_scr, dqkv, din_acc = rest[2 + outs :]
    step = pl.program_id(0)
    project(x_ref, weights, w_scr, qkv)
    cosines, sines = cos_ref[...], sin_ref[...]
    q_gain, k_gain = qg_ref[...], kg_ref[...]
    q_inv, q_hat, q = heads_of(qkv[:, :128], q_gain, cosines, sines)
    q_scr[...] = q.astype(bf16) * jnp.asarray(0.125, bf16)
    k_inv, k_hat, k = heads_of(qkv[:, 128:], k_gain, cosines, sines)
    k_scr[...] = k[:, :64].astype(bf16)
    kt_scr[...] = k[:, :64].astype(bf16).T
    v_scr[...] = qkv[:, 192:].astype(bf16)
    dkv_scr[...] = jnp.zeros_like(dkv_scr)
    for block in range(q_scr.shape[0] // BLOCK):
        at = slice(block * BLOCK, (block + 1) * BLOCK)
        q2 = stack_heads(q_scr[at, :])
        do2 = stack_heads(natural_load(dm_ref, block))
        probs = probs_of(q2, k_scr, block)
        backs = [
            dot(v_scr[i * BLOCK : (i + 1) * BLOCK, :], do2, NT) for i in range(block + 1)
        ]
        delta = functools.reduce(
            jnp.add, [jnp.sum(p * b, axis=0, keepdims=True) for p, b in zip(probs, backs)]
        )
        total = None
        for i, (p, b) in enumerate(zip(probs, backs)):
            ds = (p * (b - delta)).astype(bf16)
            keys = slice(i * BLOCK, (i + 1) * BLOCK)
            term = dot(kt_scr[:, keys], ds)
            total = term if total is None else total + term
            dkv_scr[keys, :] += jnp.concatenate([dot(ds, q2), dot(p.astype(bf16), do2)], axis=1)
        dq_scr[at, :] = unstack_heads(total) * 0.125
    first = lanes_first()
    dq = dq_scr[...].astype(bf16).astype(f32)
    dkv = dkv_scr[...].astype(bf16).astype(f32)
    dq = dq * cosines - partner(dq) * sines
    dk = dkv * cosines - partner(dkv) * sines
    q_part = jnp.sum(dq * q_hat, axis=0, keepdims=True)
    k_part = jnp.sum(jnp.where(first, dk * k_hat, 0.0), axis=0, keepdims=True)
    both = jnp.concatenate([q_part, k_part], axis=0)

    @pl.when(step == 0)
    def _():
        gains_ref[...] = both
        din_acc[...] = jnp.zeros_like(din_acc)

    @pl.when(step > 0)
    def _():
        gains_ref[...] += both

    scaled = dq * q_gain
    d_q = q_inv * (scaled - q_hat * head_mean(scaled * q_hat))
    scaled = dk * k_gain
    d_k = k_inv * (scaled - k_hat * head_mean(scaled * k_hat))
    d_kv = jnp.where(first, d_k, dkv)
    dall = jnp.concatenate([d_q, d_kv], axis=1).astype(bf16)
    for block in range(q_scr.shape[0] // BLOCK):
        natural_store(dqkv, block, dall[block * BLOCK : (block + 1) * BLOCK])
    rows = din_acc.shape[0]
    grad = dqkv[...].reshape(rows, 256)
    din_acc[...] += dot(grad, w_scr[...], NT)
    size = xt_ref.shape[0] // 8
    for block in range(4):
        term = dot(xt_ref[2 * block * size : 2 * (block + 1) * size, :], grad).astype(bf16)
        for part in range(2):
            which, row = slots[2 * block + part]
            grads[which][0, row * size : (row + 1) * size, :] = term[part * size : (part + 1) * size]

    @pl.when(step == steps - 1)
    def _():
        din_ref[...] = din_acc[...].astype(bf16)


def attention_cost(length, heads, model, products):
    return pl.CostEstimate(
        flops=heads * (products * 2 * length * length * 64 + 2 * length * model * 256),
        bytes_accessed=4 * length * model * 2,
        transcendentals=heads * 2 * length * length,
    )


def weight_specs(weights):
    return [pl.BlockSpec((1, w.shape[1], 256), lambda j: (j, 0, 0)) for w in weights]


def attention_call(x, cosines, sines, q_gain, k_gain, weights):
    members, quarters, size, model = x.shape
    length = members * quarters * size
    heads = weights[0].shape[0]
    return pl.pallas_call(
        functools.partial(attention_kernel, len(weights)),
        grid=(heads,),
        in_specs=[single_spec(a.shape) for a in (x, cosines, sines, q_gain, k_gain)]
        + weight_specs(weights),
        out_specs=pl.BlockSpec((members, quarters, size, 128), lambda j: (0, 0, 0, j)),
        out_shape=jax.ShapeDtypeStruct((members, quarters, size, heads * 128), bf16),
        scratch_shapes=[
            pltpu.VMEM((model, 256), bf16),
            pltpu.VMEM((length, 256), f32),
            pltpu.VMEM((length, 128), bf16),
            pltpu.VMEM((length, 64), bf16),
            pltpu.VMEM((64, length), bf16),
        ],
        compiler_params=pltpu.CompilerParams(vmem_limit_bytes=48 * 2**20),
        cost_estimate=attention_cost(length, heads, model, 4),
        name="attention",
    )(x, cosines, sines, q_gain, k_gain, *weights)


def attention_back_call(x, x_t, cosines, sines, q_gain, k_gain, d_mixed, weights):
    members, quarters, size, model = x.shape
    length = members * quarters * size
    heads = weights[0].shape[0]
    slots, heights = grad_slots(model)
    eighth = model // 8
    return pl.pallas_call(
        functools.partial(attention_back_kernel, len(weights), slots, heads),
        grid=(heads,),
        in_specs=[single_spec(a.shape) for a in (x, x_t, cosines, sines, q_gain, k_gain)]
        + [pl.BlockSpec((members, quarters, size, 128), lambda j: (0, 0, 0, j))]
        + weight_specs(weights),
        out_specs=[single_spec((length, model)), whole_spec((2, 128))]
        + [pl.BlockSpec((1, n * eighth, 256), lambda j: (j, 0, 0)) for n in heights],
        out_shape=[
            jax.ShapeDtypeStruct((length, model), bf16),
            jax.ShapeDtypeStruct((2, 128), f32),
        ]
        + [jax.ShapeDtypeStruct((heads, n * eighth, 256), bf16) for n in heights],
        scratch_shapes=[
            pltpu.VMEM((model, 256), bf16),
            pltpu.VMEM((length, 256), f32),
            pltpu.VMEM((length, 128), bf16),
            pltpu.VMEM((length, 64), bf16),
            pltpu.VMEM((length, 64), bf16),
            pltpu.VMEM((64, length), bf16),
            pltpu.VMEM((length, 128), f32),
            pltpu.VMEM((length, 128), f32),
            pltpu.VMEM((members, quarters, size, 256), bf16),
            pltpu.VMEM((length, model), f32),
        ],
        compiler_params=pltpu.CompilerParams(vmem_limit_bytes=58 * 2**20),
        cost_estimate=attention_cost(length, heads, model, 10),
        name="attention_back",
    )(x, x_t, cosines, sines, q_gain, k_gain, d_mixed, *weights)


def split_rows(full):
    slots, heights = grad_slots(full.shape[1])
    if len(heights) == 1:
        return [full]
    size = full.shape[1] // 8
    outs = [[None] * n for n in heights]
    for i, (which, row) in enumerate(slots):
        outs[which][row] = full[:, i * size : (i + 1) * size]
    return [jnp.concatenate(o, axis=1) for o in outs]


def local(
    tokens,
    positions,
    cotangent,
    q_weight,
    key_matrix,
    value_matrix,
    out_weight,
    gate_weight,
    up_weight,
    down_weight,
    attn_gain,
    ffn_gain,
    q_gain,
    k_gain,
):
    model = tokens.shape[2]
    rows_here = q_weight.shape[0]
    members = 2 * lax.axis_size("s")
    sub = lax.axis_index("s")
    at_z = lax.axis_index("z")
    q_cols, kv_cols, ff_width = q_weight.shape[1], key_matrix.shape[1], gate_weight.shape[1]
    kv_heads = kv_cols // 64
    heads_here = kv_heads // members

    per_head = jnp.concatenate(
        [
            q_weight.reshape(rows_here, kv_heads, 128),
            key_matrix.reshape(rows_here, kv_heads, 64),
            value_matrix.reshape(rows_here, kv_heads, 64),
        ],
        axis=2,
    ).transpose(1, 0, 2)

    def pair_of(array, axis):
        if members == 2:
            size = array.shape[axis] // 2
            return [lax.slice_in_dim(array, i * size, (i + 1) * size, axis=axis) for i in range(2)]
        size = array.shape[axis] // members
        return [
            lax.dynamic_slice_in_dim(array, (2 * sub + i) * size, size, axis=axis) for i in range(2)
        ]

    qkv_blocks = gather_rows(pair_of(per_head, 0))
    out_blocks = gather_rows(pair_of(out_weight[None], 2))
    chunks = 3
    trio = [pair_of(w, 1) for w in (gate_weight, up_weight, down_weight)]
    chunk_width = trio[0][0].shape[1] // chunks
    ffn_blocks = []
    for k in range(chunks):
        cols = slice(k * chunk_width, (k + 1) * chunk_width)
        ffn_blocks.append(
            gather_rows([jnp.stack([w[i][:, cols] for w in trio], axis=0) for i in range(2)])
        )

    tok = to_sequence(relative(tokens))
    quarters, size, _ = tok.shape
    own = quarters * size
    length = own * members
    tok = tok.reshape(own, model).astype(f32)
    attn_gain_r = relative(attn_gain)
    ffn_gain_r = relative(ffn_gain)
    in_scale = rms_scale(tok)
    in_hat = tok * in_scale
    x = group_gather((in_hat * attn_gain_r).astype(bf16))
    x4 = x.reshape(members, quarters, size, model)

    cot = to_sequence(relative(cotangent)).reshape(own, model)
    cot_full = group_gather(cot).reshape(length, model)
    cot_t = cot_full.T

    every_pos = lax.all_gather(positions, ("z", "s", "c"), axis=0)
    every_pos = every_pos.reshape(quarters, members // 2, 4, 2 * size)
    pos = lax.dynamic_index_in_dim(every_pos, at_z, axis=2, keepdims=False).reshape(length)
    inverse = rope_base ** (-(2.0 * jnp.arange(32, dtype=f32)) / 64)
    turned = pos.astype(f32)[:, None] * inverse[None, :]
    cosines = jnp.tile(jnp.cos(turned), (1, 4))
    sines = jnp.tile(jnp.sin(turned), (1, 4))
    q_gain2 = jnp.tile(q_gain, 2)[None]
    k_gain2 = jnp.tile(k_gain, 2)[None]

    mixed = attention_call(x4, cosines, sines, q_gain2, k_gain2, qkv_blocks)
    mixed = mixed.reshape(length, heads_here * 128)
    out_w = jnp.concatenate([b[0] for b in out_blocks], axis=0)
    partial = dot(mixed, out_w, NT).astype(bf16).reshape(members, own, model)
    residual = tok + group_scatter([partial])
    mid_scale = rms_scale(residual)
    mid_hat = residual * mid_scale
    mid = group_gather((mid_hat * ffn_gain_r).astype(bf16)).reshape(length, model)
    mid_t = mid.T

    out_parts, mid_parts, ffn_sums = [], [], []
    for k in range(chunks):
        out_part, mid_part, *grads = ffn_call(mid, mid_t, cot_full, cot_t, ffn_blocks[k])
        out_parts.append(out_part.reshape(members, own, model))
        mid_parts.append(mid_part.reshape(members, own, model))
        ffn_sums.append(reduce_rows(grads))

    d_mid = group_scatter(mid_parts)
    ffn_gain_part = jnp.sum(d_mid * mid_hat, axis=0)
    d_resid = cot.astype(f32) + norm_back(d_mid, mid_hat, mid_scale, ffn_gain_r)
    d_attn = group_gather(d_resid.astype(bf16)).reshape(length, model)
    d_mixed = dot(d_attn, out_w).astype(bf16)
    d_mixed = d_mixed.reshape(members, quarters, size, heads_here * 128)
    out_term = lax.dot_general(
        d_attn, mixed, (((0,), (0,)), ((), ())), preferred_element_type=f32
    ).astype(bf16)
    out_sum = reduce_rows(split_rows(out_term[None]))

    x_t = x.reshape(length, model).T
    d_in_part, head_gains, *grads = attention_back_call(
        x4, x_t, cosines, sines, q_gain2, k_gain2, d_mixed, qkv_blocks
    )
    qkv_sum = reduce_rows(grads)
    d_in = group_scatter([d_in_part.reshape(members, own, model)])
    attn_gain_part = jnp.sum(d_in * in_hat, axis=0)
    input_grad = d_resid + norm_back(d_in, in_hat, in_scale, attn_gain_r)
    input_grad = relative(input_grad.astype(bf16).reshape(quarters, size, model))
    input_grad = from_sequence(input_grad)

    output = (residual + group_scatter(out_parts)).astype(bf16)
    output = from_sequence(relative(output.reshape(quarters, size, model)))

    gain_terms = jnp.concatenate(
        [
            relative(attn_gain_part),
            relative(ffn_gain_part),
            head_gains[0, :64] + head_gains[0, 64:],
            head_gains[1, :64],
        ]
    )
    gain_sums = lax.psum(gain_terms, EVERY)

    heads = jnp.concatenate(qkv_sum, axis=0).transpose(1, 0, 2).astype(f32)
    ffn_grads = [
        jnp.concatenate(
            [ffn_sums[k][i][w] for i in range(members) for k in range(chunks)], axis=1
        ).astype(f32)
        for w in range(3)
    ]
    return (
        output,
        input_grad,
        heads[:, :, :128].reshape(rows_here, q_cols),
        heads[:, :, 128:192].reshape(rows_here, kv_cols),
        heads[:, :, 192:].reshape(rows_here, kv_cols),
        jnp.concatenate([o[0] for o in out_sum], axis=1).astype(f32),
        ffn_grads[0],
        ffn_grads[1],
        ffn_grads[2],
        gain_sums[:model],
        gain_sums[model : 2 * model],
        gain_sums[2 * model : 2 * model + 64],
        gain_sums[2 * model + 64 :],
    )


def solution(mesh):
    dp, seq = mesh.devices.shape
    lines = 4
    fine = Mesh(mesh.devices.reshape(dp // 4, 2, 2, lines, seq // lines), EVERY)
    rows, cols = ("o", "x", "c"), ("z", "s")
    tokens = P(rows, cols, None)
    weight = P(rows, None)
    return jax.shard_map(
        local,
        mesh=fine,
        in_specs=(tokens, P(rows, cols), tokens) + (weight,) * 7 + (P(),) * 4,
        out_specs=(tokens, tokens) + (weight,) * 7 + (P(),) * 4,
        check_vma=False,
    )
```

time: 1250 us -> 811 us (0.65)
  waiting for transfers between devices: 809 us -> 256 us
  matrix products: 206 us -> 7.98 us
  Pallas kernels: 0 us -> 135 us
  starting transfers between devices: 28.2 us -> 155 us
  other arithmetic: 45.4 us -> 133 us
  blocking collectives: 73.6 us -> 56.6 us
    reduce_scatter x1 -> x0, waiting for transfers between devices: 613 us -> none  [reduce_rows(): lax.psum_scatter(term_fn(jnp.int32(0), lax.axis_size(('dp', 'seq')) * kee...]
    ppermute x0 -> x92, waiting for transfers between devices: none -> 249 us  [the longest x5 70.2 us: gather_rows(): by_x = lax.ppermute(own, 'x', SWAP)]
    dot_general x33 -> x3, matrix products: 206 us -> 7.98 us  [the longest x2 6.7 us: dot(): return lax.dot_general(left, right, dims, preferred_element_type=f32)]
    ppermute x0 -> x92, starting transfers between devices: none -> 138 us  [the longest x10 69.2 us: line_sum(): total = part + lax.ppermute(part, 'z', ((0, 1), (3, 2))).astype(f32)]
    pallas_call x0 -> x5, Pallas kernels: none -> 135 us  [the longest x3 80.2 us: ffn_call(): pl.pallas_call(functools.partial(ffn_kernel, len(weights), slots, steps),...]
    all_gather x8 -> x0, waiting for transfers between devices: 132 us -> none  [the longest x1 49.7 us: local(): lax.all_gather(down_weight, 'dp', axis=0, tiled=True)]
    convert_element_type x8 -> x51, other arithmetic: 8.1 us -> 67.4 us  [the longest x10 13.6 us: line_sum(): total = total.astype(bf16)]
    all_to_all x6 -> x4, waiting for transfers between devices: 60.4 us -> 6.97 us  [the longest x2 6.97 us: to_sequence(): return lax.all_to_all(every, 'z', 0, 0, tiled=True)]
  transfers between devices with their start and end apart: 15 -> 96, of which waited for: 10 -> 26; matrix products, arithmetic and copies ran while one was open for 15% -> 23% of each run, Pallas kernels for 0% -> 13%
where the time goes in v1:
time: 811 us; the launch traced here: 803 us
  waiting for transfers between devices  256 us (32%)
  starting transfers between devices  155 us (19%)
  Pallas kernels  135 us (17%)
  other arithmetic  133 us (16%)
  local copies, waits for them, and re-layouts  56.8 us (7%)
  blocking collectives  56.6 us (7%)
    pallas_call x3, Pallas kernels, ffn_call(): pl.pallas_call(functools.partial(ffn_kernel, len(weights), slots, steps),...  80.2 us
    ppermute x5, waiting for transfers between devices, gather_rows(): by_x = lax.ppermute(own, 'x', SWAP)  70.2 us
    ppermute x10, starting transfers between devices, line_sum(): total = part + lax.ppermute(part, 'z', ((0, 1), (3, 2))).astype(f32)  69.2 us
    ppermute x10, waiting for transfers between devices, line_sum(): back = lax.ppermute(total, 'z', ((1, 0), (2, 3)))  62.4 us
    ppermute x5, waiting for transfers between devices, reduce_rows(): come_a = lax.ppermute(send_a, 'x', SWAP)  52.7 us
    psum x1, blocking collectives, local(): gain_sums = lax.psum(gain_terms, EVERY)  42.4 us
    pallas_call x1, Pallas kernels, attention_back_call(): pl.pallas_call(functools.partial(attention_back_kernel, len(weights), slo...  36.7 us
    ppermute x5, waiting for transfers between devices, reduce_rows(): last_a = lax.ppermute(add(keep_a, come_a, 1).astype(bf16), 'o', SWAP)  26.3 us
  transfers between devices with their start and end apart: 96, of which 26 were waited for; matrix products, arithmetic and copies ran while one was open for 23% of the time, Pallas kernels for 13%

profile of v1, /device:TPU:0, one launch (start us, length us, event | category | flops | bytes accessed | tf_op | source)
XLA Modules:
  0.0 802.5 jit_solution(14280856055853653180)
XLA Ops:
  14.9 14.2 %all-gather.1 = s32[8,2,256]{2,1,0:T(2,128)S(1)} all-gather(s32[1,2,256]{2,1,0:T(2,128)S(1)} %bitcast.251), channel_id=2, replica_groups=mesh['o'=2,'x'=2,'c'=2,'z'=4,'s'=1] {'z','s','c'}, dimensions={0}, use_global_device_ids=true | all-gather | bytes 18432 | tf_op jit(solution)/shard_map/all_gather | solution.py:595
  57.9 7.0 all-to-all-done
  68.9 4.5 all-to-all-start.1
  84.6 8.0 %collective-permute-done.3.rest_1_ = bf16[4,256,256]{2,1,0:T(8,128)(2,1)S(1)} collective-permute-done((bf16[4,256,256]{2,1,0:T(8,128)(2,1)S(1)}, bf16[4,256,256]{2,1,0:T(8,128)(2,1)S(1)}, u32[]{:S(2)}, u32[]{:S(2)}) %collective-permute-start.3) | collective-permute-done | bytes 524320 | tf_op jit(solution)/shard_map/ppermute | solution.py:109
  99.7 17.4 %collective-permute-done.5.rest_3_ = bf16[4,128,256]{2,1,0:T(8,128)(2,1)S(1)} collective-permute-done((bf16[4,128,256]{2,1,0:T(8,128)(2,1)S(1)}, bf16[4,128,256]{2,1,0:T(8,128)(2,1)S(1)}, u32[]{:S(2)}, u32[]{:S(2)}) %collective-permute-start.5) | collective-permute-done | bytes 262176 | tf_op jit(solution)/shard_map/ppermute | solution.py:111
  117.1 17.8 %attention.1 = bf16[2,4,128,512]{3,2,1,0:T(8,128)(2,1)S(1)} custom-call(bf16[2,4,128,1024]{3,2,1,0:T(8,128)(2,1)} %pad_maximum_fusion.x_ref, f32[1024,128]{1,0:T(8,128)S(1)} %copy.55.cos_ref, f32[1024,128]{1,0:T(8,128)S(1)} %copy.56.sin_ref, f32[1,128]{1,0:T(1,128)S(1)} %broadcast_in_dim_tile.6.qg_ref, f32[1,128]{1,0:T(1,128)S(1)} %broadcast_in_dim_tile.7.kg_ref, ...), custom_call_target="tpu_custom_call" | custom-call | flops 4294967296 | bytes 8388608 | tf_op jit(solution)/shard_map/attention/pallas_call | solution.py:456
  146.7 20.8 %collective-permute-done.17.rest_1_ = bf16[3,256,768]{2,1,0:T(8,128)(2,1)} collective-permute-done((bf16[3,256,768]{2,1,0:T(8,128)(2,1)S(1)}, bf16[3,256,768]{2,1,0:T(8,128)(2,1)}, u32[]{:S(2)}, u32[]{:S(2)}) %collective-permute-start.17) | collective-permute-done | bytes 1179680 | tf_op jit(solution)/shard_map/ppermute | solution.py:109
  174.4 18.4 %collective-permute-done.22.rest_1_ = bf16[3,256,768]{2,1,0:T(8,128)(2,1)} collective-permute-done((bf16[3,256,768]{2,1,0:T(8,128)(2,1)}, bf16[3,256,768]{2,1,0:T(8,128)(2,1)}, u32[]{:S(2)}, u32[]{:S(2)}) %collective-permute-start.22) | collective-permute-done | bytes 1179680 | tf_op jit(solution)/shard_map/ppermute | solution.py:109
  198.7 19.4 %collective-permute-done.27.rest_1_ = bf16[3,256,768]{2,1,0:T(8,128)(2,1)} collective-permute-done((bf16[3,256,768]{2,1,0:T(8,128)(2,1)S(1)}, bf16[3,256,768]{2,1,0:T(8,128)(2,1)}, u32[]{:S(2)}, u32[]{:S(2)}) %collective-permute-start.27) | collective-permute-done | bytes 1179680 | tf_op jit(solution)/shard_map/ppermute | solution.py:109
  237.7 5.6 collective-permute-done.30.rest_4_
  244.9 26.8 %ffn.5 = (bf16[1024,1024]{1,0:T(8,128)(2,1)}, bf16[1024,1024]{1,0:T(8,128)(2,1)}, bf16[3,256,768]{2,1,0:T(8,128)(2,1)}, bf16[3,256,768]{2,1,0:T(8,128)(2,1)}, bf...) custom-call(bf16[1024,1024]{1,0:T(8,128)(2,1)} %bitcast.225, bf16[1024,1024]{1,0:T(8,128)(2,1)} %bitcast.237, ...), custom_call_target="tpu_custom_call" | custom-call | flops 14495514624 | bytes 22020096 | tf_op jit(solution)/shard_map/ffn/pallas_call | solution.py:245
  272.6 26.6 %ffn.4 = (bf16[1024,1024]{1,0:T(8,128)(2,1)}, bf16[1024,1024]{1,0:T(8,128)(2,1)}, bf16[3,256,768]{2,1,0:T(8,128)(2,1)}, bf16[3,256,768]{2,1,0:T(8,128)(2,1)}, bf...) custom-call(bf16[1024,1024]{1,0:T(8,128)(2,1)} %bitcast.226, bf16[1024,1024]{1,0:T(8,128)(2,1)} %bitcast.238, ...), custom_call_target="tpu_custom_call" | custom-call | flops 14495514624 | bytes 22020096 | tf_op jit(solution)/shard_map/ffn/pallas_call | solution.py:245
  299.2 26.8 %ffn.3 = (bf16[1024,1024]{1,0:T(8,128)(2,1)}, bf16[1024,1024]{1,0:T(8,128)(2,1)}, bf16[3,256,768]{2,1,0:T(8,128)(2,1)}, bf16[3,256,768]{2,1,0:T(8,128)(2,1)}, bf...) custom-call(bf16[1024,1024]{1,0:T(8,128)(2,1)} %bitcast.227, bf16[1024,1024]{1,0:T(8,128)(2,1)} %bitcast.239, ...), custom_call_target="tpu_custom_call" | custom-call | flops 14495514624 | bytes 22020096 | tf_op jit(solution)/shard_map/ffn/pallas_call | solution.py:245
  326.0 4.8 add_convert_fusion
  349.4 4.6 fusion.32
  355.8 4.8 all-to-all-start.2
  360.6 9.0 %collective-permute-done.81 = bf16[3,256,768]{2,1,0:T(8,128)(2,1)} collective-permute-done((bf16[3,256,768]{2,1,0:T(8,128)(2,1)}, bf16[3,256,768]{2,1,0:T(8,128)(2,1)}, u32[]{:S(2)}, u32[]{:S(2)}) %collective-permute-start.81) | collective-permute-done | bytes 1179680 | tf_op jit(solution)/shard_map/ppermute | solution.py:138
  372.9 22.0 %collective-permute-done.70 = bf16[3,256,768]{2,1,0:T(8,128)(2,1)} collective-permute-done((bf16[3,256,768]{2,1,0:T(8,128)(2,1)}, bf16[3,256,768]{2,1,0:T(8,128)(2,1)}, u32[]{:S(2)}, u32[]{:S(2)}) %collective-permute-start.70) | collective-permute-done | bytes 1179680 | tf_op jit(solution)/shard_map/ppermute | solution.py:138
  398.4 21.7 %collective-permute-done.59 = bf16[3,256,768]{2,1,0:T(8,128)(2,1)} collective-permute-done((bf16[3,256,768]{2,1,0:T(8,128)(2,1)}, bf16[3,256,768]{2,1,0:T(8,128)(2,1)}, u32[]{:S(2)}, u32[]{:S(2)}) %collective-permute-start.59) | collective-permute-done | bytes 1179680 | tf_op jit(solution)/shard_map/ppermute | solution.py:138
  422.6 10.6 %collective-permute-done.82 = bf16[3,128,768]{2,1,0:T(8,128)(2,1)S(1)} collective-permute-done((bf16[3,128,768]{2,1,0:T(8,128)(2,1)S(1)}, bf16[3,128,768]{2,1,0:T(8,128)(2,1)S(1)}, u32[]{:S(2)}, u32[]{:S(2)}) %collective-permute-start.82) | collective-permute-done | bytes 589856 | tf_op jit(solution)/shard_map/ppermute | solution.py:145
  437.9 8.0 collective-permute-done.71
  445.9 4.4 collective-permute-start.83
  457.3 4.4 collective-permute-start.72
  474.2 36.7 %attention_back.1 = (bf16[1024,1024]{1,0:T(8,128)(2,1)}, f32[2,128]{1,0:T(2,128)}, bf16[4,256,256]{2,1,0:T(8,128)(2,1)}, bf16[4,256,256]{2,1,0:T(8,128)(2,1)}, b...) custom-call(bf16[2,4,128,1024]{3,2,1,0:T(8,128)(2,1)} %pad_maximum_fusion.x_ref, bf16[1024,1024]{1,0:T(8,128)(2,1)} %bitcast.233, ...), custom_call_target="tpu_custom_call" | custom-call | flops 7516192768 | bytes 8388608 | tf_op jit(solution)/shard_map/attention_back/pallas_call | solution.py:482
  531.8 6.9 collective-permute-done.54
  551.0 6.2 collective-permute-start.50
  563.0 4.5 collective-permute-done.38
  583.1 43.0 %collective-permute-start.39 = (bf16[4,128,256]{2,1,0:T(8,128)(2,1)}, bf16[4,128,256]{2,1,0:T(8,128)(2,1)}, u32[]{:S(2)}, u32[]{:S(2)}) collective-permute-start(bf16[4,128,256]{2,1,0:T(8,128)(2,1)} %add_convert_fusion.33), channel_id=1, source_target_pairs={{0,1},{3,2},{4,5},{7,6},{8,9},{11,10},{12,13},{15,14},{16,17},{19,... | collective-permute-start | bytes 786440 | tf_op jit(solution)/shard_map/ppermute | solution.py:127
  639.1 42.4 %psum.7 = f32[2176]{0:T(1024)S(1)} all-reduce(f32[2176]{0:T(1024)S(1)} %concatenate.125), channel_id=1, replica_groups=mesh['o'=2,'x'=2,'c'=2,'z'=4,'s'=1] {'o','x','c','z','s'}, use_global_device_ids=true, to_apply=%region_6.7 | all-reduce | flops 2176 | bytes 17408 | tf_op jit(solution)/shard_map/psum | solution.py:655
  703.3 14.7 %collective-permute-done.74 = bf16[3,128,768]{2,1,0:T(8,128)(2,1)S(1)} collective-permute-done((bf16[3,128,768]{2,1,0:T(8,128)(2,1)S(1)}, bf16[3,128,768]{2,1,0:T(8,128)(2,1)S(1)}, u32[]{:S(2)}, u32[]{:S(2)}) %collective-permute-start.74) | collective-permute-done | bytes 589856 | tf_op jit(solution)/shard_map/ppermute | solution.py:130
  719.6 15.1 %collective-permute-done.79 = bf16[3,128,768]{2,1,0:T(8,128)(2,1)S(1)} collective-permute-done((bf16[3,128,768]{2,1,0:T(8,128)(2,1)S(1)}, bf16[3,128,768]{2,1,0:T(8,128)(2,1)S(1)}, u32[]{:S(2)}, u32[]{:S(2)}) %collective-permute-start.79) | collective-permute-done | bytes 589856 | tf_op jit(solution)/shard_map/ppermute | solution.py:130
  735.9 29.7 %collective-permute-done.41 = bf16[4,128,256]{2,1,0:T(8,128)(2,1)S(1)} collective-permute-done((bf16[4,128,256]{2,1,0:T(8,128)(2,1)S(1)}, bf16[4,128,256]{2,1,0:T(8,128)(2,1)S(1)}, u32[]{:S(2)}, u32[]{:S(2)}) %collective-permute-start.41) | collective-permute-done | bytes 262176 | tf_op jit(solution)/shard_map/ppermute | solution.py:130
  (570 shorter events, 292.5 us)
Async XLA Ops:
  11.2 55.2 %collective-permute-start.14 = (bf16[2,128,1024]{2,1,0:T(8,128)(2,1)}, bf16[2,128,1024]{2,1,0:T(8,128)(2,1)}, u32[]{:S(2)}, u32[]{:S(2)}) collective-permute-start(bf16[2,128,1024]{2,1,0:T(8,128)(2,1)} %broadcast_select_fusion.37), channel_id=1, source_target_pairs={{0,4},{4,0},{1,5},{5,1},{2,6},{6,2},{3,7},{7,3},{8,12},{12,8},{9,1... | collective-permute-start | bytes 1572872 | tf_op jit(solution)/shard_map/ppermute | solution.py:59
  14.6 127.4 %collective-permute-start.26 = (bf16[3,128,768]{2,1,0:T(8,128)(2,1)}, bf16[3,128,768]{2,1,0:T(8,128)(2,1)}, u32[]{:S(2)}, u32[]{:S(2)}) collective-permute-start(bf16[3,128,768]{2,1,0:T(8,128)(2,1)} %broadcast_select_fusion.25), channel_id=1, source_target_pairs={{0,4},{4,0},{1,5},{5,1},{2,6},{6,2},{3,7},{7,3},{8,12},{12,8},{9,1... | collective-permute-start | bytes 1769480 | tf_op jit(solution)/shard_map/ppermute | solution.py:59
  68.9 98.6 %all-to-all-start.1 = ((bf16[4,128,1024]{2,1,0:T(8,128)(2,1)}), bf16[4,128,1024]{2,1,0:T(8,128)(2,1)}, u32[]{:S(2)}, u32[]{:S(2)}) async-start(bf16[4,128,1024]{2,1,0:T(8,128)(2,1)} %pad_maximum_fusion.11), calls=%async_computation.1 | async-start | bytes 2097152 | tf_op jit(solution)/shard_map/all_to_all | solution.py:90
  81.3 57.9 %collective-permute-start.21 = (bf16[3,128,768]{2,1,0:T(8,128)(2,1)}, bf16[3,128,768]{2,1,0:T(8,128)(2,1)S(1)}, u32[]{:S(2)}, u32[]{:S(2)}) collective-permute-start(bf16[3,128,768]{2,1,0:T(8,128)(2,1)} %broadcast_select_fusion.29), channel_id=1, source_target_pairs={{0,4},{4,0},{1,5},{5,1},{2,6},{6,2},{3,7},{7,3},{8,12},{12,8},{9,1... | collective-permute-start | bytes 1769480 | tf_op jit(solution)/shard_map/ppermute | solution.py:59
  83.0 61.9 %collective-permute-start.18 = (bf16[3,256,768]{2,1,0:T(8,128)(2,1)S(1)}, bf16[3,256,768]{2,1,0:T(8,128)(2,1)S(1)}, u32[]{:S(2)}, u32[]{:S(2)}) collective-permute-start(bf16[3,256,768]{2,1,0:T(8,128)(2,1)S(1)} %pad_maximum_fusion.5.rest_0_), channel_id=1, source_target_pairs={{0,16},{16,0},{1,17},{17,1},{2,18},{18,2},{3,19},{19,3},{4,20},{20... | collective-permute-start | bytes 3538952 | tf_op jit(solution)/shard_map/ppermute | solution.py:110
  145.4 72.6 %collective-permute-start.27 = (bf16[3,256,768]{2,1,0:T(8,128)(2,1)S(1)}, bf16[3,256,768]{2,1,0:T(8,128)(2,1)}, u32[]{:S(2)}, u32[]{:S(2)}) collective-permute-start(bf16[3,256,768]{2,1,0:T(8,128)(2,1)S(1)} %pad_maximum_fusion.7.rest_0_), channel_id=1, source_target_pairs={{0,8},{8,0},{1,9},{9,1},{2,10},{10,2},{3,11},{11,3},{4,12},{12,4},... | collective-permute-start | bytes 3538952 | tf_op jit(solution)/shard_map/ppermute | solution.py:109
  167.5 53.0 %collective-permute-start.15 = (bf16[512,1024]{1,0:T(8,128)(2,1)}, bf16[512,1024]{1,0:T(8,128)(2,1)S(1)}, u32[]{:S(2)}, u32[]{:S(2)}) collective-permute-start(bf16[512,1024]{1,0:T(8,128)(2,1)} %bitcast.23), channel_id=1, source_target_pairs={{0,4},{4,0},{1,5},{5,1},{2,6},{6,2},{3,7},{7,3},{8,12},{12,8},{9,1... | collective-permute-start | bytes 3145736 | tf_op jit(solution)/shard_map/ppermute | solution.py:59
  169.7 59.3 %collective-permute-start.13 = (bf16[512,1024]{1,0:T(8,128)(2,1)}, bf16[512,1024]{1,0:T(8,128)(2,1)}, u32[]{:S(2)}, u32[]{:S(2)}) collective-permute-start(bf16[512,1024]{1,0:T(8,128)(2,1)} %multiply_convert_fusion), channel_id=1, source_target_pairs={{0,4},{4,0},{1,5},{5,1},{2,6},{6,2},{3,7},{7,3},{8,12},{12,8},{9,1... | collective-permute-start | bytes 3145736 | tf_op jit(solution)/shard_map/ppermute | solution.py:59
  192.8 106.4 %collective-permute-start.20 = (bf16[3,128,768]{2,1,0:T(8,128)(2,1)}, bf16[3,128,768]{2,1,0:T(8,128)(2,1)}, u32[]{:S(2)}, u32[]{:S(2)}) collective-permute-start(bf16[3,128,768]{2,1,0:T(8,128)(2,1)} %slice.719), channel_id=1, source_target_pairs={{0,8},{8,0},{1,9},{9,1},{2,10},{10,2},{3,11},{11,3},{4,12},{12,4},... | collective-permute-start | bytes 1769480 | tf_op jit(solution)/shard_map/ppermute | solution.py:112
  195.3 103.9 %collective-permute-start.19 = (bf16[3,128,768]{2,1,0:T(8,128)(2,1)}, bf16[3,128,768]{2,1,0:T(8,128)(2,1)}, u32[]{:S(2)}, u32[]{:S(2)}) collective-permute-start(bf16[3,128,768]{2,1,0:T(8,128)(2,1)} %slice.718), channel_id=1, source_target_pairs={{0,16},{16,0},{1,17},{17,1},{2,18},{18,2},{3,19},{19,3},{4,20},{20... | collective-permute-start | bytes 1769480 | tf_op jit(solution)/shard_map/ppermute | solution.py:111
  341.5 53.4 %collective-permute-start.70 = (bf16[3,256,768]{2,1,0:T(8,128)(2,1)}, bf16[3,256,768]{2,1,0:T(8,128)(2,1)}, u32[]{:S(2)}, u32[]{:S(2)}) collective-permute-start(bf16[3,256,768]{2,1,0:T(8,128)(2,1)} %get-tuple-element.53), channel_id=1, source_target_pairs={{0,8},{8,0},{1,9},{9,1},{2,10},{10,2},{3,11},{11,3},{4,12},{12,4},... | collective-permute-start | bytes 3538952 | tf_op jit(solution)/shard_map/ppermute | solution.py:138
  343.0 53.6 %collective-permute-start.75 = (bf16[3,256,768]{2,1,0:T(8,128)(2,1)}, bf16[3,256,768]{2,1,0:T(8,128)(2,1)}, u32[]{:S(2)}, u32[]{:S(2)}) collective-permute-start(bf16[3,256,768]{2,1,0:T(8,128)(2,1)} %get-tuple-element.55), channel_id=1, source_target_pairs={{0,16},{16,0},{1,17},{17,1},{2,18},{18,2},{3,19},{19,3},{4,20},{20... | collective-permute-start | bytes 3538952 | tf_op jit(solution)/shard_map/ppermute | solution.py:139
  348.8 71.3 %collective-permute-start.59 = (bf16[3,256,768]{2,1,0:T(8,128)(2,1)}, bf16[3,256,768]{2,1,0:T(8,128)(2,1)}, u32[]{:S(2)}, u32[]{:S(2)}) collective-permute-start(bf16[3,256,768]{2,1,0:T(8,128)(2,1)} %get-tuple-element.49), channel_id=1, source_target_pairs={{0,8},{8,0},{1,9},{9,1},{2,10},{10,2},{3,11},{11,3},{4,12},{12,4},... | collective-permute-start | bytes 3538952 | tf_op jit(solution)/shard_map/ppermute | solution.py:138
  355.8 202.2 %all-to-all-start.2 = ((bf16[4,128,1024]{2,1,0:T(8,128)(2,1)}), bf16[4,128,1024]{2,1,0:T(8,128)(2,1)S(1)}, u32[]{:S(2)}, u32[]{:S(2)}) async-start(bf16[4,128,1024]{2,1,0:T(8,128)(2,1)} %pad_maximum_fusion.12), calls=%async_computation.2 | async-start | bytes 2097152 | tf_op jit(solution)/shard_map/all_to_all | solution.py:95
  369.6 52.3 %collective-permute-start.64 = (bf16[3,256,768]{2,1,0:T(8,128)(2,1)}, bf16[3,256,768]{2,1,0:T(8,128)(2,1)S(1)}, u32[]{:S(2)}, u32[]{:S(2)}) collective-permute-start(bf16[3,256,768]{2,1,0:T(8,128)(2,1)} %get-tuple-element.51), channel_id=1, source_target_pairs={{0,16},{16,0},{1,17},{17,1},{2,18},{18,2},{3,19},{19,3},{4,20},{20... | collective-permute-start | bytes 3538952 | tf_op jit(solution)/shard_map/ppermute | solution.py:139
  371.5 93.9 %collective-permute-start.34 = (bf16[512,1024]{1,0:T(8,128)(2,1)}, bf16[512,1024]{1,0:T(8,128)(2,1)S(1)}, u32[]{:S(2)}, u32[]{:S(2)}) collective-permute-start(bf16[512,1024]{1,0:T(8,128)(2,1)} %get-tuple-element.112), channel_id=1, source_target_pairs={{0,4},{4,0},{1,5},{5,1},{2,6},{6,2},{3,7},{7,3},{8,12},{12,8},{9,1... | collective-permute-start | bytes 3145736 | tf_op jit(solution)/shard_map/ppermute | solution.py:59
  445.9 68.4 %collective-permute-start.83 = (bf16[3,128,768]{2,1,0:T(8,128)(2,1)S(1)}, bf16[3,128,768]{2,1,0:T(8,128)(2,1)}, u32[]{:S(2)}, u32[]{:S(2)}) collective-permute-start(bf16[3,128,768]{2,1,0:T(8,128)(2,1)S(1)} %add_convert_fusion.9), channel_id=1, source_target_pairs={{0,1},{3,2},{4,5},{7,6},{8,9},{11,10},{12,13},{15,14},{16,17},{19,... | collective-permute-start | bytes 1769480 | tf_op jit(solution)/shard_map/ppermute | solution.py:127
  452.4 65.2 %collective-permute-start.88 = (bf16[3,128,768]{2,1,0:T(8,128)(2,1)S(1)}, bf16[3,128,768]{2,1,0:T(8,128)(2,1)}, u32[]{:S(2)}, u32[]{:S(2)}) collective-permute-start(bf16[3,128,768]{2,1,0:T(8,128)(2,1)S(1)} %add_convert_fusion.5), channel_id=1, source_target_pairs={{0,1},{3,2},{4,5},{7,6},{8,9},{11,10},{12,13},{15,14},{16,17},{19,... | collective-permute-start | bytes 1769480 | tf_op jit(solution)/shard_map/ppermute | solution.py:127
  457.3 63.9 %collective-permute-start.72 = (bf16[3,128,768]{2,1,0:T(8,128)(2,1)}, bf16[3,128,768]{2,1,0:T(8,128)(2,1)}, u32[]{:S(2)}, u32[]{:S(2)}) collective-permute-start(bf16[3,128,768]{2,1,0:T(8,128)(2,1)} %add_convert_fusion.17), channel_id=1, source_target_pairs={{0,1},{3,2},{4,5},{7,6},{8,9},{11,10},{12,13},{15,14},{16,17},{19,... | collective-permute-start | bytes 1769480 | tf_op jit(solution)/shard_map/ppermute | solution.py:127
  463.0 60.9 %collective-permute-start.77 = (bf16[3,128,768]{2,1,0:T(8,128)(2,1)}, bf16[3,128,768]{2,1,0:T(8,128)(2,1)}, u32[]{:S(2)}, u32[]{:S(2)}) collective-permute-start(bf16[3,128,768]{2,1,0:T(8,128)(2,1)} %add_convert_fusion.13), channel_id=1, source_target_pairs={{0,1},{3,2},{4,5},{7,6},{8,9},{11,10},{12,13},{15,14},{16,17},{19,... | collective-permute-start | bytes 1769480 | tf_op jit(solution)/shard_map/ppermute | solution.py:127
  465.4 63.0 %collective-permute-start.61 = (bf16[3,128,768]{2,1,0:T(8,128)(2,1)S(1)}, bf16[3,128,768]{2,1,0:T(8,128)(2,1)}, u32[]{:S(2)}, u32[]{:S(2)}) collective-permute-start(bf16[3,128,768]{2,1,0:T(8,128)(2,1)S(1)} %add_convert_fusion.25), channel_id=1, source_target_pairs={{0,1},{3,2},{4,5},{7,6},{8,9},{11,10},{12,13},{15,14},{16,17},{19,... | collective-permute-start | bytes 1769480 | tf_op jit(solution)/shard_map/ppermute | solution.py:127
  531.8 99.3 %collective-permute-start.35 = (bf16[512,1024]{1,0:T(8,128)(2,1)}, bf16[512,1024]{1,0:T(8,128)(2,1)}, u32[]{:S(2)}, u32[]{:S(2)}) collective-permute-start(bf16[512,1024]{1,0:T(8,128)(2,1)} %broadcast_select_fusion), channel_id=1, source_target_pairs={{0,4},{4,0},{1,5},{5,1},{2,6},{6,2},{3,7},{7,3},{8,12},{12,8},{9,1... | collective-permute-start | bytes 3145736 | tf_op jit(solution)/shard_map/ppermute | solution.py:59
  577.4 112.5 %collective-permute-start.32 = (bf16[2,128,1024]{2,1,0:T(8,128)(2,1)}, bf16[2,128,1024]{2,1,0:T(8,128)(2,1)}, u32[]{:S(2)}, u32[]{:S(2)}) collective-permute-start(bf16[2,128,1024]{2,1,0:T(8,128)(2,1)} %broadcast_select_fusion.36), channel_id=1, source_target_pairs={{0,4},{4,0},{1,5},{5,1},{2,6},{6,2},{3,7},{7,3},{8,12},{12,8},{9,1... | collective-permute-start | bytes 1572872 | tf_op jit(solution)/shard_map/ppermute | solution.py:59
  583.1 104.2 %collective-permute-start.39 = (bf16[4,128,256]{2,1,0:T(8,128)(2,1)}, bf16[4,128,256]{2,1,0:T(8,128)(2,1)}, u32[]{:S(2)}, u32[]{:S(2)}) collective-permute-start(bf16[4,128,256]{2,1,0:T(8,128)(2,1)} %add_convert_fusion.33), channel_id=1, source_target_pairs={{0,1},{3,2},{4,5},{7,6},{8,9},{11,10},{12,13},{15,14},{16,17},{19,... | collective-permute-start | bytes 786440 | tf_op jit(solution)/shard_map/ppermute | solution.py:127
  627.0 64.1 %collective-permute-start.44 = (bf16[4,128,256]{2,1,0:T(8,128)(2,1)S(1)}, bf16[4,128,256]{2,1,0:T(8,128)(2,1)}, u32[]{:S(2)}, u32[]{:S(2)}) collective-permute-start(bf16[4,128,256]{2,1,0:T(8,128)(2,1)S(1)} %add_convert_fusion.29), channel_id=1, source_target_pairs={{0,1},{3,2},{4,5},{7,6},{8,9},{11,10},{12,13},{15,14},{16,17},{19,... | collective-permute-start | bytes 786440 | tf_op jit(solution)/shard_map/ppermute | solution.py:127
  629.0 69.3 %collective-permute-start.85 = (bf16[3,128,768]{2,1,0:T(8,128)(2,1)}, bf16[3,128,768]{2,1,0:T(8,128)(2,1)}, u32[]{:S(2)}, u32[]{:S(2)}) collective-permute-start(bf16[3,128,768]{2,1,0:T(8,128)(2,1)} %add_convert_fusion.7), channel_id=1, source_target_pairs={{1,0},{2,3},{5,4},{6,7},{9,8},{10,11},{13,12},{14,15},{17,16},{18,... | collective-permute-start | bytes 1769480 | tf_op jit(solution)/shard_map/ppermute | solution.py:130
  631.1 68.6 %collective-permute-start.90 = (bf16[3,128,768]{2,1,0:T(8,128)(2,1)}, bf16[3,128,768]{2,1,0:T(8,128)(2,1)}, u32[]{:S(2)}, u32[]{:S(2)}) collective-permute-start(bf16[3,128,768]{2,1,0:T(8,128)(2,1)} %add_convert_fusion.3), channel_id=1, source_target_pairs={{1,0},{2,3},{5,4},{6,7},{9,8},{10,11},{13,12},{14,15},{17,16},{18,... | collective-permute-start | bytes 1769480 | tf_op jit(solution)/shard_map/ppermute | solution.py:130
  683.2 106.0 %all-to-all-start.3 = ((bf16[4,128,1024]{2,1,0:T(8,128)(2,1)}), bf16[4,128,1024]{2,1,0:T(8,128)(2,1)S(1)}, u32[]{:S(2)}, u32[]{:S(2)}) async-start(bf16[4,128,1024]{2,1,0:T(8,128)(2,1)} %pad_maximum_fusion.14), calls=%async_computation.3 | async-start | bytes 2097152 | tf_op jit(solution)/shard_map/all_to_all | solution.py:95
  697.0 71.6 %collective-permute-start.63 = (bf16[3,128,768]{2,1,0:T(8,128)(2,1)S(1)}, bf16[3,128,768]{2,1,0:T(8,128)(2,1)S(1)}, u32[]{:S(2)}, u32[]{:S(2)}) collective-permute-start(bf16[3,128,768]{2,1,0:T(8,128)(2,1)S(1)} %copy-done.30), channel_id=1, source_target_pairs={{1,0},{2,3},{5,4},{6,7},{9,8},{10,11},{13,12},{14,15},{17,16},{18,... | collective-permute-start | bytes 1769480 | tf_op jit(solution)/shard_map/ppermute | solution.py:130
  698.4 70.2 %collective-permute-start.68 = (bf16[3,128,768]{2,1,0:T(8,128)(2,1)S(1)}, bf16[3,128,768]{2,1,0:T(8,128)(2,1)S(1)}, u32[]{:S(2)}, u32[]{:S(2)}) collective-permute-start(bf16[3,128,768]{2,1,0:T(8,128)(2,1)S(1)} %copy-done.31), channel_id=1, source_target_pairs={{1,0},{2,3},{5,4},{6,7},{9,8},{10,11},{13,12},{14,15},{17,16},{18,... | collective-permute-start | bytes 1769480 | tf_op jit(solution)/shard_map/ppermute | solution.py:130
  699.7 65.9 %collective-permute-start.41 = (bf16[4,128,256]{2,1,0:T(8,128)(2,1)S(1)}, bf16[4,128,256]{2,1,0:T(8,128)(2,1)S(1)}, u32[]{:S(2)}, u32[]{:S(2)}) collective-permute-start(bf16[4,128,256]{2,1,0:T(8,128)(2,1)S(1)} %add_convert_fusion.31), channel_id=1, source_target_pairs={{1,0},{2,3},{5,4},{6,7},{9,8},{10,11},{13,12},{14,15},{17,16},{18,... | collective-permute-start | bytes 786440 | tf_op jit(solution)/shard_map/ppermute | solution.py:130
  734.7 52.5 %collective-permute-start.91 = (bf16[3,128,768]{2,1,0:T(8,128)(2,1)}, bf16[3,128,768]{2,1,0:T(8,128)(2,1)}, u32[]{:S(2)}, u32[]{:S(2)}) collective-permute-start(bf16[3,128,768]{2,1,0:T(8,128)(2,1)} %get-tuple-element.91), channel_id=1, source_target_pairs={{0,4},{4,0},{1,5},{5,1},{2,6},{6,2},{3,7},{7,3},{8,12},{12,8},{9,1... | collective-permute-start | bytes 1769480 | tf_op jit(solution)/shard_map/ppermute | solution.py:59
  (174 other events, 2834.7 us)

commit v2 on v1

v2 whole, which is shorter than its diff:
```python
import functools

import jax
import jax.numpy as jnp
from jax import lax
from jax.experimental import pallas as pl
from jax.experimental.pallas import tpu as pltpu
from jax.sharding import Mesh, PartitionSpec as P

epsilon = 1e-05
rope_base = 1000000.0
f32 = jnp.float32
bf16 = jnp.bfloat16
SWAP = ((0, 1), (1, 0))
EVERY = ("o", "x", "c", "z", "s")
NT = (((1,), (1,)), ((), ()))
NN = (((1,), (0,)), ((), ()))


def dot(left, right, dims=NN):
    return lax.dot_general(left, right, dims, preferred_element_type=f32)


def rms_scale(rows):
    return lax.rsqrt(jnp.mean(rows * rows, axis=-1, keepdims=True) + epsilon)


def norm_back(grad_out, normed_hat, inv_scale, gain):
    scaled = grad_out * gain
    return inv_scale * (scaled - normed_hat * jnp.mean(scaled * normed_hat, axis=-1, keepdims=True))


def square():
    return lax.axis_size("o") == 2 and lax.axis_size("x") == 2


def pair_group():
    return lax.axis_size("s") == 1


def chip_at():
    if not square():
        return jnp.int32(0)
    return 2 * lax.axis_index("o") + lax.axis_index("x")


def flip_at():
    return lax.axis_index("c") if pair_group() else jnp.int32(0)


def relative(vector):
    if not square():
        return vector
    quarter = vector.shape[0] // 4
    blocks = [
        lax.dynamic_slice_in_dim(vector, (chip_at() ^ i) * quarter, quarter) for i in range(4)
    ]
    return jnp.concatenate(blocks)


def after(array, *others):
    return lax.optimization_barrier((array, *others))[0]


def swap_core(array):
    return lax.ppermute(array, "c", SWAP)


def group_gather(rows):
    if pair_group():
        return [rows, swap_core(rows)]
    full = lax.all_gather(rows, ("s", "c"), axis=0)
    return [full[i] for i in range(full.shape[0])]


def group_scatter(parts):
    if pair_group():
        away = sum(p[1].astype(f32) for p in parts).astype(bf16)
        return sum(p[0].astype(f32) for p in parts) + swap_core(away).astype(f32)
    total = jnp.stack([sum(p[m].astype(f32) for p in parts) for m in range(len(parts[0]))])
    return lax.psum_scatter(total, ("s", "c"), scatter_dimension=0, tiled=False)


def merge_kernel(relate, at_ref, mine_ref, other_ref, out_ref):
    core, chip = at_ref[0], at_ref[1]
    if not relate:
        out_ref[:, core] = mine_ref[...]
        out_ref[:, 1 - core] = other_ref[...]
        return
    quarter = mine_ref.shape[-1] // 4
    for r in range(4):
        to = pl.ds(pl.multiple_of((chip ^ r) * quarter, quarter), quarter)
        at = slice(r * quarter, (r + 1) * quarter)
        out_ref[:, core, :, to] = mine_ref[:, :, at]
        out_ref[:, 1 - core, :, to] = other_ref[:, :, at]


def smem():
    return pl.BlockSpec(memory_space=pltpu.SMEM)


def place():
    return jnp.stack([lax.axis_index("c"), chip_at()]).astype(jnp.int32)


def small_cost(bytes_moved):
    return pl.CostEstimate(flops=0, bytes_accessed=bytes_moved, transcendentals=0)


def by_core(mine, other, relate=False):
    n, rows, width = mine.shape
    step = 1 if n % 3 else n // 3
    block = pl.BlockSpec((step, rows, width), lambda i: (i, 0, 0))
    out = pl.pallas_call(
        functools.partial(merge_kernel, relate),
        grid=(n // step,),
        in_specs=[smem(), block, block],
        out_specs=pl.BlockSpec((step, 2, rows, width), lambda i: (i, 0, 0, 0)),
        out_shape=jax.ShapeDtypeStruct((n, 2, rows, width), mine.dtype),
        cost_estimate=small_cost(mine.size * 8),
        compiler_params=pltpu.CompilerParams(vmem_limit_bytes=32 * 2**20),
        name="merge",
    )(place(), mine, other)
    return out.reshape(n, 2 * rows, width)


def enter_kernel(at_ref, rows_ref, *refs):
    core, chip = at_ref[0], at_ref[1]
    mine_ref, away_ref = refs[-2:]
    size = mine_ref.shape[1]
    model = rows_ref.shape[-1]
    quarter = model // 4
    for ref, which in ((mine_ref, core), (away_ref, 1 - core)):
        span = pl.ds(pl.multiple_of(which * size, size), size)
        for r in range(4):
            at = pl.ds(pl.multiple_of((chip ^ r) * quarter, quarter), quarter)
            ref[:, :, r * quarter : (r + 1) * quarter] = rows_ref[:, span, at]
        if len(refs) == 3:
            ref[:, :, model:] = refs[0][:, span, :]


def to_sequence(rows, *extra):
    seqs, count, width = rows.shape
    width += sum(e.shape[2] for e in extra)
    half = jax.ShapeDtypeStruct((seqs, count // 2, width), rows.dtype)
    mine, away = pl.pallas_call(
        enter_kernel,
        in_specs=[smem()] + [pl.BlockSpec(memory_space=pltpu.VMEM)] * (1 + len(extra)),
        out_specs=[pl.BlockSpec(memory_space=pltpu.VMEM)] * 2,
        out_shape=[half, half],
        cost_estimate=small_cost(rows.size * 4),
        name="enter",
    )(place(), rows, *extra)
    other = swap_core(away)
    every = by_core(mine.reshape(1, -1, width), other.reshape(1, -1, width))
    return lax.all_to_all(every.reshape(2 * seqs, count // 2, width), "z", 0, 0, tiled=True)


def from_sequence(rows):
    core = lax.axis_index("c")
    every = lax.all_to_all(rows, "z", 0, 0, tiled=True)
    seqs = every.shape[0] // 2
    away = lax.dynamic_slice_in_dim(every, (1 - core) * seqs, seqs)
    mine = lax.dynamic_slice_in_dim(every, core * seqs, seqs)
    return by_core(mine, swap_core(away), relate=True)


def pair_kernel(at_ref, mine_ref, other_ref, out_ref):
    core = at_ref[0]
    out_ref[core] = mine_ref[...]
    out_ref[1 - core] = other_ref[...]


def core_pair(mine, other, tile, start, count):
    n, rows, _ = mine.shape
    block = pl.BlockSpec((n, rows, tile), lambda i: (0, 0, start + i))
    return pl.pallas_call(
        pair_kernel,
        grid=(count,),
        in_specs=[smem(), block, block],
        out_specs=pl.BlockSpec((2, n, rows, tile), lambda i: (0, 0, 0, i)),
        out_shape=jax.ShapeDtypeStruct((2, n, rows, count * tile), mine.dtype),
        cost_estimate=small_cost(8 * n * rows * count * tile),
        name="core_pair",
    )(place(), mine, other)


class Gather:
    def __init__(self, own, *before):
        self.own = own
        if square():
            own = after(own, *before)
            self.first = [lax.ppermute(own, "x", SWAP), lax.ppermute(own, "o", SWAP)]
            by_x, by_o = self.first
            self.second = [
                lax.ppermute(by_x[:1], "o", SWAP),
                lax.ppermute(by_o[1:], "x", SWAP),
            ]
        else:
            self.first = self.second = []

    def blocks(self):
        if square():
            return [self.own, *self.first, *self.second]
        full = lax.all_gather(self.own, ("o", "x"), axis=0, tiled=True)
        return [full[i : i + 2] for i in range(0, full.shape[0], 2)]


def grad_slots(model):
    if square():
        return [(2, 0), (3, 0), (0, 0), (3, 1), (2, 1), (1, 0), (0, 1), (1, 1)], [2, 2, 2, 2]
    return [(0, i) for i in range(8)], [8]


def put_rows(out_refs, slots, index, cols, term):
    size = term.shape[0] // 8
    for part, (which, row) in enumerate(slots):
        out_refs[which][index, row * size : (row + 1) * size, cols] = term[
            part * size : (part + 1) * size
        ].astype(bf16)


def add_up(*terms):
    return functools.reduce(jnp.add, [t.astype(f32) for t in terms]).astype(bf16)


def combine_kernel(keep_a, come_a, last_a, keep_b, come_b, last_b, out_ref):
    half = last_a.shape[1]
    for at, (keep, come, last) in enumerate(((keep_a, come_a, last_a), (keep_b, come_b, last_b))):
        out_ref[:, at * half : (at + 1) * half, :] = add_up(keep[...], come[...], last[...])


def combine(keep_a, come_a, last_a, keep_b, come_b, last_b):
    n, half, width = last_a.shape
    block = pl.BlockSpec((1, half, width), lambda i: (i, 0, 0))
    return pl.pallas_call(
        combine_kernel,
        grid=(n,),
        in_specs=[block] * 6,
        out_specs=pl.BlockSpec((1, 2 * half, width), lambda i: (i, 0, 0)),
        out_shape=jax.ShapeDtypeStruct((n, 2 * half, width), bf16),
        cost_estimate=small_cost(16 * n * half * width),
        name="combine",
    )(keep_a, come_a, last_a, keep_b, come_b, last_b)


class Reduction:
    def __init__(self, outs):
        self.step = 0
        self.state = outs
        if square():
            self.state = [
                *outs,
                lax.ppermute(outs[0], "x", SWAP),
                lax.ppermute(outs[1], "o", SWAP),
            ]

    def advance(self):
        step, self.step = self.step, self.step + 1
        state = self.state
        on_line = lax.axis_size("z") == 4
        if step == 0 and square():
            _, _, keep_a, keep_b, come_a, come_b = state
            half = keep_a.shape[1] // 2
            go_a = add_up(keep_a[:, half:], come_a[:, half:])
            go_b = add_up(keep_b[:, half:], come_b[:, half:])
            last_a, last_b = lax.ppermute(go_a, "o", SWAP), lax.ppermute(go_b, "x", SWAP)
            self.state = (keep_a, come_a, last_a, keep_b, come_b, last_b)
            return [go_a, go_b]
        if step == 1:
            if square():
                here = combine(*state)
            else:
                here = lax.psum_scatter(
                    state[0].astype(f32), ("o", "x"), scatter_dimension=1, tiled=True
                ).astype(bf16)
            come = lax.ppermute(here, "z", ((0, 1), (3, 2))) if on_line else None
            self.state = (here, come)
            return [here]
        if step == 2 and on_line:
            here = add_up(*state)
            self.state = (here, lax.ppermute(here, "z", ((1, 2), (2, 1))))
            return [here]
        if step == 3 and on_line:
            here = add_up(*state)
            self.state = (here, lax.ppermute(here, "z", ((1, 0), (2, 3))))
            return [here]
        if step == 4:
            if on_line:
                at = lax.axis_index("z")
                total = jnp.where((at == 0) | (at == 3), state[1], state[0])
            else:
                total = lax.psum(state[0].astype(f32), "z").astype(bf16)
            core = lax.axis_index("c")
            half = total.shape[1] // 2
            mine = lax.dynamic_slice_in_dim(total, core * half, half, 1)
            away = lax.dynamic_slice_in_dim(total, (1 - core) * half, half, 1)
            self.state = (mine, swap_core(away))
            return [total]
        return []


def every_member(done):
    mine, other = done
    first = lax.axis_index("c") == 0
    pair = jnp.stack([jnp.where(first, mine, other), jnp.where(first, other, mine)])
    every = lax.all_gather(pair, "s", axis=0, tiled=True)
    return [every[i] for i in range(every.shape[0])]


def sum_all(terms, before):
    if not (square() and pair_group() and lax.axis_size("z") == 4):
        return lax.psum(terms, EVERY)
    for axis, perm in (
        ("c", SWAP),
        ("x", SWAP),
        ("o", SWAP),
        ("z", ((0, 1), (1, 0), (2, 3), (3, 2))),
        ("z", ((0, 2), (2, 0), (1, 3), (3, 1))),
    ):
        if axis == "z":
            terms = after(terms, before)
        terms = terms + lax.ppermute(terms, axis, perm)
    return terms


def member_cols(start, count):
    return pl.ds(pl.multiple_of(start, 128), count)


def pack_attn_kernel(heads, at_ref, q_ref, k_ref, v_ref, o_ref, *outs):
    for i in range(2):
        member, attn_ref = at_ref[i], outs[i]
        for j in range(0, heads, 2):
            head = member * heads + j
            keys = k_ref[:, member_cols(head * 64, 128)]
            values = v_ref[:, member_cols(head * 64, 128)]
            for m in range(2):
                attn_ref[j + m, :, :128] = q_ref[:, member_cols((head + m) * 128, 128)]
                attn_ref[j + m, :, 128:192] = keys[:, m * 64 : (m + 1) * 64]
                attn_ref[j + m, :, 192:] = values[:, m * 64 : (m + 1) * 64]
        for j in range(heads // 2):
            attn_ref[heads + j] = o_ref[:, member_cols(member * heads * 128 + j * 256, 256)]


def pack_ffn_kernel(at_ref, g_ref, u_ref, d_ref, *outs):
    for i in range(2):
        width = outs[i].shape[2]
        for w, ref in enumerate((g_ref, u_ref, d_ref)):
            outs[i][w] = ref[:, member_cols(at_ref[i] * width, width)]


def pack_call(kernel, members_at, out, weights):
    return pl.pallas_call(
        kernel,
        in_specs=[smem()] + [pl.BlockSpec(memory_space=pltpu.VMEM)] * len(weights),
        out_specs=[pl.BlockSpec(memory_space=pltpu.VMEM)] * 2,
        out_shape=[jax.ShapeDtypeStruct(out, bf16)] * 2,
        cost_estimate=small_cost(2 * 4 * out[0] * out[1] * out[2]),
        compiler_params=pltpu.CompilerParams(vmem_limit_bytes=32 * 2**20),
        name="pack",
    )(members_at, *weights)


def finish_ffn_kernel(at_ref, *refs):
    mines, others, outs = refs[:-3:2], refs[1:-3:2], refs[-3:]
    first = at_ref[0] == 0
    total = sum(m.shape[2] for m in mines)
    start = 0
    for mine_ref, other_ref in zip(mines, others):
        width = mine_ref.shape[2]
        mine, other = mine_ref[0], other_ref[0]
        low = jnp.where(first, mine, other).astype(f32)
        high = jnp.where(first, other, mine).astype(f32)
        for w in range(3):

            @pl.when(pl.program_id(0) == w)
            def _():
                outs[w][:, start : start + width] = low
                outs[w][:, total + start : total + start + width] = high

        start += width


def finish_ffn_call(sums):
    rows = sums[0][0].shape[1]
    out = jax.ShapeDtypeStruct((rows, 2 * sum(s[0].shape[2] for s in sums)), f32)
    arrays = [a for s in sums for a in s]
    return pl.pallas_call(
        finish_ffn_kernel,
        grid=(3,),
        in_specs=[smem()] + [pl.BlockSpec((1, *a.shape[1:]), lambda w: (w, 0, 0)) for a in arrays],
        out_specs=[whole_spec(out.shape)] * 3,
        out_shape=[out] * 3,
        cost_estimate=small_cost(out.size * 18),
        compiler_params=pltpu.CompilerParams(vmem_limit_bytes=40 * 2**20),
        name="finish_ffn",
    )(place(), *arrays)


def finish_heads_kernel(calls, at_ref, *refs):
    first = at_ref[0] == 0
    q_ref, k_ref, v_ref, o_ref = refs[2 * calls :]
    per_call = refs[0].shape[0]
    heads = calls * per_call

    def pick(head):
        mine, other = refs[2 * (head // per_call)], refs[2 * (head // per_call) + 1]
        mine, other = mine[head % per_call], other[head % per_call]
        return [
            jnp.where(first, mine, other).astype(f32),
            jnp.where(first, other, mine).astype(f32),
        ]

    for j in range(0, heads, 2):
        pairs = [pick(j), pick(j + 1)]
        for g in range(2):
            pair = [p[g] for p in pairs]
            head = g * heads + j
            for m in range(2):
                at = slice((head + m) * 128, (head + m + 1) * 128)
                q_ref[:, at] = pair[m][:, :128]
                o_ref[:, at] = pair[m][:, 256:]
            at = slice(head * 64, (head + 2) * 64)
            k_ref[:, at] = jnp.concatenate([p[:, 128:192] for p in pair], axis=1)
            v_ref[:, at] = jnp.concatenate([p[:, 192:256] for p in pair], axis=1)


def finish_heads_call(heads_sums):
    per_call, rows, _ = heads_sums[0][0].shape
    heads = per_call * len(heads_sums)
    wide = jax.ShapeDtypeStruct((rows, heads * 256), f32)
    narrow = jax.ShapeDtypeStruct((rows, heads * 128), f32)
    return pl.pallas_call(
        functools.partial(finish_heads_kernel, len(heads_sums)),
        in_specs=[smem()] + [pl.BlockSpec(memory_space=pltpu.VMEM)] * (2 * len(heads_sums)),
        out_specs=[pl.BlockSpec(memory_space=pltpu.VMEM)] * 4,
        out_shape=[wide, narrow, narrow, wide],
        cost_estimate=small_cost(rows * heads * 768 * 6),
        name="finish_heads",
    )(place(), *[a for s in heads_sums for a in s])


def fill(scratch, refs, index):
    row = 0
    for ref in refs:
        for part in range(ref.shape[0]):
            block = ref[part, index]
            scratch[row : row + block.shape[0], :] = block
            row += block.shape[0]


def ffn_kernel(members, blocks, slots, steps, *refs):
    xs, xts, cots, cotts = [refs[i * members : (i + 1) * members] for i in range(4)]
    rest = refs[4 * members :]
    weights, rest = rest[:blocks], rest[blocks:]
    out_refs, mid_refs = rest[:members], rest[members : 2 * members]
    grads = rest[2 * members : -8]
    gate, up, down, hid, dgate, dup, out_acc, mid_acc = rest[-8:]
    step = pl.program_id(0)
    for i, scratch in enumerate((gate, up, down)):
        fill(scratch, weights, i)

    @pl.when(step == 0)
    def _():
        out_acc[...] = jnp.zeros_like(out_acc)
        mid_acc[...] = jnp.zeros_like(mid_acc)

    own = xs[0].shape[0]
    rows = 512
    for m in range(members):

        def body(i, carry):
            at = pl.ds(pl.multiple_of(i * rows, rows), rows)
            to = pl.ds(pl.multiple_of(m * own + i * rows, rows), rows)
            x = xs[m][at, :]
            g = dot(x, gate[...])
            u = dot(x, up[...])
            dh = dot(cots[m][at, :], down[...])
            sig = jax.nn.sigmoid(g)
            act = g * sig
            h = (act * u).astype(bf16)
            dg = (dh * u * sig * (1.0 + g * (1.0 - sig))).astype(bf16)
            du = (dh * act).astype(bf16)
            hid[to, :] = h
            dgate[to, :] = dg
            dup[to, :] = du
            out_acc[to, :] += dot(h, down[...], NT)
            mid_acc[to, :] += dot(dg, gate[...], NT) + dot(du, up[...], NT)
            return carry

        lax.fori_loop(0, own // rows, body, 0)

    def over_rows(lefts, at, right):
        return functools.reduce(
            jnp.add,
            [dot(l[at, :], right[m * own : (m + 1) * own, :]) for m, l in enumerate(lefts)],
        )

    model = xts[0].shape[0]
    for i, (lefts, right) in enumerate(((xts, dgate), (xts, dup), (cotts, hid))):
        term = over_rows(lefts, slice(0, model), right)
        put_rows(grads, slots, i, slice(None), term)

    @pl.when(step == steps - 1)
    def _():
        for m in range(members):
            out_refs[m][...] = out_acc[m * own : (m + 1) * own, :].astype(bf16)
            mid_refs[m][...] = mid_acc[m * own : (m + 1) * own, :].astype(bf16)


def turn_kernel(in_ref, out_ref):
    out_ref[...] = in_ref[...].T


def turn(rows, width):
    count = rows.shape[0]
    return pl.pallas_call(
        turn_kernel,
        grid=(2,),
        in_specs=[pl.BlockSpec((count, width // 2), lambda i: (0, i))],
        out_specs=pl.BlockSpec((width // 2, count), lambda i: (i, 0)),
        out_shape=jax.ShapeDtypeStruct((width, count), rows.dtype),
        cost_estimate=small_cost(rows.size * 4),
        name="turn",
    )(rows)


def whole_spec(shape):
    zeros = (0,) * len(shape)
    return pl.BlockSpec(shape, lambda *_: zeros)


def single_spec(shape):
    zeros = (0,) * len(shape)
    return pl.BlockSpec(shape, lambda *_: zeros, pipeline_mode=pl.Buffered(1))


SHARE = 32

CHUNKS = (3, 3, 3)


def ffn_call(tile, steps, x, x_t, cot, cot_t, weights):
    members = len(x)
    own, model = x[0].shape
    rows = own * members
    width = steps * tile
    slots, heights = grad_slots(model)
    size = model // 8
    return pl.pallas_call(
        functools.partial(ffn_kernel, members, len(weights), slots, steps),
        grid=(steps,),
        in_specs=[single_spec((own, model))] * members
        + [single_spec(a.shape) for a in (*x_t, *cot, *cot_t)]
        + [
            pl.BlockSpec((w.shape[0], 3, w.shape[2], tile), lambda j: (0, 0, 0, j))
            for w in weights
        ],
        out_specs=[single_spec((own, model))] * (2 * members)
        + [pl.BlockSpec((3, n * size, tile), lambda j: (0, 0, j)) for n in heights],
        out_shape=[jax.ShapeDtypeStruct((own, model), bf16)] * (2 * members)
        + [jax.ShapeDtypeStruct((3, n * size, width), bf16) for n in heights],
        scratch_shapes=[pltpu.VMEM((model, tile), bf16)] * 3
        + [pltpu.VMEM((rows, tile), bf16)] * 3
        + [pltpu.VMEM((rows, model), f32)] * 2,
        compiler_params=pltpu.CompilerParams(vmem_limit_bytes=58 * 2**20),
        cost_estimate=pl.CostEstimate(
            flops=18 * rows * model * width // SHARE,
            bytes_accessed=(6 * rows * model * 2 + 12 * model * width) // SHARE,
            transcendentals=rows * width // SHARE,
        ),
        name="ffn",
    )(*x, *x_t, *cot, *cot_t, *weights)


def lanes_first():
    return lax.broadcasted_iota(jnp.int32, (1, 128), 1) < 64


def head_mean(square_terms):
    first = lanes_first()
    low = jnp.sum(jnp.where(first, square_terms, 0.0), axis=-1, keepdims=True)
    high = jnp.sum(jnp.where(first, 0.0, square_terms), axis=-1, keepdims=True)
    return jnp.where(first, low, high) * (1.0 / 64)


def partner(u):
    low = (lax.broadcasted_iota(jnp.int32, (1, 128), 1) & 63) < 32
    return jnp.where(low, -pltpu.roll(u, 96, 1), pltpu.roll(u, 32, 1))


def natural_rows(flip, members, own, size):
    for m in range(members):
        for i in range(own // size):
            to = pl.multiple_of((i * members + (m ^ flip)) * size, size)
            yield m, i * size, pl.ds(to, size)


def project(flip, size, xs, weights, w_scr, qkv):
    fill(w_scr, weights, 0)
    own = xs[0].shape[0]
    terms = [dot(x[...], w_scr[...]) for x in xs]
    for m, row, at in natural_rows(flip, len(xs), own, size):
        qkv[at, :] = terms[m][row : row + size]


def heads_of(u, gain, cosines, sines):
    inv = lax.rsqrt(head_mean(u * u) + epsilon)
    hat = u * inv
    turned = hat * gain
    return inv, hat, turned * cosines + partner(turned) * sines


def stack_heads(block):
    return jnp.concatenate([block[:, :64], block[:, 64:]], axis=0)


def unstack_heads(turned):
    half = turned.shape[1] // 2
    return jnp.concatenate([turned[:, :half], turned[:, half:]], axis=0).T


BLOCK = 256


def probs_of(q2, keys, block):
    parts = []
    for at in range(block + 1):
        parts.append(dot(keys[at * BLOCK : (at + 1) * BLOCK, :], q2, NT))
    key_at = lax.broadcasted_iota(jnp.int32, parts[-1].shape, 0)
    query_at = lax.broadcasted_iota(jnp.int32, parts[-1].shape, 1) & (BLOCK - 1)
    parts[-1] = jnp.where(key_at <= query_at, parts[-1], -1e30)
    top = functools.reduce(jnp.maximum, [jnp.max(p, axis=0, keepdims=True) for p in parts])
    parts = [jnp.exp(p - top) for p in parts]
    total = functools.reduce(jnp.add, [jnp.sum(p, axis=0, keepdims=True) for p in parts])
    inv = 1.0 / total
    return [p * inv for p in parts]


def attention_kernel(members, blocks, size, at_ref, *refs):
    xs, rest = refs[:members], refs[members:]
    cos_ref, sin_ref, qg_ref, kg_ref = rest[:4]
    weights, rest = rest[4 : 4 + blocks], rest[4 + blocks :]
    mixed_refs, rest = rest[:members], rest[members:]
    w_scr, qkv, q_scr, k_scr, vt_scr, mixed_scr = rest
    flip = at_ref[0]
    project(flip, size, xs, weights, w_scr, qkv)
    cosines, sines = cos_ref[...], sin_ref[...]
    _, _, q = heads_of(qkv[:, :128], qg_ref[...], cosines, sines)
    q_scr[...] = q.astype(bf16) * jnp.asarray(0.125, bf16)
    _, _, k = heads_of(qkv[:, 128:], kg_ref[...], cosines, sines)
    k_scr[...] = k[:, :64].astype(bf16)
    vt_scr[...] = qkv[:, 192:].astype(bf16).T
    for block in range(q_scr.shape[0] // BLOCK):
        at = slice(block * BLOCK, (block + 1) * BLOCK)
        q2 = stack_heads(q_scr[at, :])
        probs = probs_of(q2, k_scr, block)
        total = None
        for i, p in enumerate(probs):
            term = dot(vt_scr[:, i * BLOCK : (i + 1) * BLOCK], p.astype(bf16))
            total = term if total is None else total + term
        mixed_scr[at, :] = unstack_heads(total).astype(bf16)
    for m, row, at in natural_rows(flip, members, xs[0].shape[0], size):
        mixed_refs[m][row : row + size, :] = mixed_scr[at, :]


def attention_back_kernel(members, blocks, slots, steps, size, at_ref, *refs):
    xs, xts, das, mixes = [refs[i * members : (i + 1) * members] for i in range(4)]
    rest = refs[4 * members :]
    cos_ref, sin_ref, qg_ref, kg_ref = rest[:4]
    dms, rest = rest[4 : 4 + members], rest[4 + members :]
    weights, rest = rest[:blocks], rest[blocks:]
    din_refs, gains_ref, grads = rest[:members], rest[members], rest[members + 1 : -12]
    rest = rest[-12:]
    w_scr, qkv, q_scr, k_scr, v_scr, kt_scr, dm_scr, dq_scr, dkv_scr, dall, dqkv, din_acc = rest
    flip = at_ref[0]
    own = xs[0].shape[0]
    step = pl.program_id(0)
    project(flip, size, xs, weights, w_scr, qkv)
    for m, row, at in natural_rows(flip, members, own, size):
        dm_scr[at, :] = dms[m][row : row + size, :]
    cosines, sines = cos_ref[...], sin_ref[...]
    q_gain, k_gain = qg_ref[...], kg_ref[...]
    q_inv, q_hat, q = heads_of(qkv[:, :128], q_gain, cosines, sines)
    q_scr[...] = q.astype(bf16) * jnp.asarray(0.125, bf16)
    k_inv, k_hat, k = heads_of(qkv[:, 128:], k_gain, cosines, sines)
    k_scr[...] = k[:, :64].astype(bf16)
    kt_scr[...] = k[:, :64].astype(bf16).T
    v_scr[...] = qkv[:, 192:].astype(bf16)
    dkv_scr[...] = jnp.zeros_like(dkv_scr)
    for block in range(q_scr.shape[0] // BLOCK):
        at = slice(block * BLOCK, (block + 1) * BLOCK)
        q2 = stack_heads(q_scr[at, :])
        do2 = stack_heads(dm_scr[at, :])
        probs = probs_of(q2, k_scr, block)
        backs = [
            dot(v_scr[i * BLOCK : (i + 1) * BLOCK, :], do2, NT) for i in range(block + 1)
        ]
        delta = functools.reduce(
            jnp.add, [jnp.sum(p * b, axis=0, keepdims=True) for p, b in zip(probs, backs)]
        )
        total = None
        for i, (p, b) in enumerate(zip(probs, backs)):
            ds = (p * (b - delta)).astype(bf16)
            keys = slice(i * BLOCK, (i + 1) * BLOCK)
            term = dot(kt_scr[:, keys], ds)
            total = term if total is None else total + term
            dkv_scr[keys, :] += jnp.concatenate([dot(ds, q2), dot(p.astype(bf16), do2)], axis=1)
        dq_scr[at, :] = unstack_heads(total) * 0.125
    first = lanes_first()
    dq = dq_scr[...].astype(bf16).astype(f32)
    dkv = dkv_scr[...].astype(bf16).astype(f32)
    dq = dq * cosines - partner(dq) * sines
    dk = dkv * cosines - partner(dkv) * sines
    q_part = jnp.sum(dq * q_hat, axis=0, keepdims=True)
    k_part = jnp.sum(jnp.where(first, dk * k_hat, 0.0), axis=0, keepdims=True)
    both = jnp.concatenate([q_part, k_part], axis=0)

    @pl.when(step == 0)
    def _():
        gains_ref[...] = both
        din_acc[...] = jnp.zeros_like(din_acc)

    @pl.when(step > 0)
    def _():
        gains_ref[...] += both

    scaled = dq * q_gain
    d_q = q_inv * (scaled - q_hat * head_mean(scaled * q_hat))
    scaled = dk * k_gain
    d_k = k_inv * (scaled - k_hat * head_mean(scaled * k_hat))
    dall[:, :128] = d_q.astype(bf16)
    dall[:, 128:] = jnp.where(first, d_k, dkv).astype(bf16)
    for m, row, at in natural_rows(flip, members, own, size):
        dqkv[m * own + row : m * own + row + size, :] = dall[at, :]
    din_acc[...] += dot(dqkv[...], w_scr[...], NT)
    term = sum(dot(xt[...], dqkv[m * own : (m + 1) * own, :]) for m, xt in enumerate(xts))
    put_rows(grads, slots, 0, slice(0, 256), term)
    term = sum(dot(da[...], mix[...]) for da, mix in zip(das, mixes))
    put_rows(grads, slots, 0, slice(256, 384), term)

    @pl.when(step == steps - 1)
    def _():
        for m in range(members):
            din_refs[m][...] = din_acc[m * own : (m + 1) * own, :].astype(bf16)


def attention_cost(length, heads, model, products):
    return pl.CostEstimate(
        flops=heads * (products * 2 * length * length * 64 + 2 * length * model * 256) // SHARE,
        bytes_accessed=4 * length * model * 2 // SHARE,
        transcendentals=heads * 2 * length * length // SHARE,
    )


def weight_specs(weights, start=0):
    return [
        pl.BlockSpec((w.shape[0], 1, w.shape[2], 256), lambda j: (0, j + start, 0, 0))
        for w in weights
    ]


def attention_call(flip, size, heads, x, cosines, sines, q_gain, k_gain, weights):
    members = len(x)
    own, model = x[0].shape[0], 128 * (x[0].shape[1] // 128 - 1)
    length = members * own
    return pl.pallas_call(
        functools.partial(attention_kernel, members, len(weights), size),
        grid=(heads,),
        in_specs=[smem()]
        + [single_spec((own, model))] * members
        + [single_spec(a.shape) for a in (cosines, sines, q_gain, k_gain)]
        + weight_specs(weights),
        out_specs=[pl.BlockSpec((own, 128), lambda j: (0, j))] * members,
        out_shape=[jax.ShapeDtypeStruct((own, heads * 128), bf16)] * members,
        scratch_shapes=[
            pltpu.VMEM((model, 256), bf16),
            pltpu.VMEM((length, 256), f32),
            pltpu.VMEM((length, 128), bf16),
            pltpu.VMEM((length, 64), bf16),
            pltpu.VMEM((64, length), bf16),
            pltpu.VMEM((length, 128), bf16),
        ],
        compiler_params=pltpu.CompilerParams(vmem_limit_bytes=48 * 2**20),
        cost_estimate=attention_cost(length, heads, model, 4),
        name="attention",
    )(flip, *x, cosines, sines, q_gain, k_gain, *weights)


def attention_back_call(
    flip, size, start, heads, x, x_t, d_attn_t, mixed, cosines, sines, q_gain, k_gain, d_mixed, weights
):
    members = len(x)
    own, model = x_t[0].shape[1], x_t[0].shape[0]
    length = members * own
    slots, heights = grad_slots(model)
    eighth = model // 8
    return pl.pallas_call(
        functools.partial(attention_back_kernel, members, len(weights), slots, heads, size),
        grid=(heads,),
        in_specs=[smem()]
        + [single_spec(s) for s in [(own, model)] * members + [(model, own)] * (2 * members)]
        + [pl.BlockSpec((own, 128), lambda j: (0, j + start))] * members
        + [single_spec(a.shape) for a in (cosines, sines, q_gain, k_gain)]
        + [pl.BlockSpec((own, 128), lambda j: (0, j + start))] * members
        + weight_specs(weights, start),
        out_specs=[single_spec((own, model))] * members
        + [whole_spec((2, 128))]
        + [pl.BlockSpec((1, n * eighth, 384), lambda j: (j, 0, 0)) for n in heights],
        out_shape=[jax.ShapeDtypeStruct((own, model), bf16)] * members
        + [jax.ShapeDtypeStruct((2, 128), f32)]
        + [jax.ShapeDtypeStruct((heads, n * eighth, 384), bf16) for n in heights],
        scratch_shapes=[
            pltpu.VMEM((model, 256), bf16),
            pltpu.VMEM((length, 256), f32),
            pltpu.VMEM((length, 128), bf16),
            pltpu.VMEM((length, 64), bf16),
            pltpu.VMEM((length, 64), bf16),
            pltpu.VMEM((64, length), bf16),
            pltpu.VMEM((length, 128), bf16),
            pltpu.VMEM((length, 128), f32),
            pltpu.VMEM((length, 128), f32),
            pltpu.VMEM((length, 256), bf16),
            pltpu.VMEM((length, 256), bf16),
            pltpu.VMEM((length, model), f32),
        ],
        compiler_params=pltpu.CompilerParams(vmem_limit_bytes=58 * 2**20),
        cost_estimate=attention_cost(length, heads, model, 10),
        name="attention_back",
    )(flip, *x, *x_t, *d_attn_t, *mixed, cosines, sines, q_gain, k_gain, *d_mixed, *weights)


def local(
    tokens,
    positions,
    cotangent,
    q_weight,
    key_matrix,
    value_matrix,
    out_weight,
    gate_weight,
    up_weight,
    down_weight,
    attn_gain,
    ffn_gain,
    q_gain,
    k_gain,
):
    model = tokens.shape[2]
    rows_here = q_weight.shape[0]
    members = 2 * lax.axis_size("s")
    q_cols, kv_cols = q_weight.shape[1], key_matrix.shape[1]
    heads = kv_cols // 64 // members
    chunks = len(CHUNKS)
    core = lax.axis_index("c")
    first_member = 2 * lax.axis_index("s")
    members_at = jnp.stack([first_member + core, first_member + 1 - core]).astype(jnp.int32)
    flip = jnp.stack([flip_at(), chip_at()]).astype(jnp.int32)

    attn_mine, attn_away = pack_call(
        functools.partial(pack_attn_kernel, heads),
        members_at,
        (heads + heads // 2, rows_here, 256),
        (q_weight, key_matrix, value_matrix, out_weight),
    )
    attn_own = core_pair(attn_mine, swap_core(attn_away), 256, 0, 1)
    attn_gather = Gather(attn_own)
    attn_blocks = attn_gather.blocks()
    ffn_cols = gate_weight.shape[1] // members
    tile = ffn_cols // sum(CHUNKS)
    ffn_mine, ffn_away = pack_call(
        pack_ffn_kernel, members_at, (3, rows_here, ffn_cols), (gate_weight, up_weight, down_weight)
    )
    ffn_other = swap_core(ffn_away)
    gathers = []
    for k, count in enumerate(CHUNKS):
        own_part = core_pair(ffn_mine, ffn_other, tile, sum(CHUNKS[:k]), count)
        before = (gathers[-1] if k else attn_gather).first
        gathers.append(Gather(own_part, *before))

    high, low = positions // 128, positions % 128
    place_cols = jnp.stack([high, low], axis=2).astype(bf16)
    place_cols = jnp.pad(place_cols, ((0, 0), (0, 0), (0, 126)))
    tok = to_sequence(tokens, place_cols)
    quarters, size, _ = tok.shape
    own = quarters * size
    length = own * members
    tok = tok.reshape(own, model + 128)
    place_cols = tok[:, model:]
    tok = tok[:, :model].astype(f32)
    attn_gain_r = relative(attn_gain)
    ffn_gain_r = relative(ffn_gain)
    in_scale = rms_scale(tok)
    in_hat = tok * in_scale
    x = group_gather(jnp.concatenate([(in_hat * attn_gain_r).astype(bf16), place_cols], axis=1))
    x_t = [turn(a, model) for a in x]

    pos = [a[:, model : model + 2].astype(f32) for a in x]
    pos = jnp.stack([(p[:, 0] * 128.0 + p[:, 1]).reshape(quarters, size) for p in pos], axis=1)
    if pair_group():
        pos = jnp.where(core == 0, pos, pos[:, ::-1])
    inverse = rope_base ** (-(2.0 * jnp.arange(32, dtype=f32)) / 64)
    turned = pos.reshape(length)[:, None] * inverse[None, :]
    cosines = jnp.tile(jnp.cos(turned), (1, 4))
    sines = jnp.tile(jnp.sin(turned), (1, 4))
    q_gain2 = jnp.tile(q_gain, 2)[None]
    k_gain2 = jnp.tile(k_gain, 2)[None]

    cot_own = to_sequence(after(cotangent, x[0])).reshape(own, model)
    cot = group_gather(cot_own)
    cot_t = [turn(a, model) for a in cot]

    mixed = attention_call(
        after(flip, *gathers[0].first), size, heads, x, cosines, sines, q_gain2, k_gain2, attn_blocks
    )
    out_w = jnp.concatenate(
        [
            jnp.concatenate([b[i, heads + j] for j in range(heads // 2)], axis=1)
            for b in attn_blocks
            for i in range(b.shape[0])
        ],
        axis=0,
    )
    mixed = [after(mixed[0], *gathers[0].second, cot[1]), *mixed[1:]]
    residual = tok + group_scatter([[dot(m, out_w, NT) for m in mixed]])
    residual = after(residual, *gathers[1].first)
    mid_scale = rms_scale(residual)
    mid_hat = residual * mid_scale
    mid = group_gather((mid_hat * ffn_gain_r).astype(bf16))
    mid_t = [turn(a, model) for a in mid]

    out_parts, mid_parts, sums = [], [], []

    def step_all(*which):
        return [a for i in which for a in sums[i].advance()]

    for k in range(chunks):
        waits = []
        if k == 0:
            waits = gathers[1].second
        elif k == 1:
            waits = gathers[2].first
        else:
            waits = step_all(0)
        parts = ffn_call(
            tile,
            CHUNKS[k],
            [after(mid[0], *waits), *mid[1:]],
            mid_t,
            cot,
            cot_t,
            gathers[k].blocks(),
        )
        out_parts.append(parts[:members])
        mid_parts.append(parts[members : 2 * members])
        sums.append(Reduction(parts[2 * members :]))

    d_mid = group_scatter(mid_parts)
    ffn_gain_part = jnp.sum(d_mid * mid_hat, axis=0)
    d_resid = cot_own.astype(f32) + norm_back(d_mid, mid_hat, mid_scale, ffn_gain_r)
    d_attn = group_gather(d_resid.astype(bf16))
    waits = step_all(0, 1) + step_all(0, 1)
    d_mixed = [dot(d, out_w).astype(bf16) for d in d_attn]
    d_attn_t = [turn(d, model) for d in d_attn]

    calls = 2 if heads % 4 == 0 else 1
    d_in_parts, gain_parts = [], []
    for call in range(calls):
        waits = waits + step_all(2) if call == 0 else step_all(0, 1, 2) + step_all(2)
        parts = attention_back_call(
            after(flip, *waits),
            size,
            call * (heads // calls),
            heads // calls,
            x,
            x_t,
            d_attn_t,
            mixed,
            cosines,
            sines,
            q_gain2,
            k_gain2,
            d_mixed,
            attn_blocks,
        )
        d_in_parts.append(parts[:members])
        gain_parts.append(parts[members])
        sums.append(Reduction(parts[members + 1 :]))
    head_gains = sum(gain_parts)
    d_in_parts[-1] = [after(d_in_parts[-1][0], *step_all(1, 2)), *d_in_parts[-1][1:]]
    out_parts[0] = [after(out_parts[0][0], d_in_parts[0][0]), *out_parts[0][1:]]
    while any(r.step < 5 for r in sums):
        step_all(*[i for i, r in enumerate(sums) if r.step < 5])
    ffn_sums = [r.state for r in sums[:chunks]]
    heads_sums = [r.state for r in sums[chunks:]]
    d_in = group_scatter(d_in_parts)
    attn_gain_part = jnp.sum(d_in * in_hat, axis=0)
    input_grad = d_resid + norm_back(d_in, in_hat, in_scale, attn_gain_r)
    input_grad = from_sequence(input_grad.astype(bf16).reshape(quarters, size, model))

    output = (residual + group_scatter(out_parts)).astype(bf16)
    output = from_sequence(output.reshape(quarters, size, model))

    gain_sums = sum_all(
        jnp.concatenate(
            [
                relative(attn_gain_part),
                relative(ffn_gain_part),
                head_gains[0, :64] + head_gains[0, 64:],
                head_gains[1, :64],
            ]
        ),
        ffn_sums[-1][0],
    )

    if members == 2:
        ffn_grads = finish_ffn_call(ffn_sums)
        q_grad, k_grad, v_grad, out_grad = finish_heads_call(heads_sums)
    else:
        heads_all = [every_member(h) for h in heads_sums]
        every = jnp.concatenate([h[i] for i in range(members) for h in heads_all], axis=0)
        every = every.transpose(1, 0, 2).astype(f32)
        ffn_sums = [every_member(s) for s in ffn_sums]
        q_grad = every[:, :, :128].reshape(rows_here, q_cols)
        k_grad = every[:, :, 128:192].reshape(rows_here, kv_cols)
        v_grad = every[:, :, 192:256].reshape(rows_here, kv_cols)
        out_grad = every[:, :, 256:].reshape(rows_here, q_cols)
        ffn_grads = [
            jnp.concatenate(
                [ffn_sums[k][i][w] for i in range(members) for k in range(chunks)], axis=1
            ).astype(f32)
            for w in range(3)
        ]
    return (
        output,
        input_grad,
        q_grad,
        k_grad,
        v_grad,
        out_grad,
        ffn_grads[0],
        ffn_grads[1],
        ffn_grads[2],
        gain_sums[:model],
        gain_sums[model : 2 * model],
        gain_sums[2 * model : 2 * model + 64],
        gain_sums[2 * model + 64 :],
    )


def solution(mesh):
    dp, seq = mesh.devices.shape
    lines = 4
    fine = Mesh(mesh.devices.reshape(dp // 4, 2, 2, lines, seq // lines), EVERY)
    rows, cols = ("o", "x", "c"), ("z", "s")
    tokens = P(rows, cols, None)
    weight = P(rows, None)
    return jax.shard_map(
        local,
        mesh=fine,
        in_specs=(tokens, P(rows, cols), tokens) + (weight,) * 7 + (P(),) * 4,
        out_specs=(tokens, tokens) + (weight,) * 7 + (P(),) * 4,
        check_vma=False,
    )
```

time: 811 us -> 637 us (0.79)
  waiting for transfers between devices: 256 us -> 169 us
  Pallas kernels: 135 us -> 208 us
  blocking collectives: 56.6 us -> 0 us
  other arithmetic: 133 us -> 80 us
  starting transfers between devices: 155 us -> 118 us
  local copies, waits for them, and re-layouts: 56.8 us -> 41.7 us
    ppermute x70 -> x56, waiting for transfers between devices: 249 us -> 169 us  [the longest x5 49.1 us: advance(): self.state = (here, lax.ppermute(here, 'z', ((1, 0), (2, 3))))]
    pallas_call x5 -> x33, Pallas kernels: 135 us -> 208 us  [the longest x3 71.7 us: ffn_call(): pl.pallas_call(functools.partial(ffn_kernel, members, len(weights), slots...]
    ppermute x70 -> x56, starting transfers between devices: 135 us -> 79.9 us  [the longest x5 23.6 us: advance(): come = lax.ppermute(here, 'z', ((0, 1), (3, 2))) if on_line else None]
    psum x1 -> x0, blocking collectives: 42.4 us -> none  [local(): gain_sums = lax.psum(gain_terms, EVERY)]
    select_n x41 -> x4, other arithmetic: 39.3 us -> 4.06 us  [the longest x3 4.06 us: advance(): total = jnp.where((at == 0) | (at == 3), state[1], state[0])]
    all_to_all x2, starting transfers between devices: 8.32 us -> 24.4 us  [from_sequence(): every = lax.all_to_all(rows, 'z', 0, 0, tiled=True)]
    all_gather x1 -> x0, blocking collectives: 14.2 us -> none  [local(): every_pos = lax.all_gather(positions, ('z', 's', 'c'), axis=0)]
    concatenate x22 -> x4, other arithmetic: 15.7 us -> 1.79 us  [the longest x1 1.11 us: local(): jnp.concatenate([(in_hat * attn_gain_r).astype(bf16), place_cols], axis=1)]
  transfers between devices with their start and end apart: 96 -> 79, of which waited for: 26 -> 18; matrix products, arithmetic and copies ran while one was open for 23% -> 18% of each run, Pallas kernels for 13% -> 32%
where the time goes in v2:
time: 637 us; the launch traced here: 631 us
  Pallas kernels  208 us (33%)
  waiting for transfers between devices  169 us (27%)
  starting transfers between devices  118 us (19%)
  other arithmetic  80 us (13%)
  local copies, waits for them, and re-layouts  41.7 us (7%)
  matrix products  11.9 us (2%)
    pallas_call x3, Pallas kernels, ffn_call(): pl.pallas_call(functools.partial(ffn_kernel, members, len(weights), slots...  71.7 us
    ppermute x5, waiting for transfers between devices, advance(): self.state = (here, lax.ppermute(here, 'z', ((1, 0), (2, 3))))  49.1 us
    pallas_call x2, Pallas kernels, attention_back_call(): pl.pallas_call(functools.partial(attention_back_kernel, members, len(weig...  48.1 us
    ppermute x4, waiting for transfers between devices, __init__(): lax.ppermute(by_o[1:], 'x', SWAP)  38.4 us
    ppermute x4, waiting for transfers between devices, __init__(): lax.ppermute(by_x[:1], 'o', SWAP)  33.8 us
    convert_element_type x20, other arithmetic, add_up(): functools.reduce(jnp.add, [t.astype(f32) for t in terms]).astype(bf16)  30.9 us
    ppermute x8, waiting for transfers between devices, __init__(): self.first = [lax.ppermute(own, 'x', SWAP), lax.ppermute(own, 'o', SWAP)]  30.2 us
    all_to_all x2, starting transfers between devices, from_sequence(): every = lax.all_to_all(rows, 'z', 0, 0, tiled=True)  24.4 us
  transfers between devices with their start and end apart: 79, of which 18 were waited for; matrix products, arithmetic and copies ran while one was open for 18% of the time, Pallas kernels for 32%

profile of v2, /device:TPU:0, one launch (start us, length us, event | category | flops | bytes accessed | tf_op | source)
XLA Modules:
  0.0 630.8 jit_solution(227079143552297269)
XLA Ops:
  16.7 6.3 %all-to-all-start = ((bf16[4,128,1152]{2,1,0:T(8,128)(2,1)}), bf16[4,128,1152]{2,1,0:T(8,128)(2,1)}, u32[]{:S(2)}, u32[]{:S(2)}) async-start(bf16[4,128,1152]{2,1,0:T(8,128)(2,1)} %bitcast.6), calls=%async_computation | async-start | bytes 2359296 | tf_op jit(solution)/shard_map/all_to_all | solution.py:156
  34.5 14.2 %collective-permute-done.3.refs_7_.refs_15_ = bf16[2,6,128,256]{3,2,1,0:T(8,128)(2,1)S(1)} collective-permute-done((bf16[2,6,128,256]{3,2,1,0:T(8,128)(2,1)}, bf16[2,6,128,256]{3,2,1,0:T(8,128)(2,1)S(1)}, u32[]{:S(2)}, u32[]{:S(2)}) %collective-permute-start.3) | collective-permute-done | bytes 786464 | tf_op jit(solution)/shard_map/ppermute | solution.py:193
  64.4 3.3 core_pair.4.refs_8_
  72.8 5.3 all-to-all-start.1
  80.7 15.7 %collective-permute-done.5.refs_9_ = bf16[2,3,128,768]{3,2,1,0:T(8,128)(2,1)} collective-permute-done((bf16[2,3,128,768]{3,2,1,0:T(8,128)(2,1)}, bf16[2,3,128,768]{3,2,1,0:T(8,128)(2,1)}, u32[]{:S(2)}, u32[]{:S(2)}) %collective-permute-start.5) | collective-permute-done | bytes 1179680 | tf_op jit(solution)/shard_map/ppermute | solution.py:193
  105.4 18.7 %attention.1 = (bf16[512,512]{1,0:T(8,128)(2,1)S(1)}, bf16[512,512]{1,0:T(8,128)(2,1)S(1)}) custom-call(s32[2]{0:T(128)S(1)} %copy-done.28, bf16[512,1152]{1,0:T(8,128)(2,1)} %pad_maximum_fusion.refs_0_.in_ref, bf16[512,1152]{1,0:T(8,128)(2,1)} %collective-permute-done.7.refs_1_.in_ref, f32[1024,128]{1,0:T(8,128)S(1)} %copy.58.refs_2_.refs_8_, ...), custom_call_target="tpu_custom_call" | custom-call | flops 134217728 | bytes 262144 | tf_op jit(solution)/shard_map/attention/pallas_call | solution.py:768
  137.4 36.0 %collective-permute-done.11.refs_12_ = bf16[1,3,128,768]{3,2,1,0:T(8,128)(2,1)S(1)} collective-permute-done((bf16[1,3,128,768]{3,2,1,0:T(8,128)(2,1)S(1)}, bf16[1,3,128,768]{3,2,1,0:T(8,128)(2,1)S(1)}, u32[]{:S(2)}, u32[]{:S(2)}) %collective-permute-start.11) | collective-permute-done | bytes 589856 | tf_op jit(solution)/shard_map/ppermute | solution.py:197
  192.3 3.8 collective-permute-done.17.refs_11_
  203.0 23.9 %ffn.3 = (bf16[512,1024]{1,0:T(8,128)(2,1)}, bf16[512,1024]{1,0:T(8,128)(2,1)}, bf16[512,1024]{1,0:T(8,128)(2,1)}, bf16[512,1024]{1,0:T(8,128)(2,1)}, bf16[3,256...) custom-call(bf16[512,1024]{1,0:T(8,128)(2,1)} %multiply_convert_fusi, ...), custom_call_target="tpu_custom_call" | custom-call | flops 452984832 | bytes 688128 | tf_op jit(solution)/shard_map/ffn/pallas_call | solution.py:551
  229.0 23.7 %ffn.4 = (bf16[512,1024]{1,0:T(8,128)(2,1)}, bf16[512,1024]{1,0:T(8,128)(2,1)}, bf16[512,1024]{1,0:T(8,128)(2,1)}, bf16[512,1024]{1,0:T(8,128)(2,1)}, bf16[3,256...) custom-call(bf16[512,1024]{1,0:T(8,128)(2,1)} %multiply_convert_fusi, ...), custom_call_target="tpu_custom_call" | custom-call | flops 452984832 | bytes 688128 | tf_op jit(solution)/shard_map/ffn/pallas_call | solution.py:551
  261.7 29.9 %collective-permute-done.31.refs_11_ = bf16[1,3,128,768]{3,2,1,0:T(8,128)(2,1)S(1)} collective-permute-done((bf16[1,3,128,768]{3,2,1,0:T(8,128)(2,1)S(1)}, bf16[1,3,128,768]{3,2,1,0:T(8,128)(2,1)S(1)}, u32[]{:S(2)}, u32[]{:S(2)}) %collective-permute-start.31) | collective-permute-done | bytes 589856 | tf_op jit(solution)/shard_map/ppermute | solution.py:196
  293.1 24.1 %ffn.5 = (bf16[512,1024]{1,0:T(8,128)(2,1)}, bf16[512,1024]{1,0:T(8,128)(2,1)}, bf16[512,1024]{1,0:T(8,128)(2,1)}, bf16[512,1024]{1,0:T(8,128)(2,1)}, bf16[3,256...) custom-call(bf16[512,1024]{1,0:T(8,128)(2,1)} %multiply_convert_fusi, ...), custom_call_target="tpu_custom_call" | custom-call | flops 452984832 | bytes 688128 | tf_op jit(solution)/shard_map/ffn/pallas_call | solution.py:551
  317.3 3.6 add_convert_fusion.9
  331.6 3.5 add_convert_fusion.8
  337.0 3.9 combine.5
  342.4 5.0 collective-permute-start.28
  347.3 4.0 combine.6
  351.3 3.3 multiply_reduce_fusion
  354.7 4.3 fusion.21
  366.9 5.1 collective-permute-start.40
  386.0 24.1 %attention_back.2 = (bf16[512,1024]{1,0:T(8,128)(2,1)}, bf16[512,1024]{1,0:T(8,128)(2,1)}, f32[2,128]{1,0:T(2,128)}, bf16[2,256,384]{2,1,0:T(8,128)(2,1)}, bf16[...) custom-call(s32[2]{0:T(128)} %pad_add_fusion.at_ref, ...), custom_call_target="tpu_custom_call" | custom-call | flops 117440512 | bytes 262144 | tf_op jit(solution)/shard_map/attention_back/pallas_call | solution.py:799
  413.1 4.0 combine.7
  435.0 4.4 all-to-all-start.2
  442.9 4.0 collective-permute-start.52
  454.0 24.0 %attention_back.3 = (bf16[512,1024]{1,0:T(8,128)(2,1)}, bf16[512,1024]{1,0:T(8,128)(2,1)}, f32[2,128]{1,0:T(2,128)}, bf16[2,256,384]{2,1,0:T(8,128)(2,1)}, bf16[...) custom-call(s32[2]{0:T(128)} %pad_add_fusion.at_ref, ...), custom_call_target="tpu_custom_call" | custom-call | flops 117440512 | bytes 262144 | tf_op jit(solution)/shard_map/attention_back/pallas_call | solution.py:799
  483.7 4.1 collective-permute-done.58.come_b
  497.7 6.4 %collective-permute-start.60 = (bf16[2,256,384]{2,1,0:T(8,128)(2,1)}, bf16[2,256,384]{2,1,0:T(8,128)(2,1)}, u32[]{:S(2)}, u32[]{:S(2)}) collective-permute-start(bf16[2,256,384]{2,1,0:T(8,128)(2,1)} %combine.9), channel_id=1, source_target_pairs={{0,1},{3,2},{4,5},{7,6},{8,9},{11,10},{12,13},{15,14},{16,17},{19,... | collective-permute-start | bytes 1179656 | tf_op jit(solution)/shard_map/ppermute | solution.py:277
  520.4 4.3 fusion.9
  524.7 20.0 %all-to-all-start.3 = ((bf16[4,128,1024]{2,1,0:T(8,128)(2,1)}), bf16[4,128,1024]{2,1,0:T(8,128)(2,1)}, u32[]{:S(2)}, u32[]{:S(2)}) async-start(bf16[4,128,1024]{2,1,0:T(8,128)(2,1)} %bitcast.75), calls=%async_computation.3 | async-start | bytes 2097152 | tf_op jit(solution)/shard_map/all_to_all | solution.py:161
  554.7 7.8 %collective-permute-done.54 = bf16[2,256,384]{2,1,0:T(8,128)(2,1)} collective-permute-done((bf16[2,256,384]{2,1,0:T(8,128)(2,1)}, bf16[2,256,384]{2,1,0:T(8,128)(2,1)}, u32[]{:S(2)}, u32[]{:S(2)}) %collective-permute-start.54) | collective-permute-done | bytes 393248 | tf_op jit(solution)/shard_map/ppermute | solution.py:286
  562.5 41.3 %collective-permute-done.62 = bf16[2,256,384]{2,1,0:T(8,128)(2,1)S(1)} collective-permute-done((bf16[2,256,384]{2,1,0:T(8,128)(2,1)S(1)}, bf16[2,256,384]{2,1,0:T(8,128)(2,1)S(1)}, u32[]{:S(2)}, u32[]{:S(2)}) %collective-permute-start.62) | collective-permute-done | bytes 393248 | tf_op jit(solution)/shard_map/ppermute | solution.py:286
  622.7 5.8 finish_ffn.1
  (444 shorter events, 240.9 us)
Async XLA Ops:
  16.7 38.7 %all-to-all-start = ((bf16[4,128,1152]{2,1,0:T(8,128)(2,1)}), bf16[4,128,1152]{2,1,0:T(8,128)(2,1)}, u32[]{:S(2)}, u32[]{:S(2)}) async-start(bf16[4,128,1152]{2,1,0:T(8,128)(2,1)} %bitcast.6), calls=%async_computation | async-start | bytes 2359296 | tf_op jit(solution)/shard_map/all_to_all | solution.py:156
  26.3 38.1 %collective-permute-start.1 = (bf16[3,128,2304]{2,1,0:T(8,128)(2,1)}, bf16[3,128,2304]{2,1,0:T(8,128)(2,1)}, u32[]{:S(2)}, u32[]{:S(2)}) collective-permute-start(bf16[3,128,2304]{2,1,0:T(8,128)(2,1)} %get-tuple-element.87), channel_id=1, source_target_pairs={{0,4},{4,0},{1,5},{5,1},{2,6},{6,2},{3,7},{7,3},{8,12},{12,8},{9,1... | collective-permute-start | bytes 5308424 | tf_op jit(solution)/shard_map/ppermute | solution.py:66
  72.8 52.9 %all-to-all-start.1 = ((bf16[4,128,1024]{2,1,0:T(8,128)(2,1)}), bf16[4,128,1024]{2,1,0:T(8,128)(2,1)}, u32[]{:S(2)}, u32[]{:S(2)}) async-start(bf16[4,128,1024]{2,1,0:T(8,128)(2,1)} %bitcast.14), calls=%async_computation.1 | async-start | bytes 2097152 | tf_op jit(solution)/shard_map/all_to_all | solution.py:156
  98.6 38.1 %collective-permute-start.10 = (bf16[1,3,128,768]{3,2,1,0:T(8,128)(2,1)}, bf16[1,3,128,768]{3,2,1,0:T(8,128)(2,1)}, u32[]{:S(2)}, u32[]{:S(2)}) collective-permute-start(bf16[1,3,128,768]{3,2,1,0:T(8,128)(2,1)} %slice.247), channel_id=1, source_target_pairs={{0,16},{16,0},{1,17},{17,1},{2,18},{18,2},{3,19},{19,3},{4,20},{20... | collective-permute-start | bytes 1769480 | tf_op jit(solution)/shard_map/ppermute | solution.py:196
  125.7 47.6 %collective-permute-start.13 = (bf16[512,1024]{1,0:T(8,128)(2,1)}, bf16[512,1024]{1,0:T(8,128)(2,1)S(1)}, u32[]{:S(2)}, u32[]{:S(2)}) collective-permute-start(bf16[512,1024]{1,0:T(8,128)(2,1)} %bitcast.15.in_ref.refs_4_), channel_id=1, source_target_pairs={{0,4},{4,0},{1,5},{5,1},{2,6},{6,2},{3,7},{7,3},{8,12},{12,8},{9,1... | collective-permute-start | bytes 3145736 | tf_op jit(solution)/shard_map/ppermute | solution.py:66
  128.8 45.6 %collective-permute-start.14 = (bf16[512,1024]{1,0:T(8,128)(2,1)}, bf16[512,1024]{1,0:T(8,128)(2,1)}, u32[]{:S(2)}, u32[]{:S(2)}) collective-permute-start(bf16[512,1024]{1,0:T(8,128)(2,1)} %convolution_convert_fusion), channel_id=1, source_target_pairs={{0,4},{4,0},{1,5},{5,1},{2,6},{6,2},{3,7},{7,3},{8,12},{12,8},{9,1... | collective-permute-start | bytes 3145736 | tf_op jit(solution)/shard_map/ppermute | solution.py:66
  132.5 44.4 %collective-permute-start.15 = (bf16[2,3,128,768]{3,2,1,0:T(8,128)(2,1)}, bf16[2,3,128,768]{3,2,1,0:T(8,128)(2,1)S(1)}, u32[]{:S(2)}, u32[]{:S(2)}) collective-permute-start(bf16[2,3,128,768]{3,2,1,0:T(8,128)(2,1)} %core_pair.6.refs_8_), channel_id=1, source_target_pairs={{0,8},{8,0},{1,9},{9,1},{2,10},{10,2},{3,11},{11,3},{4,12},{12,4},... | collective-permute-start | bytes 3538952 | tf_op jit(solution)/shard_map/ppermute | solution.py:193
  134.0 43.0 %collective-permute-start.16 = (bf16[2,3,128,768]{3,2,1,0:T(8,128)(2,1)}, bf16[2,3,128,768]{3,2,1,0:T(8,128)(2,1)S(1)}, u32[]{:S(2)}, u32[]{:S(2)}) collective-permute-start(bf16[2,3,128,768]{3,2,1,0:T(8,128)(2,1)} %core_pair.6.refs_8_), channel_id=1, source_target_pairs={{0,16},{16,0},{1,17},{17,1},{2,18},{18,2},{3,19},{19,3},{4,20},{20... | collective-permute-start | bytes 3538952 | tf_op jit(solution)/shard_map/ppermute | solution.py:193
  136.7 36.7 %collective-permute-start.11 = (bf16[1,3,128,768]{3,2,1,0:T(8,128)(2,1)S(1)}, bf16[1,3,128,768]{3,2,1,0:T(8,128)(2,1)S(1)}, u32[]{:S(2)}, u32[]{:S(2)}) collective-permute-start(bf16[1,3,128,768]{3,2,1,0:T(8,128)(2,1)S(1)} %slice.248), channel_id=1, source_target_pairs={{0,8},{8,0},{1,9},{9,1},{2,10},{10,2},{3,11},{11,3},{4,12},{12,4},... | collective-permute-start | bytes 1769480 | tf_op jit(solution)/shard_map/ppermute | solution.py:197
  186.7 42.2 %collective-permute-start.24 = (bf16[2,3,128,768]{3,2,1,0:T(8,128)(2,1)}, bf16[2,3,128,768]{3,2,1,0:T(8,128)(2,1)}, u32[]{:S(2)}, u32[]{:S(2)}) collective-permute-start(bf16[2,3,128,768]{3,2,1,0:T(8,128)(2,1)} %core_pair.7.refs_8_), channel_id=1, source_target_pairs={{0,8},{8,0},{1,9},{9,1},{2,10},{10,2},{3,11},{11,3},{4,12},{12,4},... | collective-permute-start | bytes 3538952 | tf_op jit(solution)/shard_map/ppermute | solution.py:193
  187.3 41.7 %collective-permute-start.25 = (bf16[2,3,128,768]{3,2,1,0:T(8,128)(2,1)}, bf16[2,3,128,768]{3,2,1,0:T(8,128)(2,1)}, u32[]{:S(2)}, u32[]{:S(2)}) collective-permute-start(bf16[2,3,128,768]{3,2,1,0:T(8,128)(2,1)} %core_pair.7.refs_8_), channel_id=1, source_target_pairs={{0,16},{16,0},{1,17},{17,1},{2,18},{18,2},{3,19},{19,3},{4,20},{20... | collective-permute-start | bytes 3538952 | tf_op jit(solution)/shard_map/ppermute | solution.py:193
  252.7 68.2 %collective-permute-start.27 = (bf16[3,256,768]{2,1,0:T(8,128)(2,1)}, bf16[3,256,768]{2,1,0:T(8,128)(2,1)}, u32[]{:S(2)}, u32[]{:S(2)}) collective-permute-start(bf16[3,256,768]{2,1,0:T(8,128)(2,1)} %get-tuple-element.111), channel_id=1, source_target_pairs={{0,16},{16,0},{1,17},{17,1},{2,18},{18,2},{3,19},{19,3},{4,20},{20... | collective-permute-start | bytes 3538952 | tf_op jit(solution)/shard_map/ppermute | solution.py:255
  257.7 66.0 %collective-permute-start.26 = (bf16[3,256,768]{2,1,0:T(8,128)(2,1)}, bf16[3,256,768]{2,1,0:T(8,128)(2,1)}, u32[]{:S(2)}, u32[]{:S(2)}) collective-permute-start(bf16[3,256,768]{2,1,0:T(8,128)(2,1)} %get-tuple-element.109), channel_id=1, source_target_pairs={{0,8},{8,0},{1,9},{9,1},{2,10},{10,2},{3,11},{11,3},{4,12},{12,4},... | collective-permute-start | bytes 3538952 | tf_op jit(solution)/shard_map/ppermute | solution.py:254
  260.2 74.8 %collective-permute-start.23 = (bf16[3,128,768]{2,1,0:T(8,128)(2,1)}, bf16[3,128,768]{2,1,0:T(8,128)(2,1)S(1)}, u32[]{:S(2)}, u32[]{:S(2)}) collective-permute-start(bf16[3,128,768]{2,1,0:T(8,128)(2,1)} %add_convert_fusion.14), channel_id=1, source_target_pairs={{0,8},{8,0},{1,9},{9,1},{2,10},{10,2},{3,11},{11,3},{4,12},{12,4},... | collective-permute-start | bytes 1769480 | tf_op jit(solution)/shard_map/ppermute | solution.py:267
  291.7 44.2 %collective-permute-start.21 = (bf16[3,128,768]{2,1,0:T(8,128)(2,1)}, bf16[3,128,768]{2,1,0:T(8,128)(2,1)}, u32[]{:S(2)}, u32[]{:S(2)}) collective-permute-start(bf16[3,128,768]{2,1,0:T(8,128)(2,1)} %add_convert_fusion.15), channel_id=1, source_target_pairs={{0,16},{16,0},{1,17},{17,1},{2,18},{18,2},{3,19},{19,3},{4,20},{20... | collective-permute-start | bytes 1769480 | tf_op jit(solution)/shard_map/ppermute | solution.py:267
  335.9 38.2 %collective-permute-start.33 = (bf16[3,256,768]{2,1,0:T(8,128)(2,1)}, bf16[3,256,768]{2,1,0:T(8,128)(2,1)}, u32[]{:S(2)}, u32[]{:S(2)}) collective-permute-start(bf16[3,256,768]{2,1,0:T(8,128)(2,1)} %get-tuple-element.114), channel_id=1, source_target_pairs={{0,8},{8,0},{1,9},{9,1},{2,10},{10,2},{3,11},{11,3},{4,12},{12,4},... | collective-permute-start | bytes 3538952 | tf_op jit(solution)/shard_map/ppermute | solution.py:254
  341.0 89.5 %collective-permute-start.37 = (bf16[512,1024]{1,0:T(8,128)(2,1)}, bf16[512,1024]{1,0:T(8,128)(2,1)}, u32[]{:S(2)}, u32[]{:S(2)}) collective-permute-start(bf16[512,1024]{1,0:T(8,128)(2,1)} %add_convert_fusion.8), channel_id=1, source_target_pairs={{0,4},{4,0},{1,5},{5,1},{2,6},{6,2},{3,7},{7,3},{8,12},{12,8},{9,1... | collective-permute-start | bytes 3145736 | tf_op jit(solution)/shard_map/ppermute | solution.py:66
  366.9 53.3 %collective-permute-start.40 = (bf16[3,256,768]{2,1,0:T(8,128)(2,1)}, bf16[3,256,768]{2,1,0:T(8,128)(2,1)}, u32[]{:S(2)}, u32[]{:S(2)}) collective-permute-start(bf16[3,256,768]{2,1,0:T(8,128)(2,1)} %combine.6), channel_id=1, source_target_pairs={{0,1},{3,2},{4,5},{7,6},{8,9},{11,10},{12,13},{15,14},{16,17},{19,... | collective-permute-start | bytes 3538952 | tf_op jit(solution)/shard_map/ppermute | solution.py:277
  374.0 37.3 %collective-permute-start.42 = (bf16[3,128,768]{2,1,0:T(8,128)(2,1)}, bf16[3,128,768]{2,1,0:T(8,128)(2,1)S(1)}, u32[]{:S(2)}, u32[]{:S(2)}) collective-permute-start(bf16[3,128,768]{2,1,0:T(8,128)(2,1)} %add_convert_fusion.10), channel_id=1, source_target_pairs={{0,8},{8,0},{1,9},{9,1},{2,10},{10,2},{3,11},{11,3},{4,12},{12,4},... | collective-permute-start | bytes 1769480 | tf_op jit(solution)/shard_map/ppermute | solution.py:267
  411.4 38.8 %collective-permute-start.39 = (bf16[3,256,768]{2,1,0:T(8,128)(2,1)}, bf16[3,256,768]{2,1,0:T(8,128)(2,1)}, u32[]{:S(2)}, u32[]{:S(2)}) collective-permute-start(bf16[3,256,768]{2,1,0:T(8,128)(2,1)} %add_convert_fusion.5), channel_id=1, source_target_pairs={{1,2},{2,1},{5,6},{6,5},{9,10},{10,9},{13,14},{14,13},{17,18},{18,... | collective-permute-start | bytes 3538952 | tf_op jit(solution)/shard_map/ppermute | solution.py:282
  424.2 54.8 %collective-permute-start.44 = (bf16[3,256,768]{2,1,0:T(8,128)(2,1)}, bf16[3,256,768]{2,1,0:T(8,128)(2,1)}, u32[]{:S(2)}, u32[]{:S(2)}) collective-permute-start(bf16[3,256,768]{2,1,0:T(8,128)(2,1)} %add_convert_fusion.3), channel_id=1, source_target_pairs={{1,2},{2,1},{5,6},{6,5},{9,10},{10,9},{13,14},{14,13},{17,18},{18,... | collective-permute-start | bytes 3538952 | tf_op jit(solution)/shard_map/ppermute | solution.py:282
  435.0 72.3 %all-to-all-start.2 = ((bf16[4,128,1024]{2,1,0:T(8,128)(2,1)}), bf16[4,128,1024]{2,1,0:T(8,128)(2,1)}, u32[]{:S(2)}, u32[]{:S(2)}) async-start(bf16[4,128,1024]{2,1,0:T(8,128)(2,1)} %bitcast.74), calls=%async_computation.2 | async-start | bytes 2097152 | tf_op jit(solution)/shard_map/all_to_all | solution.py:161
  442.9 39.3 %collective-permute-start.52 = (bf16[2,256,384]{2,1,0:T(8,128)(2,1)}, bf16[2,256,384]{2,1,0:T(8,128)(2,1)S(1)}, u32[]{:S(2)}, u32[]{:S(2)}) collective-permute-start(bf16[2,256,384]{2,1,0:T(8,128)(2,1)} %combine.8), channel_id=1, source_target_pairs={{0,1},{3,2},{4,5},{7,6},{8,9},{11,10},{12,13},{15,14},{16,17},{19,... | collective-permute-start | bytes 1179656 | tf_op jit(solution)/shard_map/ppermute | solution.py:277
  448.4 65.6 %collective-permute-start.45 = (bf16[3,256,768]{2,1,0:T(8,128)(2,1)S(1)}, bf16[3,256,768]{2,1,0:T(8,128)(2,1)}, u32[]{:S(2)}, u32[]{:S(2)}) collective-permute-start(bf16[3,256,768]{2,1,0:T(8,128)(2,1)S(1)} %add_convert_fusion.2), channel_id=1, source_target_pairs={{1,2},{2,1},{5,6},{6,5},{9,10},{10,9},{13,14},{14,13},{17,18},{18,... | collective-permute-start | bytes 3538952 | tf_op jit(solution)/shard_map/ppermute | solution.py:282
  452.7 95.3 %collective-permute-start.64 = (bf16[3,256,768]{2,1,0:T(8,128)(2,1)}, bf16[3,256,768]{2,1,0:T(8,128)(2,1)}, u32[]{:S(2)}, u32[]{:S(2)}) collective-permute-start(bf16[3,256,768]{2,1,0:T(8,128)(2,1)} %add_convert_fusion.4), channel_id=1, source_target_pairs={{1,0},{2,3},{5,4},{6,7},{9,8},{10,11},{13,12},{14,15},{17,16},{18,... | collective-permute-start | bytes 3538952 | tf_op jit(solution)/shard_map/ppermute | solution.py:286
  504.2 102.3 %collective-permute-start.66 = (bf16[3,256,768]{2,1,0:T(8,128)(2,1)S(1)}, bf16[3,256,768]{2,1,0:T(8,128)(2,1)}, u32[]{:S(2)}, u32[]{:S(2)}) collective-permute-start(bf16[3,256,768]{2,1,0:T(8,128)(2,1)S(1)} %add_convert_fusion.1), channel_id=1, source_target_pairs={{1,0},{2,3},{5,4},{6,7},{9,8},{10,11},{13,12},{14,15},{17,16},{18,... | collective-permute-start | bytes 3538952 | tf_op jit(solution)/shard_map/ppermute | solution.py:286
  510.9 51.6 %collective-permute-start.54 = (bf16[2,256,384]{2,1,0:T(8,128)(2,1)}, bf16[2,256,384]{2,1,0:T(8,128)(2,1)}, u32[]{:S(2)}, u32[]{:S(2)}) collective-permute-start(bf16[2,256,384]{2,1,0:T(8,128)(2,1)} %add_convert_fusion.18), channel_id=1, source_target_pairs={{1,0},{2,3},{5,4},{6,7},{9,8},{10,11},{13,12},{14,15},{17,16},{18,... | collective-permute-start | bytes 1179656 | tf_op jit(solution)/shard_map/ppermute | solution.py:286
  524.7 87.5 %all-to-all-start.3 = ((bf16[4,128,1024]{2,1,0:T(8,128)(2,1)}), bf16[4,128,1024]{2,1,0:T(8,128)(2,1)}, u32[]{:S(2)}, u32[]{:S(2)}) async-start(bf16[4,128,1024]{2,1,0:T(8,128)(2,1)} %bitcast.75), calls=%async_computation.3 | async-start | bytes 2097152 | tf_op jit(solution)/shard_map/all_to_all | solution.py:161
  544.7 62.3 %collective-permute-start.68 = (bf16[3,256,768]{2,1,0:T(8,128)(2,1)}, bf16[3,256,768]{2,1,0:T(8,128)(2,1)S(1)}, u32[]{:S(2)}, u32[]{:S(2)}) collective-permute-start(bf16[3,256,768]{2,1,0:T(8,128)(2,1)} %add_convert_fusion), channel_id=1, source_target_pairs={{1,0},{2,3},{5,4},{6,7},{9,8},{10,11},{13,12},{14,15},{17,16},{18,... | collective-permute-start | bytes 3538952 | tf_op jit(solution)/shard_map/ppermute | solution.py:286
  548.1 55.7 %collective-permute-start.62 = (bf16[2,256,384]{2,1,0:T(8,128)(2,1)S(1)}, bf16[2,256,384]{2,1,0:T(8,128)(2,1)S(1)}, u32[]{:S(2)}, u32[]{:S(2)}) collective-permute-start(bf16[2,256,384]{2,1,0:T(8,128)(2,1)S(1)} %add_convert_fusion.16), channel_id=1, source_target_pairs={{1,0},{2,3},{5,4},{6,7},{9,8},{10,11},{13,12},{14,15},{17,16},{18,... | collective-permute-start | bytes 1179656 | tf_op jit(solution)/shard_map/ppermute | solution.py:286
  554.7 55.6 %collective-permute-start.38 = (bf16[2,128,1024]{2,1,0:T(8,128)(2,1)S(1)}, bf16[2,128,1024]{2,1,0:T(8,128)(2,1)S(1)}, u32[]{:S(2)}, u32[]{:S(2)}) collective-permute-start(bf16[2,128,1024]{2,1,0:T(8,128)(2,1)S(1)} %copy-done.72), channel_id=1, source_target_pairs={{0,4},{4,0},{1,5},{5,1},{2,6},{6,2},{3,7},{7,3},{8,12},{12,8},{9,1... | collective-permute-start | bytes 1572872 | tf_op jit(solution)/shard_map/ppermute | solution.py:66
  562.5 60.2 %collective-permute-start.65 = (bf16[3,128,768]{2,1,0:T(8,128)(2,1)}, bf16[3,128,768]{2,1,0:T(8,128)(2,1)S(1)}, u32[]{:S(2)}, u32[]{:S(2)}) collective-permute-start(bf16[3,128,768]{2,1,0:T(8,128)(2,1)} %get-tuple-element.165), channel_id=1, source_target_pairs={{0,4},{4,0},{1,5},{5,1},{2,6},{6,2},{3,7},{7,3},{8,12},{12,8},{9,1... | collective-permute-start | bytes 1769480 | tf_op jit(solution)/shard_map/ppermute | solution.py:66
  (134 other events, 1796.7 us)

commit v3 on v2

--- a/solution.py
+++ b/solution.py
@@ -876,7 +876,10 @@
     gathers = []
     for k, count in enumerate(CHUNKS):
         own_part = core_pair(ffn_mine, ffn_other, tile, sum(CHUNKS[:k]), count)
-        before = (gathers[-1] if k else attn_gather).first
+        if k == 0:
+            before = attn_gather.first
+        else:
+            before = gathers[0].first if k == 1 else gathers[-1].second
         gathers.append(Gather(own_part, *before))
 
     high, low = positions // 128, positions % 128
@@ -912,7 +915,7 @@
     cot_t = [turn(a, model) for a in cot]
 
     mixed = attention_call(
-        after(flip, *gathers[0].first), size, heads, x, cosines, sines, q_gain2, k_gain2, attn_blocks
+        flip, size, heads, x, cosines, sines, q_gain2, k_gain2, attn_blocks
     )
     out_w = jnp.concatenate(
         [
@@ -922,9 +925,9 @@
         ],
         axis=0,
     )
-    mixed = [after(mixed[0], *gathers[0].second, cot[1]), *mixed[1:]]
+    mixed = [after(mixed[0], *gathers[0].first), *mixed[1:]]
     residual = tok + group_scatter([[dot(m, out_w, NT) for m in mixed]])
-    residual = after(residual, *gathers[1].first)
+    residual = after(residual, *gathers[0].second)
     mid_scale = rms_scale(residual)
     mid_hat = residual * mid_scale
     mid = group_gather((mid_hat * ffn_gain_r).astype(bf16))
@@ -943,6 +946,8 @@
             waits = gathers[2].first
         else:
             waits = step_all(0)
+        if k:
+            waits = waits + [mid_parts[-1][0]]
         parts = ffn_call(
             tile,
             CHUNKS[k],
@@ -988,16 +993,19 @@
         gain_parts.append(parts[members])
         sums.append(Reduction(parts[members + 1 :]))
     head_gains = sum(gain_parts)
-    d_in_parts[-1] = [after(d_in_parts[-1][0], *step_all(1, 2)), *d_in_parts[-1][1:]]
+    waits = step_all(1, 2)
     out_parts[0] = [after(out_parts[0][0], d_in_parts[0][0]), *out_parts[0][1:]]
+    d_in = group_scatter(d_in_parts)
+    attn_gain_part = jnp.sum(d_in * in_hat, axis=0)
+    input_grad = d_resid + norm_back(d_in, in_hat, in_scale, attn_gain_r)
+    input_grad = input_grad.astype(bf16).reshape(quarters, size, model)
+    if square():
+        sums[-1].state[2] = after(sums[-1].state[2], input_grad, *waits)
+    input_grad = from_sequence(input_grad)
     while any(r.step < 5 for r in sums):
         step_all(*[i for i, r in enumerate(sums) if r.step < 5])
     ffn_sums = [r.state for r in sums[:chunks]]
     heads_sums = [r.state for r in sums[chunks:]]
-    d_in = group_scatter(d_in_parts)
-    attn_gain_part = jnp.sum(d_in * in_hat, axis=0)
-    input_grad = d_resid + norm_back(d_in, in_hat, in_scale, attn_gain_r)
-    input_grad = from_sequence(input_grad.astype(bf16).reshape(quarters, size, model))
 
     output = (residual + group_scatter(out_parts)).astype(bf16)
     output = from_sequence(output.reshape(quarters, size, model))
@@ -1016,6 +1024,8 @@
 
     if members == 2:
         ffn_grads = finish_ffn_call(ffn_sums)
+        mine, other = heads_sums[-1]
+        heads_sums[-1] = (after(mine, ffn_grads[0]), other)
         q_grad, k_grad, v_grad, out_grad = finish_heads_call(heads_sums)
     else:
         heads_all = [every_member(h) for h in heads_sums]

time: 637 us -> 600 us (0.942)
  waiting for transfers between devices: 169 us -> 151 us
  starting transfers between devices: 118 us -> 106 us
    ppermute x4, waiting for transfers between devices: 38.4 us -> 7.33 us  [__init__(): lax.ppermute(by_o[1:], 'x', SWAP)]
    ppermute x5, waiting for transfers between devices: 49.1 us -> 22.1 us  [advance(): self.state = (here, lax.ppermute(here, 'z', ((1, 0), (2, 3))))]
    ppermute x5, waiting for transfers between devices: 1.6 us -> 14 us  [sum_all(): terms = terms + lax.ppermute(terms, axis, perm)]
    ppermute x5, waiting for transfers between devices: 1.52 us -> 13.2 us  [advance(): come = lax.ppermute(here, 'z', ((0, 1), (3, 2))) if on_line else None]
    ppermute x4, waiting for transfers between devices: 33.8 us -> 44 us  [__init__(): lax.ppermute(by_x[:1], 'o', SWAP)]
    all_to_all x2, starting transfers between devices: 24.4 us -> 14.6 us  [from_sequence(): every = lax.all_to_all(rows, 'z', 0, 0, tiled=True)]
    ppermute x8, waiting for transfers between devices: 30.2 us -> 38.7 us  [__init__(): self.first = [lax.ppermute(own, 'x', SWAP), lax.ppermute(own, 'o', SWAP)]]
    unnamed x174 -> x168, local copies, waits for them, and re-layouts: 16.9 us -> 15 us
  transfers between devices with their start and end apart: 79 -> 79, of which waited for: 18 -> 20; matrix products, arithmetic and copies ran while one was open for 18% -> 18% of each run, Pallas kernels for 32% -> 34%
where the time goes in v3:
time: 600 us; the launch traced here: 593 us
  Pallas kernels  209 us (35%)
  waiting for transfers between devices  151 us (25%)
  starting transfers between devices  106 us (18%)
  other arithmetic  75.6 us (13%)
  local copies, waits for them, and re-layouts  40.7 us (7%)
  matrix products  9.32 us (2%)
    pallas_call x3, Pallas kernels, ffn_call(): pl.pallas_call(functools.partial(ffn_kernel, members, len(weights), slots...  72.2 us
    pallas_call x2, Pallas kernels, attention_back_call(): pl.pallas_call(functools.partial(attention_back_kernel, members, len(weig...  48.1 us
    ppermute x4, waiting for transfers between devices, __init__(): lax.ppermute(by_x[:1], 'o', SWAP)  44 us
    ppermute x8, waiting for transfers between devices, __init__(): self.first = [lax.ppermute(own, 'x', SWAP), lax.ppermute(own, 'o', SWAP)]  38.7 us
    convert_element_type x20, other arithmetic, add_up(): functools.reduce(jnp.add, [t.astype(f32) for t in terms]).astype(bf16)  30.9 us
    ppermute x5, starting transfers between devices, advance(): come = lax.ppermute(here, 'z', ((0, 1), (3, 2))) if on_line else None  22.6 us
    ppermute x5, waiting for transfers between devices, advance(): self.state = (here, lax.ppermute(here, 'z', ((1, 0), (2, 3))))  22.1 us
    pallas_call x1, Pallas kernels, attention_call(): pl.pallas_call(functools.partial(attention_kernel, members, len(weights),...  19 us
  transfers between devices with their start and end apart: 79, of which 20 were waited for; matrix products, arithmetic and copies ran while one was open for 18% of the time, Pallas kernels for 34%

profile of v3, /device:TPU:0, one launch (start us, length us, event | category | flops | bytes accessed | tf_op | source)
XLA Modules:
  0.0 592.9 jit_solution(7111851566040001162)
XLA Ops:
  16.7 6.3 %all-to-all-start = ((bf16[4,128,1152]{2,1,0:T(8,128)(2,1)}), bf16[4,128,1152]{2,1,0:T(8,128)(2,1)}, u32[]{:S(2)}, u32[]{:S(2)}) async-start(bf16[4,128,1152]{2,1,0:T(8,128)(2,1)} %bitcast.6), calls=%async_computation | async-start | bytes 2359296 | tf_op jit(solution)/shard_map/all_to_all | solution.py:156
  33.2 15.5 %collective-permute-done.3.refs_7_.refs_15_ = bf16[2,6,128,256]{3,2,1,0:T(8,128)(2,1)S(1)} collective-permute-done((bf16[2,6,128,256]{3,2,1,0:T(8,128)(2,1)}, bf16[2,6,128,256]{3,2,1,0:T(8,128)(2,1)S(1)}, u32[]{:S(2)}, u32[]{:S(2)}) %collective-permute-start.3) | collective-permute-done | bytes 786464 | tf_op jit(solution)/shard_map/ppermute | solution.py:193
  76.1 5.4 all-to-all-start.1
  87.8 19.0 %attention.1 = (bf16[512,512]{1,0:T(8,128)(2,1)S(1)}, bf16[512,512]{1,0:T(8,128)(2,1)S(1)}) custom-call(s32[2]{0:T(128)S(1)} %copy-done.26, bf16[512,1152]{1,0:T(8,128)(2,1)} %pad_maximum_fusion.refs_0_.in_ref, bf16[512,1152]{1,0:T(8,128)(2,1)} %collective-permute-done.1.refs_1_.in_ref, f32[1024,128]{1,0:T(8,128)S(1)} %copy.58.refs_2_.refs_8_, ...), custom_call_target="tpu_custom_call" | custom-call | flops 134217728 | bytes 262144 | tf_op jit(solution)/shard_map/attention/pallas_call | solution.py:768
  125.9 3.6 collective-permute-done.12.refs_12_
  130.9 23.1 %collective-permute-done.13.refs_9_ = bf16[2,3,128,768]{3,2,1,0:T(8,128)(2,1)} collective-permute-done((bf16[2,3,128,768]{3,2,1,0:T(8,128)(2,1)}, bf16[2,3,128,768]{3,2,1,0:T(8,128)(2,1)}, u32[]{:S(2)}, u32[]{:S(2)}) %collective-permute-start.13) | collective-permute-done | bytes 1179680 | tf_op jit(solution)/shard_map/ppermute | solution.py:193
  161.4 8.4 %collective-permute-done.14.refs_11_ = bf16[1,3,128,768]{3,2,1,0:T(8,128)(2,1)S(1)} collective-permute-done((bf16[1,3,128,768]{3,2,1,0:T(8,128)(2,1)S(1)}, bf16[1,3,128,768]{3,2,1,0:T(8,128)(2,1)S(1)}, u32[]{:S(2)}, u32[]{:S(2)}) %collective-permute-start.14) | collective-permute-done | bytes 589856 | tf_op jit(solution)/shard_map/ppermute | solution.py:196
  183.4 23.9 %ffn.3 = (bf16[512,1024]{1,0:T(8,128)(2,1)}, bf16[512,1024]{1,0:T(8,128)(2,1)}, bf16[512,1024]{1,0:T(8,128)(2,1)}, bf16[512,1024]{1,0:T(8,128)(2,1)}, bf16[3,256...) custom-call(bf16[512,1024]{1,0:T(8,128)(2,1)} %multiply_convert_fusi, ...), custom_call_target="tpu_custom_call" | custom-call | flops 452984832 | bytes 688128 | tf_op jit(solution)/shard_map/ffn/pallas_call | solution.py:551
  209.4 24.2 %ffn.4 = (bf16[512,1024]{1,0:T(8,128)(2,1)}, bf16[512,1024]{1,0:T(8,128)(2,1)}, bf16[512,1024]{1,0:T(8,128)(2,1)}, bf16[512,1024]{1,0:T(8,128)(2,1)}, bf16[3,256...) custom-call(bf16[512,1024]{1,0:T(8,128)(2,1)} %multiply_convert_fusi, ...), custom_call_target="tpu_custom_call" | custom-call | flops 452984832 | bytes 688128 | tf_op jit(solution)/shard_map/ffn/pallas_call | solution.py:551
  241.5 30.9 %collective-permute-done.31.refs_11_ = bf16[1,3,128,768]{3,2,1,0:T(8,128)(2,1)} collective-permute-done((bf16[1,3,128,768]{3,2,1,0:T(8,128)(2,1)S(1)}, bf16[1,3,128,768]{3,2,1,0:T(8,128)(2,1)}, u32[]{:S(2)}, u32[]{:S(2)}) %collective-permute-start.31) | collective-permute-done | bytes 589856 | tf_op jit(solution)/shard_map/ppermute | solution.py:196
  273.9 24.1 %ffn.5 = (bf16[512,1024]{1,0:T(8,128)(2,1)}, bf16[512,1024]{1,0:T(8,128)(2,1)}, bf16[512,1024]{1,0:T(8,128)(2,1)}, bf16[512,1024]{1,0:T(8,128)(2,1)}, bf16[3,256...) custom-call(bf16[512,1024]{1,0:T(8,128)(2,1)} %multiply_convert_fusi, ...), custom_call_target="tpu_custom_call" | custom-call | flops 452984832 | bytes 688128 | tf_op jit(solution)/shard_map/ffn/pallas_call | solution.py:551
  298.1 3.6 add_convert_fusion.9
  310.5 3.5 add_convert_fusion.8
  317.0 3.9 combine.5
  322.0 5.0 collective-permute-start.28
  326.9 4.0 combine.6
  333.9 4.3 fusion.21
  346.5 5.1 collective-permute-start.40
  364.6 24.0 %attention_back.2 = (bf16[512,1024]{1,0:T(8,128)(2,1)}, bf16[512,1024]{1,0:T(8,128)(2,1)}, f32[2,128]{1,0:T(2,128)}, bf16[2,256,384]{2,1,0:T(8,128)(2,1)}, bf16[...) custom-call(s32[2]{0:T(128)} %pad_add_fusion.at_ref, ...), custom_call_target="tpu_custom_call" | custom-call | flops 117440512 | bytes 262144 | tf_op jit(solution)/shard_map/attention_back/pallas_call | solution.py:799
  392.0 4.0 combine.7
  413.4 4.4 all-to-all-start.2
  420.6 3.9 collective-permute-start.50
  433.0 24.0 %attention_back.3 = (bf16[512,1024]{1,0:T(8,128)(2,1)}, bf16[512,1024]{1,0:T(8,128)(2,1)}, f32[2,128]{1,0:T(2,128)}, bf16[2,256,384]{2,1,0:T(8,128)(2,1)}, bf16[...) custom-call(s32[2]{0:T(128)} %pad_add_fusion.at_ref, ...), custom_call_target="tpu_custom_call" | custom-call | flops 117440512 | bytes 262144 | tf_op jit(solution)/shard_map/attention_back/pallas_call | solution.py:799
  464.9 5.7 collective-permute-done.58.come_b
  481.2 4.0 fusion.9
  496.9 10.3 %all-to-all-start.3 = ((bf16[4,128,1024]{2,1,0:T(8,128)(2,1)}), bf16[4,128,1024]{2,1,0:T(8,128)(2,1)}, u32[]{:S(2)}, u32[]{:S(2)}) async-start(bf16[4,128,1024]{2,1,0:T(8,128)(2,1)} %bitcast.34), calls=%async_computation.3 | async-start | bytes 2097152 | tf_op jit(solution)/shard_map/all_to_all | solution.py:161
  510.6 5.6 collective-permute-start.60
  520.1 12.9 %collective-permute-done.60 = bf16[2,256,384]{2,1,0:T(8,128)(2,1)S(1)} collective-permute-done((bf16[2,256,384]{2,1,0:T(8,128)(2,1)}, bf16[2,256,384]{2,1,0:T(8,128)(2,1)S(1)}, u32[]{:S(2)}, u32[]{:S(2)}) %collective-permute-start.60) | collective-permute-done | bytes 393248 | tf_op jit(solution)/shard_map/ppermute | solution.py:277
  533.9 22.0 %collective-permute-done.67 = bf16[3,256,768]{2,1,0:T(8,128)(2,1)} collective-permute-done((bf16[3,256,768]{2,1,0:T(8,128)(2,1)S(1)}, bf16[3,256,768]{2,1,0:T(8,128)(2,1)}, u32[]{:S(2)}, u32[]{:S(2)}) %collective-permute-start.67) | collective-permute-done | bytes 1179680 | tf_op jit(solution)/shard_map/ppermute | solution.py:286
  561.0 9.1 %collective-permute-done.73 = f32[2176]{0:T(1024)S(1)} collective-permute-done((f32[2176]{0:T(1024)S(1)}, f32[2176]{0:T(1024)S(1)}, u32[]{:S(2)}, u32[]{:S(2)}) %collective-permute-start.73) | collective-permute-done | bytes 8736 | tf_op jit(solution)/shard_map/ppermute | solution.py:323
  571.0 3.8 collective-permute-done.74
  581.8 5.6 finish_ffn.1
  (438 shorter events, 237.8 us)
Async XLA Ops:
  16.7 37.4 %all-to-all-start = ((bf16[4,128,1152]{2,1,0:T(8,128)(2,1)}), bf16[4,128,1152]{2,1,0:T(8,128)(2,1)}, u32[]{:S(2)}, u32[]{:S(2)}) async-start(bf16[4,128,1152]{2,1,0:T(8,128)(2,1)} %bitcast.6), calls=%async_computation | async-start | bytes 2359296 | tf_op jit(solution)/shard_map/all_to_all | solution.py:156
  26.3 41.6 %collective-permute-start.7 = (bf16[3,128,2304]{2,1,0:T(8,128)(2,1)}, bf16[3,128,2304]{2,1,0:T(8,128)(2,1)}, u32[]{:S(2)}, u32[]{:S(2)}) collective-permute-start(bf16[3,128,2304]{2,1,0:T(8,128)(2,1)} %get-tuple-element.90), channel_id=1, source_target_pairs={{0,4},{4,0},{1,5},{5,1},{2,6},{6,2},{3,7},{7,3},{8,12},{12,8},{9,1... | collective-permute-start | bytes 5308424 | tf_op jit(solution)/shard_map/ppermute | solution.py:66
  71.3 36.3 %collective-permute-start.8 = (bf16[2,3,128,768]{3,2,1,0:T(8,128)(2,1)}, bf16[2,3,128,768]{3,2,1,0:T(8,128)(2,1)}, u32[]{:S(2)}, u32[]{:S(2)}) collective-permute-start(bf16[2,3,128,768]{3,2,1,0:T(8,128)(2,1)} %core_pair.5.refs_8_), channel_id=1, source_target_pairs={{0,8},{8,0},{1,9},{9,1},{2,10},{10,2},{3,11},{11,3},{4,12},{12,4},... | collective-permute-start | bytes 3538952 | tf_op jit(solution)/shard_map/ppermute | solution.py:193
  72.8 38.2 %collective-permute-start.9 = (bf16[2,3,128,768]{3,2,1,0:T(8,128)(2,1)}, bf16[2,3,128,768]{3,2,1,0:T(8,128)(2,1)}, u32[]{:S(2)}, u32[]{:S(2)}) collective-permute-start(bf16[2,3,128,768]{3,2,1,0:T(8,128)(2,1)} %core_pair.5.refs_8_), channel_id=1, source_target_pairs={{0,16},{16,0},{1,17},{17,1},{2,18},{18,2},{3,19},{19,3},{4,20},{20... | collective-permute-start | bytes 3538952 | tf_op jit(solution)/shard_map/ppermute | solution.py:193
  76.1 42.9 %all-to-all-start.1 = ((bf16[4,128,1024]{2,1,0:T(8,128)(2,1)}), bf16[4,128,1024]{2,1,0:T(8,128)(2,1)}, u32[]{:S(2)}, u32[]{:S(2)}) async-start(bf16[4,128,1024]{2,1,0:T(8,128)(2,1)} %bitcast.30), calls=%async_computation.1 | async-start | bytes 2097152 | tf_op jit(solution)/shard_map/all_to_all | solution.py:156
  116.9 37.1 %collective-permute-start.13 = (bf16[2,3,128,768]{3,2,1,0:T(8,128)(2,1)}, bf16[2,3,128,768]{3,2,1,0:T(8,128)(2,1)}, u32[]{:S(2)}, u32[]{:S(2)}) collective-permute-start(bf16[2,3,128,768]{3,2,1,0:T(8,128)(2,1)} %core_pair.6.refs_8_), channel_id=1, source_target_pairs={{0,8},{8,0},{1,9},{9,1},{2,10},{10,2},{3,11},{11,3},{4,12},{12,4},... | collective-permute-start | bytes 3538952 | tf_op jit(solution)/shard_map/ppermute | solution.py:193
  118.5 37.2 %collective-permute-start.15 = (bf16[2,3,128,768]{3,2,1,0:T(8,128)(2,1)}, bf16[2,3,128,768]{3,2,1,0:T(8,128)(2,1)}, u32[]{:S(2)}, u32[]{:S(2)}) collective-permute-start(bf16[2,3,128,768]{3,2,1,0:T(8,128)(2,1)} %core_pair.6.refs_8_), channel_id=1, source_target_pairs={{0,16},{16,0},{1,17},{17,1},{2,18},{18,2},{3,19},{19,3},{4,20},{20... | collective-permute-start | bytes 3538952 | tf_op jit(solution)/shard_map/ppermute | solution.py:193
  119.9 58.9 %collective-permute-start.19 = (bf16[512,1024]{1,0:T(8,128)(2,1)}, bf16[512,1024]{1,0:T(8,128)(2,1)}, u32[]{:S(2)}, u32[]{:S(2)}) collective-permute-start(bf16[512,1024]{1,0:T(8,128)(2,1)} %bitcast.31.in_ref.refs_4_), channel_id=1, source_target_pairs={{0,4},{4,0},{1,5},{5,1},{2,6},{6,2},{3,7},{7,3},{8,12},{12,8},{9,1... | collective-permute-start | bytes 3145736 | tf_op jit(solution)/shard_map/ppermute | solution.py:66
  130.9 50.2 %collective-permute-start.17 = (bf16[512,1024]{1,0:T(8,128)(2,1)}, bf16[512,1024]{1,0:T(8,128)(2,1)}, u32[]{:S(2)}, u32[]{:S(2)}) collective-permute-start(bf16[512,1024]{1,0:T(8,128)(2,1)} %multiply_convert_fusion.in_ref.refs_0_), channel_id=1, source_target_pairs={{0,4},{4,0},{1,5},{5,1},{2,6},{6,2},{3,7},{7,3},{8,12},{12,8},{9,1... | collective-permute-start | bytes 3145736 | tf_op jit(solution)/shard_map/ppermute | solution.py:66
  172.3 37.1 %collective-permute-start.24 = (bf16[2,3,128,768]{3,2,1,0:T(8,128)(2,1)}, bf16[2,3,128,768]{3,2,1,0:T(8,128)(2,1)S(1)}, u32[]{:S(2)}, u32[]{:S(2)}) collective-permute-start(bf16[2,3,128,768]{3,2,1,0:T(8,128)(2,1)} %core_pair.7.refs_8_), channel_id=1, source_target_pairs={{0,8},{8,0},{1,9},{9,1},{2,10},{10,2},{3,11},{11,3},{4,12},{12,4},... | collective-permute-start | bytes 3538952 | tf_op jit(solution)/shard_map/ppermute | solution.py:193
  172.9 36.5 %collective-permute-start.25 = (bf16[2,3,128,768]{3,2,1,0:T(8,128)(2,1)}, bf16[2,3,128,768]{3,2,1,0:T(8,128)(2,1)}, u32[]{:S(2)}, u32[]{:S(2)}) collective-permute-start(bf16[2,3,128,768]{3,2,1,0:T(8,128)(2,1)} %core_pair.7.refs_8_), channel_id=1, source_target_pairs={{0,16},{16,0},{1,17},{17,1},{2,18},{18,2},{3,19},{19,3},{4,20},{20... | collective-permute-start | bytes 3538952 | tf_op jit(solution)/shard_map/ppermute | solution.py:193
  233.6 68.2 %collective-permute-start.27 = (bf16[3,256,768]{2,1,0:T(8,128)(2,1)}, bf16[3,256,768]{2,1,0:T(8,128)(2,1)}, u32[]{:S(2)}, u32[]{:S(2)}) collective-permute-start(bf16[3,256,768]{2,1,0:T(8,128)(2,1)} %get-tuple-element.111), channel_id=1, source_target_pairs={{0,16},{16,0},{1,17},{17,1},{2,18},{18,2},{3,19},{19,3},{4,20},{20... | collective-permute-start | bytes 3538952 | tf_op jit(solution)/shard_map/ppermute | solution.py:255
  235.2 37.2 %collective-permute-start.31 = (bf16[1,3,128,768]{3,2,1,0:T(8,128)(2,1)S(1)}, bf16[1,3,128,768]{3,2,1,0:T(8,128)(2,1)}, u32[]{:S(2)}, u32[]{:S(2)}) collective-permute-start(bf16[1,3,128,768]{3,2,1,0:T(8,128)(2,1)S(1)} %slice.271), channel_id=1, source_target_pairs={{0,16},{16,0},{1,17},{17,1},{2,18},{18,2},{3,19},{19,3},{4,20},{20... | collective-permute-start | bytes 1769480 | tf_op jit(solution)/shard_map/ppermute | solution.py:196
  236.9 37.1 %collective-permute-start.32 = (bf16[1,3,128,768]{3,2,1,0:T(8,128)(2,1)S(1)}, bf16[1,3,128,768]{3,2,1,0:T(8,128)(2,1)}, u32[]{:S(2)}, u32[]{:S(2)}) collective-permute-start(bf16[1,3,128,768]{3,2,1,0:T(8,128)(2,1)S(1)} %slice.272), channel_id=1, source_target_pairs={{0,8},{8,0},{1,9},{9,1},{2,10},{10,2},{3,11},{11,3},{4,12},{12,4},... | collective-permute-start | bytes 1769480 | tf_op jit(solution)/shard_map/ppermute | solution.py:197
  237.5 66.9 %collective-permute-start.26 = (bf16[3,256,768]{2,1,0:T(8,128)(2,1)}, bf16[3,256,768]{2,1,0:T(8,128)(2,1)S(1)}, u32[]{:S(2)}, u32[]{:S(2)}) collective-permute-start(bf16[3,256,768]{2,1,0:T(8,128)(2,1)} %get-tuple-element.109), channel_id=1, source_target_pairs={{0,8},{8,0},{1,9},{9,1},{2,10},{10,2},{3,11},{11,3},{4,12},{12,4},... | collective-permute-start | bytes 3538952 | tf_op jit(solution)/shard_map/ppermute | solution.py:254
  240.0 74.0 %collective-permute-start.23 = (bf16[3,128,768]{2,1,0:T(8,128)(2,1)}, bf16[3,128,768]{2,1,0:T(8,128)(2,1)}, u32[]{:S(2)}, u32[]{:S(2)}) collective-permute-start(bf16[3,128,768]{2,1,0:T(8,128)(2,1)} %add_convert_fusion.14), channel_id=1, source_target_pairs={{0,8},{8,0},{1,9},{9,1},{2,10},{10,2},{3,11},{11,3},{4,12},{12,4},... | collective-permute-start | bytes 1769480 | tf_op jit(solution)/shard_map/ppermute | solution.py:267
  272.4 43.1 %collective-permute-start.21 = (bf16[3,128,768]{2,1,0:T(8,128)(2,1)}, bf16[3,128,768]{2,1,0:T(8,128)(2,1)}, u32[]{:S(2)}, u32[]{:S(2)}) collective-permute-start(bf16[3,128,768]{2,1,0:T(8,128)(2,1)} %add_convert_fusion.15), channel_id=1, source_target_pairs={{0,16},{16,0},{1,17},{17,1},{2,18},{18,2},{3,19},{19,3},{4,20},{20... | collective-permute-start | bytes 1769480 | tf_op jit(solution)/shard_map/ppermute | solution.py:267
  315.5 38.2 %collective-permute-start.33 = (bf16[3,256,768]{2,1,0:T(8,128)(2,1)}, bf16[3,256,768]{2,1,0:T(8,128)(2,1)}, u32[]{:S(2)}, u32[]{:S(2)}) collective-permute-start(bf16[3,256,768]{2,1,0:T(8,128)(2,1)} %get-tuple-element.115), channel_id=1, source_target_pairs={{0,8},{8,0},{1,9},{9,1},{2,10},{10,2},{3,11},{11,3},{4,12},{12,4},... | collective-permute-start | bytes 3538952 | tf_op jit(solution)/shard_map/ppermute | solution.py:254
  320.9 88.8 %collective-permute-start.37 = (bf16[512,1024]{1,0:T(8,128)(2,1)}, bf16[512,1024]{1,0:T(8,128)(2,1)}, u32[]{:S(2)}, u32[]{:S(2)}) collective-permute-start(bf16[512,1024]{1,0:T(8,128)(2,1)} %add_convert_fusion.8), channel_id=1, source_target_pairs={{0,4},{4,0},{1,5},{5,1},{2,6},{6,2},{3,7},{7,3},{8,12},{12,8},{9,1... | collective-permute-start | bytes 3145736 | tf_op jit(solution)/shard_map/ppermute | solution.py:66
  346.5 52.6 %collective-permute-start.40 = (bf16[3,256,768]{2,1,0:T(8,128)(2,1)}, bf16[3,256,768]{2,1,0:T(8,128)(2,1)}, u32[]{:S(2)}, u32[]{:S(2)}) collective-permute-start(bf16[3,256,768]{2,1,0:T(8,128)(2,1)} %combine.6), channel_id=1, source_target_pairs={{0,1},{3,2},{4,5},{7,6},{8,9},{11,10},{12,13},{15,14},{16,17},{19,... | collective-permute-start | bytes 3538952 | tf_op jit(solution)/shard_map/ppermute | solution.py:277
  353.7 36.6 %collective-permute-start.42 = (bf16[3,128,768]{2,1,0:T(8,128)(2,1)}, bf16[3,128,768]{2,1,0:T(8,128)(2,1)}, u32[]{:S(2)}, u32[]{:S(2)}) collective-permute-start(bf16[3,128,768]{2,1,0:T(8,128)(2,1)} %add_convert_fusion.10), channel_id=1, source_target_pairs={{0,8},{8,0},{1,9},{9,1},{2,10},{10,2},{3,11},{11,3},{4,12},{12,4},... | collective-permute-start | bytes 1769480 | tf_op jit(solution)/shard_map/ppermute | solution.py:267
  390.3 38.7 %collective-permute-start.39 = (bf16[3,256,768]{2,1,0:T(8,128)(2,1)S(1)}, bf16[3,256,768]{2,1,0:T(8,128)(2,1)}, u32[]{:S(2)}, u32[]{:S(2)}) collective-permute-start(bf16[3,256,768]{2,1,0:T(8,128)(2,1)S(1)} %add_convert_fusion.5), channel_id=1, source_target_pairs={{1,2},{2,1},{5,6},{6,5},{9,10},{10,9},{13,14},{14,13},{17,18},{18,... | collective-permute-start | bytes 3538952 | tf_op jit(solution)/shard_map/ppermute | solution.py:282
  403.0 57.4 %collective-permute-start.54 = (bf16[3,256,768]{2,1,0:T(8,128)(2,1)}, bf16[3,256,768]{2,1,0:T(8,128)(2,1)}, u32[]{:S(2)}, u32[]{:S(2)}) collective-permute-start(bf16[3,256,768]{2,1,0:T(8,128)(2,1)} %add_convert_fusion.3), channel_id=1, source_target_pairs={{1,2},{2,1},{5,6},{6,5},{9,10},{10,9},{13,14},{14,13},{17,18},{18,... | collective-permute-start | bytes 3538952 | tf_op jit(solution)/shard_map/ppermute | solution.py:282
  413.4 58.8 %all-to-all-start.2 = ((bf16[4,128,1024]{2,1,0:T(8,128)(2,1)}), bf16[4,128,1024]{2,1,0:T(8,128)(2,1)}, u32[]{:S(2)}, u32[]{:S(2)}) async-start(bf16[4,128,1024]{2,1,0:T(8,128)(2,1)} %bitcast.74), calls=%async_computation.2 | async-start | bytes 2097152 | tf_op jit(solution)/shard_map/all_to_all | solution.py:161
  420.6 38.4 %collective-permute-start.50 = (bf16[2,256,384]{2,1,0:T(8,128)(2,1)}, bf16[2,256,384]{2,1,0:T(8,128)(2,1)S(1)}, u32[]{:S(2)}, u32[]{:S(2)}) collective-permute-start(bf16[2,256,384]{2,1,0:T(8,128)(2,1)} %combine.8), channel_id=1, source_target_pairs={{0,1},{3,2},{4,5},{7,6},{8,9},{11,10},{12,13},{15,14},{16,17},{19,... | collective-permute-start | bytes 1179656 | tf_op jit(solution)/shard_map/ppermute | solution.py:277
  427.3 59.3 %collective-permute-start.55 = (bf16[3,256,768]{2,1,0:T(8,128)(2,1)}, bf16[3,256,768]{2,1,0:T(8,128)(2,1)}, u32[]{:S(2)}, u32[]{:S(2)}) collective-permute-start(bf16[3,256,768]{2,1,0:T(8,128)(2,1)} %add_convert_fusion.2), channel_id=1, source_target_pairs={{1,2},{2,1},{5,6},{6,5},{9,10},{10,9},{13,14},{14,13},{17,18},{18,... | collective-permute-start | bytes 3538952 | tf_op jit(solution)/shard_map/ppermute | solution.py:282
  431.6 79.0 %collective-permute-start.63 = (bf16[3,256,768]{2,1,0:T(8,128)(2,1)}, bf16[3,256,768]{2,1,0:T(8,128)(2,1)}, u32[]{:S(2)}, u32[]{:S(2)}) collective-permute-start(bf16[3,256,768]{2,1,0:T(8,128)(2,1)} %add_convert_fusion.4), channel_id=1, source_target_pairs={{1,0},{2,3},{5,4},{6,7},{9,8},{10,11},{13,12},{14,15},{17,16},{18,... | collective-permute-start | bytes 3538952 | tf_op jit(solution)/shard_map/ppermute | solution.py:286
  485.2 48.6 %collective-permute-start.65 = (bf16[3,256,768]{2,1,0:T(8,128)(2,1)}, bf16[3,256,768]{2,1,0:T(8,128)(2,1)}, u32[]{:S(2)}, u32[]{:S(2)}) collective-permute-start(bf16[3,256,768]{2,1,0:T(8,128)(2,1)} %add_convert_fusion.1), channel_id=1, source_target_pairs={{1,0},{2,3},{5,4},{6,7},{9,8},{10,11},{13,12},{14,15},{17,16},{18,... | collective-permute-start | bytes 3538952 | tf_op jit(solution)/shard_map/ppermute | solution.py:286
  490.8 65.1 %collective-permute-start.67 = (bf16[3,256,768]{2,1,0:T(8,128)(2,1)S(1)}, bf16[3,256,768]{2,1,0:T(8,128)(2,1)}, u32[]{:S(2)}, u32[]{:S(2)}) collective-permute-start(bf16[3,256,768]{2,1,0:T(8,128)(2,1)S(1)} %add_convert_fusion), channel_id=1, source_target_pairs={{1,0},{2,3},{5,4},{6,7},{9,8},{10,11},{13,12},{14,15},{17,16},{18,... | collective-permute-start | bytes 3538952 | tf_op jit(solution)/shard_map/ppermute | solution.py:286
  496.9 78.5 %all-to-all-start.3 = ((bf16[4,128,1024]{2,1,0:T(8,128)(2,1)}), bf16[4,128,1024]{2,1,0:T(8,128)(2,1)}, u32[]{:S(2)}, u32[]{:S(2)}) async-start(bf16[4,128,1024]{2,1,0:T(8,128)(2,1)} %bitcast.34), calls=%async_computation.3 | async-start | bytes 2097152 | tf_op jit(solution)/shard_map/all_to_all | solution.py:161
  507.2 70.3 %collective-permute-start.52 = (bf16[2,256,384]{2,1,0:T(8,128)(2,1)}, bf16[2,256,384]{2,1,0:T(8,128)(2,1)}, u32[]{:S(2)}, u32[]{:S(2)}) collective-permute-start(bf16[2,256,384]{2,1,0:T(8,128)(2,1)} %add_convert_fusion.18), channel_id=1, source_target_pairs={{1,0},{2,3},{5,4},{6,7},{9,8},{10,11},{13,12},{14,15},{17,16},{18,... | collective-permute-start | bytes 1179656 | tf_op jit(solution)/shard_map/ppermute | solution.py:286
  518.5 62.2 %collective-permute-start.64 = (bf16[3,128,768]{2,1,0:T(8,128)(2,1)}, bf16[3,128,768]{2,1,0:T(8,128)(2,1)S(1)}, u32[]{:S(2)}, u32[]{:S(2)}) collective-permute-start(bf16[3,128,768]{2,1,0:T(8,128)(2,1)} %get-tuple-element.165), channel_id=1, source_target_pairs={{0,4},{4,0},{1,5},{5,1},{2,6},{6,2},{3,7},{7,3},{8,12},{12,8},{9,1... | collective-permute-start | bytes 1769480 | tf_op jit(solution)/shard_map/ppermute | solution.py:66
  (131 other events, 1625.0 us)

commit v4 on v3

--- a/solution.py
+++ b/solution.py
@@ -943,7 +943,7 @@
         if k == 0:
             waits = gathers[1].second
         elif k == 1:
-            waits = gathers[2].first
+            waits = gathers[2].second
         else:
             waits = step_all(0)
         if k:

time: 600 us -> 590 us (0.983)
  waiting for transfers between devices: 151 us -> 145 us
    ppermute x8, waiting for transfers between devices: 38.7 us -> 22.2 us  [__init__(): self.first = [lax.ppermute(own, 'x', SWAP), lax.ppermute(own, 'o', SWAP)]]
    ppermute x5, waiting for transfers between devices: 0.01 us -> 8.3 us  [advance(): lax.ppermute(go_b, 'x', SWAP)]
    unnamed x168 -> x158, local copies, waits for them, and re-layouts: 15 us -> 14.1 us
  transfers between devices with their start and end apart: 79 -> 79, of which waited for: 20 -> 18; matrix products, arithmetic and copies ran while one was open for 18% -> 18% of each run, Pallas kernels for 34% -> 35%
where the time goes in v4:
time: 590 us; the launch traced here: 583 us
  Pallas kernels  207 us (35%)
  waiting for transfers between devices  145 us (25%)
  starting transfers between devices  104 us (18%)
  other arithmetic  74.7 us (13%)
  local copies, waits for them, and re-layouts  40.7 us (7%)
  matrix products  9.14 us (2%)
    pallas_call x3, Pallas kernels, ffn_call(): pl.pallas_call(functools.partial(ffn_kernel, members, len(weights), slots...  71.8 us
    pallas_call x2, Pallas kernels, attention_back_call(): pl.pallas_call(functools.partial(attention_back_kernel, members, len(weig...  48.2 us
    ppermute x4, waiting for transfers between devices, __init__(): lax.ppermute(by_x[:1], 'o', SWAP)  41.1 us
    convert_element_type x20, other arithmetic, add_up(): functools.reduce(jnp.add, [t.astype(f32) for t in terms]).astype(bf16)  32.2 us
    ppermute x5, starting transfers between devices, advance(): come = lax.ppermute(here, 'z', ((0, 1), (3, 2))) if on_line else None  25.8 us
    ppermute x5, waiting for transfers between devices, advance(): self.state = (here, lax.ppermute(here, 'z', ((1, 0), (2, 3))))  24.7 us
    ppermute x8, waiting for transfers between devices, __init__(): self.first = [lax.ppermute(own, 'x', SWAP), lax.ppermute(own, 'o', SWAP)]  22.2 us
    pallas_call x1, Pallas kernels, attention_call(): pl.pallas_call(functools.partial(attention_kernel, members, len(weights),...  19 us
  transfers between devices with their start and end apart: 79, of which 18 were waited for; matrix products, arithmetic and copies ran while one was open for 18% of the time, Pallas kernels for 35%

profile of v4, /device:TPU:0, one launch (start us, length us, event | category | flops | bytes accessed | tf_op | source)
XLA Modules:
  0.0 583.4 jit_solution(7310863308253361897)
XLA Ops:
  18.2 6.0 %all-to-all-start = ((bf16[4,128,1152]{2,1,0:T(8,128)(2,1)}), bf16[4,128,1152]{2,1,0:T(8,128)(2,1)}, u32[]{:S(2)}, u32[]{:S(2)}) async-start(bf16[4,128,1152]{2,1,0:T(8,128)(2,1)} %bitcast.6), calls=%async_computation | async-start | bytes 2359296 | tf_op jit(solution)/shard_map/all_to_all | solution.py:156
  31.1 15.3 %collective-permute-done.3.refs_7_.refs_15_ = bf16[2,6,128,256]{3,2,1,0:T(8,128)(2,1)S(1)} collective-permute-done((bf16[2,6,128,256]{3,2,1,0:T(8,128)(2,1)}, bf16[2,6,128,256]{3,2,1,0:T(8,128)(2,1)S(1)}, u32[]{:S(2)}, u32[]{:S(2)}) %collective-permute-start.3) | collective-permute-done | bytes 786464 | tf_op jit(solution)/shard_map/ppermute | solution.py:193
  73.2 5.2 all-to-all-start.1
  78.4 6.9 %collective-permute-done.8.refs_9_ = bf16[2,3,128,768]{3,2,1,0:T(8,128)(2,1)} collective-permute-done((bf16[2,3,128,768]{3,2,1,0:T(8,128)(2,1)}, bf16[2,3,128,768]{3,2,1,0:T(8,128)(2,1)}, u32[]{:S(2)}, u32[]{:S(2)}) %collective-permute-start.8) | collective-permute-done | bytes 1179680 | tf_op jit(solution)/shard_map/ppermute | solution.py:193
  93.6 19.0 %attention.1 = (bf16[512,512]{1,0:T(8,128)(2,1)S(1)}, bf16[512,512]{1,0:T(8,128)(2,1)S(1)}) custom-call(s32[2]{0:T(128)S(1)} %copy-done.24, bf16[512,1152]{1,0:T(8,128)(2,1)} %pad_maximum_fusion.refs_0_.in_ref, bf16[512,1152]{1,0:T(8,128)(2,1)} %collective-permute-done.1.refs_1_.in_ref, f32[1024,128]{1,0:T(8,128)S(1)} %copy.58.refs_2_.refs_8_, ...), custom_call_target="tpu_custom_call" | custom-call | flops 134217728 | bytes 262144 | tf_op jit(solution)/shard_map/attention/pallas_call | solution.py:768
  139.9 4.0 collective-permute-done.14.refs_11_
  157.2 24.2 %ffn.3 = (bf16[512,1024]{1,0:T(8,128)(2,1)}, bf16[512,1024]{1,0:T(8,128)(2,1)}, bf16[512,1024]{1,0:T(8,128)(2,1)}, bf16[512,1024]{1,0:T(8,128)(2,1)}, bf16[3,256...) custom-call(bf16[512,1024]{1,0:T(8,128)(2,1)} %multiply_convert_fusi, ...), custom_call_target="tpu_custom_call" | custom-call | flops 452984832 | bytes 688128 | tf_op jit(solution)/shard_map/ffn/pallas_call | solution.py:551
  186.8 34.2 %collective-permute-done.25.refs_11_ = bf16[1,3,128,768]{3,2,1,0:T(8,128)(2,1)S(1)} collective-permute-done((bf16[1,3,128,768]{3,2,1,0:T(8,128)(2,1)S(1)}, bf16[1,3,128,768]{3,2,1,0:T(8,128)(2,1)S(1)}, u32[]{:S(2)}, u32[]{:S(2)}) %collective-permute-start.25) | collective-permute-done | bytes 589856 | tf_op jit(solution)/shard_map/ppermute | solution.py:196
  223.1 23.7 %ffn.4 = (bf16[512,1024]{1,0:T(8,128)(2,1)}, bf16[512,1024]{1,0:T(8,128)(2,1)}, bf16[512,1024]{1,0:T(8,128)(2,1)}, bf16[512,1024]{1,0:T(8,128)(2,1)}, bf16[3,256...) custom-call(bf16[512,1024]{1,0:T(8,128)(2,1)} %multiply_convert_fusi, ...), custom_call_target="tpu_custom_call" | custom-call | flops 452984832 | bytes 688128 | tf_op jit(solution)/shard_map/ffn/pallas_call | solution.py:551
  254.1 23.9 %ffn.5 = (bf16[512,1024]{1,0:T(8,128)(2,1)}, bf16[512,1024]{1,0:T(8,128)(2,1)}, bf16[512,1024]{1,0:T(8,128)(2,1)}, bf16[512,1024]{1,0:T(8,128)(2,1)}, bf16[3,256...) custom-call(bf16[512,1024]{1,0:T(8,128)(2,1)} %multiply_convert_fusi, ...), custom_call_target="tpu_custom_call" | custom-call | flops 452984832 | bytes 688128 | tf_op jit(solution)/shard_map/ffn/pallas_call | solution.py:551
  291.4 3.9 combine.5
  295.3 4.7 collective-permute-start.30
  307.0 4.0 fusion.21
  313.3 4.5 collective-permute-done.34.come_b
  322.6 8.3 %collective-permute-done.32.last_b = bf16[3,128,768]{2,1,0:T(8,128)(2,1)} collective-permute-done((bf16[3,128,768]{2,1,0:T(8,128)(2,1)}, bf16[3,128,768]{2,1,0:T(8,128)(2,1)}, u32[]{:S(2)}, u32[]{:S(2)}) %collective-permute-start.32) | collective-permute-done | bytes 589856 | tf_op jit(solution)/shard_map/ppermute | solution.py:267
  336.1 3.9 combine.6
  340.0 4.5 collective-permute-start.40
  348.3 4.0 combine.7
  352.2 5.4 collective-permute-start.43
  362.9 24.2 %attention_back.2 = (bf16[512,1024]{1,0:T(8,128)(2,1)}, bf16[512,1024]{1,0:T(8,128)(2,1)}, f32[2,128]{1,0:T(2,128)}, bf16[2,256,384]{2,1,0:T(8,128)(2,1)}, bf16[...) custom-call(s32[2]{0:T(128)} %pad_add_fusion.at_ref, ...), custom_call_target="tpu_custom_call" | custom-call | flops 117440512 | bytes 262144 | tf_op jit(solution)/shard_map/attention_back/pallas_call | solution.py:799
  393.1 4.8 all-to-all-start.2
  408.9 5.3 collective-permute-start.50
  421.5 24.1 %attention_back.3 = (bf16[512,1024]{1,0:T(8,128)(2,1)}, bf16[512,1024]{1,0:T(8,128)(2,1)}, f32[2,128]{1,0:T(2,128)}, bf16[2,256,384]{2,1,0:T(8,128)(2,1)}, bf16[...) custom-call(s32[2]{0:T(128)} %pad_add_fusion.at_ref, ...), custom_call_target="tpu_custom_call" | custom-call | flops 117440512 | bytes 262144 | tf_op jit(solution)/shard_map/attention_back/pallas_call | solution.py:799
  450.8 9.1 %collective-permute-done.58.come_b = bf16[2,256,384]{2,1,0:T(8,128)(2,1)S(1)} collective-permute-done((bf16[2,256,384]{2,1,0:T(8,128)(2,1)S(1)}, bf16[2,256,384]{2,1,0:T(8,128)(2,1)S(1)}, u32[]{:S(2)}, u32[]{:S(2)}) %collective-permute-start.58) | collective-permute-done | bytes 393248 | tf_op jit(solution)/shard_map/ppermute | solution.py:255
  473.6 4.0 fusion.9
  489.1 5.9 %all-to-all-start.3 = ((bf16[4,128,1024]{2,1,0:T(8,128)(2,1)}), bf16[4,128,1024]{2,1,0:T(8,128)(2,1)}, u32[]{:S(2)}, u32[]{:S(2)}) async-start(bf16[4,128,1024]{2,1,0:T(8,128)(2,1)} %bitcast.34), calls=%async_computation.3 | async-start | bytes 2097152 | tf_op jit(solution)/shard_map/all_to_all | solution.py:161
  498.5 5.9 %collective-permute-start.60 = (bf16[2,256,384]{2,1,0:T(8,128)(2,1)}, bf16[2,256,384]{2,1,0:T(8,128)(2,1)S(1)}, u32[]{:S(2)}, u32[]{:S(2)}) collective-permute-start(bf16[2,256,384]{2,1,0:T(8,128)(2,1)} %combine.9), channel_id=1, source_target_pairs={{0,1},{3,2},{4,5},{7,6},{8,9},{11,10},{12,13},{15,14},{16,17},{19,... | collective-permute-start | bytes 1179656 | tf_op jit(solution)/shard_map/ppermute | solution.py:277
  508.4 12.6 %collective-permute-done.60 = bf16[2,256,384]{2,1,0:T(8,128)(2,1)S(1)} collective-permute-done((bf16[2,256,384]{2,1,0:T(8,128)(2,1)}, bf16[2,256,384]{2,1,0:T(8,128)(2,1)S(1)}, u32[]{:S(2)}, u32[]{:S(2)}) %collective-permute-start.60) | collective-permute-done | bytes 393248 | tf_op jit(solution)/shard_map/ppermute | solution.py:277
  521.8 24.7 %collective-permute-done.67 = bf16[3,256,768]{2,1,0:T(8,128)(2,1)} collective-permute-done((bf16[3,256,768]{2,1,0:T(8,128)(2,1)S(1)}, bf16[3,256,768]{2,1,0:T(8,128)(2,1)}, u32[]{:S(2)}, u32[]{:S(2)}) %collective-permute-start.67) | collective-permute-done | bytes 1179680 | tf_op jit(solution)/shard_map/ppermute | solution.py:286
  551.7 9.1 %collective-permute-done.73 = f32[2176]{0:T(1024)S(1)} collective-permute-done((f32[2176]{0:T(1024)S(1)}, f32[2176]{0:T(1024)S(1)}, u32[]{:S(2)}, u32[]{:S(2)}) %collective-permute-start.73) | collective-permute-done | bytes 8736 | tf_op jit(solution)/shard_map/ppermute | solution.py:323
  561.6 3.8 collective-permute-done.74
  572.4 5.6 finish_ffn.1
  (428 shorter events, 236.8 us)
Async XLA Ops:
  16.1 35.7 %collective-permute-start.7 = (bf16[3,128,2304]{2,1,0:T(8,128)(2,1)}, bf16[3,128,2304]{2,1,0:T(8,128)(2,1)}, u32[]{:S(2)}, u32[]{:S(2)}) collective-permute-start(bf16[3,128,2304]{2,1,0:T(8,128)(2,1)} %get-tuple-element.90), channel_id=1, source_target_pairs={{0,4},{4,0},{1,5},{5,1},{2,6},{6,2},{3,7},{7,3},{8,12},{12,8},{9,1... | collective-permute-start | bytes 5308424 | tf_op jit(solution)/shard_map/ppermute | solution.py:66
  18.2 37.8 %all-to-all-start = ((bf16[4,128,1152]{2,1,0:T(8,128)(2,1)}), bf16[4,128,1152]{2,1,0:T(8,128)(2,1)}, u32[]{:S(2)}, u32[]{:S(2)}) async-start(bf16[4,128,1152]{2,1,0:T(8,128)(2,1)} %bitcast.6), calls=%async_computation | async-start | bytes 2359296 | tf_op jit(solution)/shard_map/all_to_all | solution.py:156
  55.0 30.4 %collective-permute-start.8 = (bf16[2,3,128,768]{3,2,1,0:T(8,128)(2,1)}, bf16[2,3,128,768]{3,2,1,0:T(8,128)(2,1)}, u32[]{:S(2)}, u32[]{:S(2)}) collective-permute-start(bf16[2,3,128,768]{3,2,1,0:T(8,128)(2,1)} %core_pair.5.refs_8_), channel_id=1, source_target_pairs={{0,8},{8,0},{1,9},{9,1},{2,10},{10,2},{3,11},{11,3},{4,12},{12,4},... | collective-permute-start | bytes 3538952 | tf_op jit(solution)/shard_map/ppermute | solution.py:193
  73.2 52.2 %all-to-all-start.1 = ((bf16[4,128,1024]{2,1,0:T(8,128)(2,1)}), bf16[4,128,1024]{2,1,0:T(8,128)(2,1)}, u32[]{:S(2)}, u32[]{:S(2)}) async-start(bf16[4,128,1024]{2,1,0:T(8,128)(2,1)} %bitcast.30), calls=%async_computation.1 | async-start | bytes 2097152 | tf_op jit(solution)/shard_map/all_to_all | solution.py:156
  85.4 34.1 %collective-permute-start.13 = (bf16[2,3,128,768]{3,2,1,0:T(8,128)(2,1)}, bf16[2,3,128,768]{3,2,1,0:T(8,128)(2,1)}, u32[]{:S(2)}, u32[]{:S(2)}) collective-permute-start(bf16[2,3,128,768]{3,2,1,0:T(8,128)(2,1)} %core_pair.6.refs_8_), channel_id=1, source_target_pairs={{0,8},{8,0},{1,9},{9,1},{2,10},{10,2},{3,11},{11,3},{4,12},{12,4},... | collective-permute-start | bytes 3538952 | tf_op jit(solution)/shard_map/ppermute | solution.py:193
  86.9 35.1 %collective-permute-start.15 = (bf16[2,3,128,768]{3,2,1,0:T(8,128)(2,1)}, bf16[2,3,128,768]{3,2,1,0:T(8,128)(2,1)}, u32[]{:S(2)}, u32[]{:S(2)}) collective-permute-start(bf16[2,3,128,768]{3,2,1,0:T(8,128)(2,1)} %core_pair.6.refs_8_), channel_id=1, source_target_pairs={{0,16},{16,0},{1,17},{17,1},{2,18},{18,2},{3,19},{19,3},{4,20},{20... | collective-permute-start | bytes 3538952 | tf_op jit(solution)/shard_map/ppermute | solution.py:193
  147.2 37.3 %collective-permute-start.24 = (bf16[2,3,128,768]{3,2,1,0:T(8,128)(2,1)}, bf16[2,3,128,768]{3,2,1,0:T(8,128)(2,1)S(1)}, u32[]{:S(2)}, u32[]{:S(2)}) collective-permute-start(bf16[2,3,128,768]{3,2,1,0:T(8,128)(2,1)} %core_pair.7.refs_8_), channel_id=1, source_target_pairs={{0,8},{8,0},{1,9},{9,1},{2,10},{10,2},{3,11},{11,3},{4,12},{12,4},... | collective-permute-start | bytes 3538952 | tf_op jit(solution)/shard_map/ppermute | solution.py:193
  147.8 37.4 %collective-permute-start.26 = (bf16[2,3,128,768]{3,2,1,0:T(8,128)(2,1)}, bf16[2,3,128,768]{3,2,1,0:T(8,128)(2,1)}, u32[]{:S(2)}, u32[]{:S(2)}) collective-permute-start(bf16[2,3,128,768]{3,2,1,0:T(8,128)(2,1)} %core_pair.7.refs_8_), channel_id=1, source_target_pairs={{0,16},{16,0},{1,17},{17,1},{2,18},{18,2},{3,19},{19,3},{4,20},{20... | collective-permute-start | bytes 3538952 | tf_op jit(solution)/shard_map/ppermute | solution.py:193
  181.4 68.1 %collective-permute-start.22 = (bf16[3,256,768]{2,1,0:T(8,128)(2,1)}, bf16[3,256,768]{2,1,0:T(8,128)(2,1)S(1)}, u32[]{:S(2)}, u32[]{:S(2)}) collective-permute-start(bf16[3,256,768]{2,1,0:T(8,128)(2,1)} %get-tuple-element.104), channel_id=1, source_target_pairs={{0,16},{16,0},{1,17},{17,1},{2,18},{18,2},{3,19},{19,3},{4,20},{20... | collective-permute-start | bytes 3538952 | tf_op jit(solution)/shard_map/ppermute | solution.py:255
  183.0 68.1 %collective-permute-start.20 = (bf16[3,256,768]{2,1,0:T(8,128)(2,1)}, bf16[3,256,768]{2,1,0:T(8,128)(2,1)}, u32[]{:S(2)}, u32[]{:S(2)}) collective-permute-start(bf16[3,256,768]{2,1,0:T(8,128)(2,1)} %get-tuple-element.102), channel_id=1, source_target_pairs={{0,8},{8,0},{1,9},{9,1},{2,10},{10,2},{3,11},{11,3},{4,12},{12,4},... | collective-permute-start | bytes 3538952 | tf_op jit(solution)/shard_map/ppermute | solution.py:254
  184.5 36.5 %collective-permute-start.25 = (bf16[1,3,128,768]{3,2,1,0:T(8,128)(2,1)S(1)}, bf16[1,3,128,768]{3,2,1,0:T(8,128)(2,1)S(1)}, u32[]{:S(2)}, u32[]{:S(2)}) collective-permute-start(bf16[1,3,128,768]{3,2,1,0:T(8,128)(2,1)S(1)} %slice.269), channel_id=1, source_target_pairs={{0,16},{16,0},{1,17},{17,1},{2,18},{18,2},{3,19},{19,3},{4,20},{20... | collective-permute-start | bytes 1769480 | tf_op jit(solution)/shard_map/ppermute | solution.py:196
  186.2 36.1 %collective-permute-start.27 = (bf16[1,3,128,768]{3,2,1,0:T(8,128)(2,1)S(1)}, bf16[1,3,128,768]{3,2,1,0:T(8,128)(2,1)S(1)}, u32[]{:S(2)}, u32[]{:S(2)}) collective-permute-start(bf16[1,3,128,768]{3,2,1,0:T(8,128)(2,1)S(1)} %slice.270), channel_id=1, source_target_pairs={{0,8},{8,0},{1,9},{9,1},{2,10},{10,2},{3,11},{11,3},{4,12},{12,4},... | collective-permute-start | bytes 1769480 | tf_op jit(solution)/shard_map/ppermute | solution.py:197
  246.9 48.5 %collective-permute-start.29 = (bf16[3,256,768]{2,1,0:T(8,128)(2,1)}, bf16[3,256,768]{2,1,0:T(8,128)(2,1)}, u32[]{:S(2)}, u32[]{:S(2)}) collective-permute-start(bf16[3,256,768]{2,1,0:T(8,128)(2,1)} %get-tuple-element.111), channel_id=1, source_target_pairs={{0,16},{16,0},{1,17},{17,1},{2,18},{18,2},{3,19},{19,3},{4,20},{20... | collective-permute-start | bytes 3538952 | tf_op jit(solution)/shard_map/ppermute | solution.py:255
  248.0 54.2 %collective-permute-start.28 = (bf16[3,256,768]{2,1,0:T(8,128)(2,1)}, bf16[3,256,768]{2,1,0:T(8,128)(2,1)}, u32[]{:S(2)}, u32[]{:S(2)}) collective-permute-start(bf16[3,256,768]{2,1,0:T(8,128)(2,1)} %get-tuple-element.109), channel_id=1, source_target_pairs={{0,8},{8,0},{1,9},{9,1},{2,10},{10,2},{3,11},{11,3},{4,12},{12,4},... | collective-permute-start | bytes 3538952 | tf_op jit(solution)/shard_map/ppermute | solution.py:254
  250.6 38.1 %collective-permute-start.23 = (bf16[3,128,768]{2,1,0:T(8,128)(2,1)}, bf16[3,128,768]{2,1,0:T(8,128)(2,1)}, u32[]{:S(2)}, u32[]{:S(2)}) collective-permute-start(bf16[3,128,768]{2,1,0:T(8,128)(2,1)} %add_convert_fusion.14), channel_id=1, source_target_pairs={{0,8},{8,0},{1,9},{9,1},{2,10},{10,2},{3,11},{11,3},{4,12},{12,4},... | collective-permute-start | bytes 1769480 | tf_op jit(solution)/shard_map/ppermute | solution.py:267
  253.2 36.7 %collective-permute-start.21 = (bf16[3,128,768]{2,1,0:T(8,128)(2,1)}, bf16[3,128,768]{2,1,0:T(8,128)(2,1)}, u32[]{:S(2)}, u32[]{:S(2)}) collective-permute-start(bf16[3,128,768]{2,1,0:T(8,128)(2,1)} %add_convert_fusion.15), channel_id=1, source_target_pairs={{0,16},{16,0},{1,17},{17,1},{2,18},{18,2},{3,19},{19,3},{4,20},{20... | collective-permute-start | bytes 1769480 | tf_op jit(solution)/shard_map/ppermute | solution.py:267
  295.3 44.7 %collective-permute-start.30 = (bf16[3,256,768]{2,1,0:T(8,128)(2,1)}, bf16[3,256,768]{2,1,0:T(8,128)(2,1)}, u32[]{:S(2)}, u32[]{:S(2)}) collective-permute-start(bf16[3,256,768]{2,1,0:T(8,128)(2,1)} %combine.5), channel_id=1, source_target_pairs={{0,1},{3,2},{4,5},{7,6},{8,9},{11,10},{12,13},{15,14},{16,17},{19,... | collective-permute-start | bytes 3538952 | tf_op jit(solution)/shard_map/ppermute | solution.py:277
  317.9 39.7 %collective-permute-start.36 = (bf16[512,1024]{1,0:T(8,128)(2,1)}, bf16[512,1024]{1,0:T(8,128)(2,1)}, u32[]{:S(2)}, u32[]{:S(2)}) collective-permute-start(bf16[512,1024]{1,0:T(8,128)(2,1)} %get-tuple-element.159.in_ref), channel_id=1, source_target_pairs={{0,4},{4,0},{1,5},{5,1},{2,6},{6,2},{3,7},{7,3},{8,12},{12,8},{9,1... | collective-permute-start | bytes 3145736 | tf_op jit(solution)/shard_map/ppermute | solution.py:66
  320.1 68.0 %collective-permute-start.37 = (bf16[512,1024]{1,0:T(8,128)(2,1)}, bf16[512,1024]{1,0:T(8,128)(2,1)}, u32[]{:S(2)}, u32[]{:S(2)}) collective-permute-start(bf16[512,1024]{1,0:T(8,128)(2,1)} %add_convert_fusion.8), channel_id=1, source_target_pairs={{0,4},{4,0},{1,5},{5,1},{2,6},{6,2},{3,7},{7,3},{8,12},{12,8},{9,1... | collective-permute-start | bytes 3145736 | tf_op jit(solution)/shard_map/ppermute | solution.py:66
  340.0 61.5 %collective-permute-start.40 = (bf16[3,256,768]{2,1,0:T(8,128)(2,1)}, bf16[3,256,768]{2,1,0:T(8,128)(2,1)}, u32[]{:S(2)}, u32[]{:S(2)}) collective-permute-start(bf16[3,256,768]{2,1,0:T(8,128)(2,1)} %combine.6), channel_id=1, source_target_pairs={{0,1},{3,2},{4,5},{7,6},{8,9},{11,10},{12,13},{15,14},{16,17},{19,... | collective-permute-start | bytes 3538952 | tf_op jit(solution)/shard_map/ppermute | solution.py:277
  346.5 72.4 %collective-permute-start.39 = (bf16[3,256,768]{2,1,0:T(8,128)(2,1)S(1)}, bf16[3,256,768]{2,1,0:T(8,128)(2,1)}, u32[]{:S(2)}, u32[]{:S(2)}) collective-permute-start(bf16[3,256,768]{2,1,0:T(8,128)(2,1)S(1)} %add_convert_fusion.5), channel_id=1, source_target_pairs={{1,2},{2,1},{5,6},{6,5},{9,10},{10,9},{13,14},{14,13},{17,18},{18,... | collective-permute-start | bytes 3538952 | tf_op jit(solution)/shard_map/ppermute | solution.py:282
  352.2 62.0 %collective-permute-start.43 = (bf16[3,256,768]{2,1,0:T(8,128)(2,1)}, bf16[3,256,768]{2,1,0:T(8,128)(2,1)}, u32[]{:S(2)}, u32[]{:S(2)}) collective-permute-start(bf16[3,256,768]{2,1,0:T(8,128)(2,1)} %combine.7), channel_id=1, source_target_pairs={{0,1},{3,2},{4,5},{7,6},{8,9},{11,10},{12,13},{15,14},{16,17},{19,... | collective-permute-start | bytes 3538952 | tf_op jit(solution)/shard_map/ppermute | solution.py:277
  393.1 68.3 %all-to-all-start.2 = ((bf16[4,128,1024]{2,1,0:T(8,128)(2,1)}), bf16[4,128,1024]{2,1,0:T(8,128)(2,1)}, u32[]{:S(2)}, u32[]{:S(2)}) async-start(bf16[4,128,1024]{2,1,0:T(8,128)(2,1)} %bitcast.74), calls=%async_computation.2 | async-start | bytes 2097152 | tf_op jit(solution)/shard_map/all_to_all | solution.py:161
  403.5 60.0 %collective-permute-start.54 = (bf16[3,256,768]{2,1,0:T(8,128)(2,1)S(1)}, bf16[3,256,768]{2,1,0:T(8,128)(2,1)}, u32[]{:S(2)}, u32[]{:S(2)}) collective-permute-start(bf16[3,256,768]{2,1,0:T(8,128)(2,1)S(1)} %add_convert_fusion.3), channel_id=1, source_target_pairs={{1,2},{2,1},{5,6},{6,5},{9,10},{10,9},{13,14},{14,13},{17,18},{18,... | collective-permute-start | bytes 3538952 | tf_op jit(solution)/shard_map/ppermute | solution.py:282
  408.9 40.4 %collective-permute-start.50 = (bf16[2,256,384]{2,1,0:T(8,128)(2,1)}, bf16[2,256,384]{2,1,0:T(8,128)(2,1)S(1)}, u32[]{:S(2)}, u32[]{:S(2)}) collective-permute-start(bf16[2,256,384]{2,1,0:T(8,128)(2,1)} %combine.8), channel_id=1, source_target_pairs={{0,1},{3,2},{4,5},{7,6},{8,9},{11,10},{12,13},{15,14},{16,17},{19,... | collective-permute-start | bytes 1179656 | tf_op jit(solution)/shard_map/ppermute | solution.py:277
  417.2 61.7 %collective-permute-start.55 = (bf16[3,256,768]{2,1,0:T(8,128)(2,1)}, bf16[3,256,768]{2,1,0:T(8,128)(2,1)}, u32[]{:S(2)}, u32[]{:S(2)}) collective-permute-start(bf16[3,256,768]{2,1,0:T(8,128)(2,1)} %add_convert_fusion.2), channel_id=1, source_target_pairs={{1,2},{2,1},{5,6},{6,5},{9,10},{10,9},{13,14},{14,13},{17,18},{18,... | collective-permute-start | bytes 3538952 | tf_op jit(solution)/shard_map/ppermute | solution.py:282
  449.3 49.2 %collective-permute-start.63 = (bf16[3,256,768]{2,1,0:T(8,128)(2,1)}, bf16[3,256,768]{2,1,0:T(8,128)(2,1)}, u32[]{:S(2)}, u32[]{:S(2)}) collective-permute-start(bf16[3,256,768]{2,1,0:T(8,128)(2,1)} %add_convert_fusion.4), channel_id=1, source_target_pairs={{1,0},{2,3},{5,4},{6,7},{9,8},{10,11},{13,12},{14,15},{17,16},{18,... | collective-permute-start | bytes 3538952 | tf_op jit(solution)/shard_map/ppermute | solution.py:286
  478.9 42.9 %collective-permute-start.65 = (bf16[3,256,768]{2,1,0:T(8,128)(2,1)}, bf16[3,256,768]{2,1,0:T(8,128)(2,1)}, u32[]{:S(2)}, u32[]{:S(2)}) collective-permute-start(bf16[3,256,768]{2,1,0:T(8,128)(2,1)} %add_convert_fusion.1), channel_id=1, source_target_pairs={{1,0},{2,3},{5,4},{6,7},{9,8},{10,11},{13,12},{14,15},{17,16},{18,... | collective-permute-start | bytes 3538952 | tf_op jit(solution)/shard_map/ppermute | solution.py:286
  483.1 63.4 %collective-permute-start.67 = (bf16[3,256,768]{2,1,0:T(8,128)(2,1)S(1)}, bf16[3,256,768]{2,1,0:T(8,128)(2,1)}, u32[]{:S(2)}, u32[]{:S(2)}) collective-permute-start(bf16[3,256,768]{2,1,0:T(8,128)(2,1)S(1)} %add_convert_fusion), channel_id=1, source_target_pairs={{1,0},{2,3},{5,4},{6,7},{9,8},{10,11},{13,12},{14,15},{17,16},{18,... | collective-permute-start | bytes 3538952 | tf_op jit(solution)/shard_map/ppermute | solution.py:286
  489.1 76.9 %all-to-all-start.3 = ((bf16[4,128,1024]{2,1,0:T(8,128)(2,1)}), bf16[4,128,1024]{2,1,0:T(8,128)(2,1)}, u32[]{:S(2)}, u32[]{:S(2)}) async-start(bf16[4,128,1024]{2,1,0:T(8,128)(2,1)} %bitcast.34), calls=%async_computation.3 | async-start | bytes 2097152 | tf_op jit(solution)/shard_map/all_to_all | solution.py:161
  495.1 73.1 %collective-permute-start.52 = (bf16[2,256,384]{2,1,0:T(8,128)(2,1)}, bf16[2,256,384]{2,1,0:T(8,128)(2,1)}, u32[]{:S(2)}, u32[]{:S(2)}) collective-permute-start(bf16[2,256,384]{2,1,0:T(8,128)(2,1)} %add_convert_fusion.18), channel_id=1, source_target_pairs={{1,0},{2,3},{5,4},{6,7},{9,8},{10,11},{13,12},{14,15},{17,16},{18,... | collective-permute-start | bytes 1179656 | tf_op jit(solution)/shard_map/ppermute | solution.py:286
  506.8 64.6 %collective-permute-start.64 = (bf16[3,128,768]{2,1,0:T(8,128)(2,1)}, bf16[3,128,768]{2,1,0:T(8,128)(2,1)S(1)}, u32[]{:S(2)}, u32[]{:S(2)}) collective-permute-start(bf16[3,128,768]{2,1,0:T(8,128)(2,1)} %get-tuple-element.165), channel_id=1, source_target_pairs={{0,4},{4,0},{1,5},{5,1},{2,6},{6,2},{3,7},{7,3},{8,12},{12,8},{9,1... | collective-permute-start | bytes 1769480 | tf_op jit(solution)/shard_map/ppermute | solution.py:66
  (126 other events, 1647.7 us)
